TPU v7x, 32 devices: a whole 2x2x4 slice. The times are simulated.
32 devices in a mesh: pipe: 4 (over z), dp: 4 (over y, x), tensor: 2 (over core).
Axes of the slice: x: 2, y: 2, z: 4, core: 2. Of those that a mesh axis runs over, the one named last changes fastest.
Arguments:
- up_weight: bfloat16 [4, 2048, 4096], P('pipe', None, 'tensor'), may hold values from -0.125 to 0.125
- down_weight: bfloat16 [4, 2048, 4096], P('pipe', None, 'tensor'), may hold values from -0.09375 to 0.09375
- gate_act: bfloat16 [4, 512, 4096], P('pipe', 'dp', 'tensor'), may hold values from -0.27734375 to 2.5
- hidden: bfloat16 [4, 512, 4096], P('pipe', 'dp', 'tensor'), may hold values from -6 to 6
- block_input: bfloat16 [4, 512, 2048], P('pipe', ('dp', 'tensor')), may hold values from -6 to 6
- norm_gain: float32 [4, 2048], P('pipe'), may hold values from 0.1 to 1.9
- loss_grad: bfloat16 [512, 2048], P(('dp', 'tensor')), may hold values from -0.796875 to 0.796875
- moment_one: float32 [4, 2048, 4096], P('pipe', 'dp', 'tensor'), may hold values from -6 to 6
- moment_two: float32 [4, 2048, 4096], P('pipe', 'dp', 'tensor'), may hold values from 1 to 30
Outputs:
- input_grad: bfloat16 [4, 512, 2048], P('pipe', ('dp', 'tensor'))
- new_moment_one: float32 [4, 2048, 4096], P('pipe', 'dp', 'tensor')
- new_moment_two: float32 [4, 2048, 4096], P('pipe', 'dp', 'tensor')
- new_down_weight: float32 [4, 2048, 4096], P('pipe', 'dp', 'tensor')
All inputs are finite; a program needn't handle non-finite values.
Results may differ from a plain program's by a relative error of at most 0.028.
Values may be sent and summed in bfloat16 or wider, within the bound.
No kernel may reach another device: no remote copies, remote signals or barrier semaphores. Data moves between devices by JAX's collectives and lax.ppermute only.
A program may use at most 128 MiB of HBM per device.

v0:
```python
import jax
import jax.numpy as jnp
from jax import lax
from jax.sharding import PartitionSpec as P

EPS_NORM = 1e-05
EPS_ADAM = 1e-08
BETA_ONE = 0.9
BETA_TWO = 0.95
RATE = 0.01
DECAY = 0.1
CORRECT_ONE = 1.0 - 0.9**10
CORRECT_TWO = 1.0 - 0.95**10


def shifted(shard, axis, by):
    size = lax.axis_size(axis)
    pairs = [(i, i + by) for i in range(size) if 0 <= i + by < size]
    return lax.ppermute(shard, axis, pairs)


def rounded(value):
    return lax.optimization_barrier(value.astype(jnp.bfloat16)).astype(jnp.float32)


def on_device(
    up_weight,
    down_weight,
    gate_act,
    hidden,
    block_input,
    norm_gain,
    loss_grad,
    moment_one,
    moment_two,
):
    w_up = up_weight[0]
    w_down = down_weight[0]
    gates = gate_act[0].astype(jnp.float32)
    saved = hidden[0]
    rows_in = block_input[0].astype(jnp.float32)
    gain = norm_gain[0][None, :]
    sections = lax.axis_size("pipe")
    segment = lax.axis_index("pipe")
    tok_share = rows_in.shape[0]
    model_width = rows_in.shape[1]
    unit_width = w_up.shape[1]
    inverse_rms = lax.rsqrt(jnp.mean(rows_in * rows_in, axis=-1, keepdims=True) + EPS_NORM)
    upstream0 = jnp.where(segment == sections - 1, loss_grad, jnp.zeros_like(loss_grad))
    kept_dx0 = jnp.zeros_like(loss_grad)
    kept_full0 = jnp.zeros((tok_share * lax.axis_size("tensor"), model_width), jnp.bfloat16)

    def section_step(layer_step, carry):
        upstream, kept_dx, kept_full = carry
        active = segment == sections - 1 - layer_step
        full_grad = lax.all_gather(upstream, "tensor", axis=0, tiled=True)
        unit_grad = lax.cond(
            active,
            lambda: (jnp.dot(full_grad, w_down, preferred_element_type=jnp.float32) * gates).astype(
                jnp.bfloat16
            ),
            lambda: jnp.zeros((full_grad.shape[0], unit_width), jnp.bfloat16),
        )
        normed = lax.psum_scatter(
            lax.cond(
                active,
                lambda: lax.dot_general(
                    unit_grad, w_up, (((1,), (1,)), ((), ())), preferred_element_type=jnp.float32
                ),
                lambda: jnp.zeros((tok_share * lax.axis_size("tensor"), model_width), jnp.float32),
            ).astype(jnp.bfloat16),
            "tensor",
            scatter_dimension=0,
            tiled=True,
        ).astype(jnp.float32)
        scaled = normed * gain
        mean_term = jnp.mean(rows_in * scaled, axis=-1, keepdims=True)
        out_grad = (
            upstream.astype(jnp.float32)
            + inverse_rms * scaled
            - rows_in * inverse_rms**3 * mean_term
        ).astype(jnp.bfloat16)
        kept_dx = jnp.where(active, out_grad, kept_dx)
        kept_full = jnp.where(active, full_grad, kept_full)
        arrived = shifted(out_grad, "pipe", -1)
        upstream = jnp.where(segment == sections - 2 - layer_step, arrived, upstream)
        return (upstream, kept_dx, kept_full)

    final_up, kept_dx, kept_full = lax.fori_loop(
        0, sections, section_step, (upstream0, kept_dx0, kept_full0)
    )
    owners = lax.axis_size("dp")
    row_share = model_width // owners
    partial_grad = lax.dot_general(
        kept_full, saved, (((0,), (0,)), ((), ())), preferred_element_type=jnp.float32
    )
    gradient = lax.psum_scatter(rounded(partial_grad), "dp", scatter_dimension=0, tiled=True)
    owner = lax.axis_index("dp")
    current = lax.dynamic_slice_in_dim(w_down, owner * row_share, row_share, 0).astype(jnp.float32)
    first = BETA_ONE * moment_one[0] + (1.0 - BETA_ONE) * gradient
    second = BETA_TWO * moment_two[0] + (1.0 - BETA_TWO) * gradient * gradient
    direction = first / CORRECT_ONE / (jnp.sqrt(second / CORRECT_TWO) + EPS_ADAM) + DECAY * current
    updated = current - RATE * direction
    return (kept_dx[None], first[None], second[None], updated[None])


def solution(mesh):
    in_specs = (
        P("pipe", None, "tensor"),
        P("pipe", None, "tensor"),
        P("pipe", "dp", "tensor"),
        P("pipe", "dp", "tensor"),
        P("pipe", ("dp", "tensor"), None),
        P("pipe", None),
        P(("dp", "tensor"), None),
        P("pipe", "dp", "tensor"),
        P("pipe", "dp", "tensor"),
    )
    out_specs = (
        P("pipe", ("dp", "tensor"), None),
        P("pipe", "dp", "tensor"),
        P("pipe", "dp", "tensor"),
        P("pipe", "dp", "tensor"),
    )
    return jax.shard_map(
        on_device, mesh=mesh, in_specs=in_specs, out_specs=out_specs, check_vma=False
    )
```

profile of v0, /device:TPU:0, one launch (start us, length us, event | category | flops | bytes accessed | tf_op | source)
XLA Modules:
  0.0 346.2 jit_solution(9096211403070457053)
XLA Ops:
  8.0 1.2 multiply_reduce_fusion.1
  9.2 1.0 bitcast_convert_fusion.1
  10.2 2.1 bitcast_convert_fusion
  12.4 145.6 %while.20 = (s32[]{:T(128)}, bf16[64,2048]{1,0:T(8,128)(2,1)S(1)}, bf16[64,2048]{1,0:T(8,128)(2,1)}, bf16[128,2048]{1,0:T(8,128)(2,1)S(1)}, s32[]{:T(128)}, /*in...) while((s32[]{:T(128)}, bf16[64,2048]{1,0:T(8,128)(2,1)S(1)}, ...), condition=%wide.region_8.9_spmd.clone, body=%wide.region_1.8_spmd.clone.sunk | while | flops 2150629376 | bytes 31246236 | solution.py:89
  12.4 0.0 reduce-scatter.5.cloned.1.call-start
  12.4 2.3 all_gather.11
  14.7 0.1 conditional.6
  14.8 0.1 conditional.7
  14.9 0.8 copy-done.1
  15.6 0.0 reduce-scatter.5.cloned.1.call-update
  15.7 22.7 %reduce-scatter.5.cloned.1.call-done = bf16[64,2048]{1,0:T(8,128)(2,1)} async-done(((bf16[128,2048]{1,0:T(8,128)(2,1)}), bf16[64,2048]{1,0:T(8,128)(2,1)}) %reduce-scatter.5.cloned.1.call-update) | async-done | bytes 262160 | tf_op jit(solution)/shard_map/while/body/eval_jaxpr/reduce_scatter | solution.py:64
  38.4 1.1 multiply_reduce_fusion.3
  39.5 1.9 select_select_fusion.4
  41.5 1.3 collective-permute-start
  42.8 0.2 select_select_fusion.5
  43.0 8.9 %collective-permute-done = bf16[64,2048]{1,0:T(8,128)(2,1)S(1)} collective-permute-done((bf16[64,2048]{1,0:T(8,128)(2,1)S(1)}, bf16[64,2048]{1,0:T(8,128)(2,1)S(1)}, u32[]{:S(2)}, u32[]{:S(2)}) %collective-permute-start) | collective-permute-done | bytes 262176 | tf_op jit(solution)/shard_map/while/body/eval_jaxpr/ppermute | solution.py:19
  51.9 0.1 broadcast_select_fusion.3
  52.0 0.0 reduce-scatter.5.cloned.1.call-start
  52.0 2.2 all_gather.11
  54.2 0.1 conditional.6
  54.3 0.1 conditional.7
  54.4 0.8 copy-done.1
  55.1 0.0 reduce-scatter.5.cloned.1.call-update
  55.2 19.4 %reduce-scatter.5.cloned.1.call-done = bf16[64,2048]{1,0:T(8,128)(2,1)} async-done(((bf16[128,2048]{1,0:T(8,128)(2,1)}), bf16[64,2048]{1,0:T(8,128)(2,1)}) %reduce-scatter.5.cloned.1.call-update) | async-done | bytes 262160 | tf_op jit(solution)/shard_map/while/body/eval_jaxpr/reduce_scatter | solution.py:64
  74.6 1.1 multiply_reduce_fusion.3
  75.7 2.0 select_select_fusion.4
  77.7 1.3 collective-permute-start
  79.0 0.2 select_select_fusion.5
  79.2 8.9 %collective-permute-done = bf16[64,2048]{1,0:T(8,128)(2,1)S(1)} collective-permute-done((bf16[64,2048]{1,0:T(8,128)(2,1)S(1)}, bf16[64,2048]{1,0:T(8,128)(2,1)S(1)}, u32[]{:S(2)}, u32[]{:S(2)}) %collective-permute-start) | collective-permute-done | bytes 262176 | tf_op jit(solution)/shard_map/while/body/eval_jaxpr/ppermute | solution.py:19
  88.1 0.1 broadcast_select_fusion.3
  88.2 0.0 reduce-scatter.5.cloned.1.call-start
  88.3 2.2 all_gather.11
  90.5 0.1 conditional.6
  90.5 0.1 conditional.7
  90.6 0.8 copy-done.1
  91.4 0.0 reduce-scatter.5.cloned.1.call-update
  91.4 18.4 %reduce-scatter.5.cloned.1.call-done = bf16[64,2048]{1,0:T(8,128)(2,1)} async-done(((bf16[128,2048]{1,0:T(8,128)(2,1)}), bf16[64,2048]{1,0:T(8,128)(2,1)}) %reduce-scatter.5.cloned.1.call-update) | async-done | bytes 262160 | tf_op jit(solution)/shard_map/while/body/eval_jaxpr/reduce_scatter | solution.py:64
  109.9 1.1 multiply_reduce_fusion.3
  111.0 2.0 select_select_fusion.4
  113.0 1.3 collective-permute-start
  114.3 0.2 select_select_fusion.5
  114.5 8.9 %collective-permute-done = bf16[64,2048]{1,0:T(8,128)(2,1)S(1)} collective-permute-done((bf16[64,2048]{1,0:T(8,128)(2,1)S(1)}, bf16[64,2048]{1,0:T(8,128)(2,1)S(1)}, u32[]{:S(2)}, u32[]{:S(2)}) %collective-permute-start) | collective-permute-done | bytes 262176 | tf_op jit(solution)/shard_map/while/body/eval_jaxpr/ppermute | solution.py:19
  123.4 0.1 broadcast_select_fusion.3
  123.5 0.0 reduce-scatter.5.cloned.1.call-start
  123.6 2.2 all_gather.11
  125.8 4.9 %conditional.6 = (bf16[128,2048]{1,0:T(8,128)(2,1)S(1)}) conditional(s32[]{:T(128)} %convert_element_type.104, () %tuple.69, (bf16[128,2048]{1,0:T(8,128)(2,1)S(1)}, bf16[2048,2048]{1,0:T(8,128)(2,1)}, f32[128,2048]{1,0:T(8,128)}) %tuple.70), branch_computations={%region_2.2_spmd, %region_3.3_spmd} | conditional | flops 1074266112 | bytes 10485768 | solution.py:57
  125.8 4.9 %fusion = bf16[128,2048]{1,0:T(8,128)(2,1)S(1)} fusion(f32[128,2048]{1,0:T(8,128)} %get-tuple-element.275, bf16[128,2048]{1,0:T(8,128)(2,1)S(1)} %get-tuple-element.273, bf16[2048,2048]{1,0:T(8,128)(2,1)} %get-tuple-element.274), kind=kOutput, calls=%fused_computation.1 | convolution fusion | flops 1074266112 | bytes 10485760 | tf_op jit(solution)/shard_map/while/body/eval_jaxpr/cond/branch_1_fun/dot_general | solution.py:59
  130.7 6.3 %conditional.7 = (bf16[128,2048]{1,0:T(8,128)(2,1)S(1)}) conditional(s32[]{:T(128)} %convert_element_type.104, () %tuple.68, (bf16[128,2048]{1,0:T(8,128)(2,1)S(1)}, bf16[2048,2048]{1,0:T(8,128)(2,1)}) %tuple.71), branch_computations={%region_4.4_spmd, %region_5.5_spmd} | conditional | flops 1073741824 | bytes 9437192 | solution.py:65
  130.7 6.3 %fusion.8 = bf16[128,2048]{1,0:T(8,128)(2,1)S(1)} fusion(bf16[128,2048]{1,0:T(8,128)(2,1)S(1)} %get-tuple-element.276, bf16[2048,2048]{1,0:T(8,128)(2,1)} %get-tuple-element.277), kind=kOutput, calls=%fused_computation.27 | convolution fusion | flops 1073741824 | bytes 9437184 | tf_op jit(solution)/shard_map/while/body/eval_jaxpr/cond/branch_1_fun/dot_general | solution.py:67
  137.0 0.8 copy-done.1
  137.8 0.0 reduce-scatter.5.cloned.1.call-update
  137.8 6.5 %reduce-scatter.5.cloned.1.call-done = bf16[64,2048]{1,0:T(8,128)(2,1)} async-done(((bf16[128,2048]{1,0:T(8,128)(2,1)}), bf16[64,2048]{1,0:T(8,128)(2,1)}) %reduce-scatter.5.cloned.1.call-update) | async-done | bytes 262160 | tf_op jit(solution)/shard_map/while/body/eval_jaxpr/reduce_scatter | solution.py:64
  144.3 1.1 multiply_reduce_fusion.3
  145.4 2.0 select_select_fusion.4
  147.4 1.3 collective-permute-start
  148.7 0.2 select_select_fusion.5
  148.9 8.9 %collective-permute-done = bf16[64,2048]{1,0:T(8,128)(2,1)S(1)} collective-permute-done((bf16[64,2048]{1,0:T(8,128)(2,1)S(1)}, bf16[64,2048]{1,0:T(8,128)(2,1)S(1)}, u32[]{:S(2)}, u32[]{:S(2)}) %collective-permute-start) | collective-permute-done | bytes 262176 | tf_op jit(solution)/shard_map/while/body/eval_jaxpr/ppermute | solution.py:19
  157.8 0.1 broadcast_select_fusion.3
  157.9 0.0 reduce-scatter.3.cloned.1.call-start
  158.0 5.6 %convolution_convert_fusion = bf16[2048,2048]{1,0:T(8,128)(2,1)} fusion(bf16[128,2048]{1,0:T(8,128)(2,1)S(1)} %get-tuple-element.298, bf16[1,128,2048]{2,1,0:T(8,128)(2,1)S(1)} %copy-done), kind=kOutput, calls=%fused_computation.9 | convolution fusion | flops 1077936128 | bytes 9437184 | tf_op jit(solution)/shard_map/dot_general | solution.py:94
  163.6 11.2 %convert_element_type.78 = f32[2048,2048]{1,0:T(8,128)} convert(bf16[2048,2048]{1,0:T(8,128)(2,1)} %convolution_convert_fusion) | non-fusion elementwise | flops 4194304 | bytes 25165824 | tf_op jit(solution)/shard_map/convert_element_type | solution.py:23
  174.8 0.0 reduce-scatter.3.cloned.1.call-update
  174.8 154.0 %reduce-scatter.3.cloned.1.call-done = f32[512,2048]{1,0:T(8,128)} async-done(((f32[2048,2048]{1,0:T(8,128)}), f32[512,2048]{1,0:T(8,128)}) %reduce-scatter.3.cloned.1.call-update) | async-done | bytes 4194320 | tf_op jit(solution)/shard_map/reduce_scatter | solution.py:97
  328.9 10.2 %fusion.3 = (f32[1,512,2048]{2,1,0:T(8,128)}, f32[1,512,2048]{2,1,0:T(8,128)}, f32[1,512,2048]{2,1,0:T(8,128)}) fusion(bf16[1,2048,2048]{2,1,0:T(8,128)(2,1)} %bitcast.54, s32[]{:T(128)S(6)} %select_n.69, f32[512,2048]{1,0:T(8,128)} %reduce-scatter.3.cloned.1.call-done, f32[1,512,2048]{2,1,0:T(8,128)} %param.22, f32[1,512,2048]{2,1,0:T(8,128)} %param.23), kind=kLoop, calls=%fused_computation.15 | loop fusion | flops 16777216 | bytes 27262980 | tf_op jit(solution)/shard_map/broadcast_in_dim | solution.py:104
  (29 shorter events, 0.4 us)
Async XLA Ops:
  8.0 150.0 %copy-start = (bf16[1,128,2048]{2,1,0:T(8,128)(2,1)S(1)}, bf16[1,128,2048]{2,1,0:T(8,128)(2,1)}, u32[]{:S(2)}) copy-start(bf16[1,128,2048]{2,1,0:T(8,128)(2,1)} %param.18) | copy-start | bytes 1572868
  12.4 26.0 %reduce-scatter.5.cloned.1.call-start = ((), (), s32[]{:S(2)}) async-start(), calls=%async_computation.3 | async-start | bytes 786432 | tf_op jit(solution)/shard_map/while/body/eval_jaxpr/reduce_scatter | solution.py:64
  14.8 23.6 %copy-start.2 = (f32[1,2048]{1,0:T(1,128)S(1)}, f32[1,2048]{1,0:T(1,128)}, u32[]{:S(2)}) copy-start(f32[1,2048]{1,0:T(1,128)} %get-tuple-element.485) | copy-start | bytes 24580 | tf_op jit(solution)/shard_map/while
  14.8 0.8 copy-start.1
  41.5 10.4 %collective-permute-start = (bf16[64,2048]{1,0:T(8,128)(2,1)S(1)}, bf16[64,2048]{1,0:T(8,128)(2,1)S(1)}, u32[]{:S(2)}, u32[]{:S(2)}) collective-permute-start(bf16[64,2048]{1,0:T(8,128)(2,1)S(1)} %get-tuple-element.442), channel_id=1, source_target_pairs={{8,0},{16,8},{24,16},{9,1},{17,9},{25,17},{10,2},{18,10},{26,18},{... | collective-permute-start | bytes 786440 | tf_op jit(solution)/shard_map/while/body/eval_jaxpr/ppermute | solution.py:19
  52.0 22.6 %reduce-scatter.5.cloned.1.call-start = ((), (), s32[]{:S(2)}) async-start(), calls=%async_computation.3 | async-start | bytes 786432 | tf_op jit(solution)/shard_map/while/body/eval_jaxpr/reduce_scatter | solution.py:64
  54.3 20.3 %copy-start.2 = (f32[1,2048]{1,0:T(1,128)S(1)}, f32[1,2048]{1,0:T(1,128)}, u32[]{:S(2)}) copy-start(f32[1,2048]{1,0:T(1,128)} %get-tuple-element.485) | copy-start | bytes 24580 | tf_op jit(solution)/shard_map/while
  54.4 0.8 copy-start.1
  77.7 10.4 %collective-permute-start = (bf16[64,2048]{1,0:T(8,128)(2,1)S(1)}, bf16[64,2048]{1,0:T(8,128)(2,1)S(1)}, u32[]{:S(2)}, u32[]{:S(2)}) collective-permute-start(bf16[64,2048]{1,0:T(8,128)(2,1)S(1)} %get-tuple-element.442), channel_id=1, source_target_pairs={{8,0},{16,8},{24,16},{9,1},{17,9},{25,17},{10,2},{18,10},{26,18},{... | collective-permute-start | bytes 786440 | tf_op jit(solution)/shard_map/while/body/eval_jaxpr/ppermute | solution.py:19
  88.2 21.7 %reduce-scatter.5.cloned.1.call-start = ((), (), s32[]{:S(2)}) async-start(), calls=%async_computation.3 | async-start | bytes 786432 | tf_op jit(solution)/shard_map/while/body/eval_jaxpr/reduce_scatter | solution.py:64
  90.5 19.4 %copy-start.2 = (f32[1,2048]{1,0:T(1,128)S(1)}, f32[1,2048]{1,0:T(1,128)}, u32[]{:S(2)}) copy-start(f32[1,2048]{1,0:T(1,128)} %get-tuple-element.485) | copy-start | bytes 24580 | tf_op jit(solution)/shard_map/while
  90.6 0.8 copy-start.1
  113.0 10.4 %collective-permute-start = (bf16[64,2048]{1,0:T(8,128)(2,1)S(1)}, bf16[64,2048]{1,0:T(8,128)(2,1)S(1)}, u32[]{:S(2)}, u32[]{:S(2)}) collective-permute-start(bf16[64,2048]{1,0:T(8,128)(2,1)S(1)} %get-tuple-element.442), channel_id=1, source_target_pairs={{8,0},{16,8},{24,16},{9,1},{17,9},{25,17},{10,2},{18,10},{26,18},{... | collective-permute-start | bytes 786440 | tf_op jit(solution)/shard_map/while/body/eval_jaxpr/ppermute | solution.py:19
  123.5 20.7 %reduce-scatter.5.cloned.1.call-start = ((), (), s32[]{:S(2)}) async-start(), calls=%async_computation.3 | async-start | bytes 786432 | tf_op jit(solution)/shard_map/while/body/eval_jaxpr/reduce_scatter | solution.py:64
  130.7 13.6 %copy-start.2 = (f32[1,2048]{1,0:T(1,128)S(1)}, f32[1,2048]{1,0:T(1,128)}, u32[]{:S(2)}) copy-start(f32[1,2048]{1,0:T(1,128)} %get-tuple-element.485) | copy-start | bytes 24580 | tf_op jit(solution)/shard_map/while
  137.0 0.8 copy-start.1
  147.4 10.4 %collective-permute-start = (bf16[64,2048]{1,0:T(8,128)(2,1)S(1)}, bf16[64,2048]{1,0:T(8,128)(2,1)S(1)}, u32[]{:S(2)}, u32[]{:S(2)}) collective-permute-start(bf16[64,2048]{1,0:T(8,128)(2,1)S(1)} %get-tuple-element.442), channel_id=1, source_target_pairs={{8,0},{16,8},{24,16},{9,1},{17,9},{25,17},{10,2},{18,10},{26,18},{... | collective-permute-start | bytes 786440 | tf_op jit(solution)/shard_map/while/body/eval_jaxpr/ppermute | solution.py:19
  157.9 170.9 %reduce-scatter.3.cloned.1.call-start = ((), (), s32[]{:S(2)}) async-start(), calls=%async_computation.2 | async-start | bytes 20971520 | tf_op jit(solution)/shard_map/reduce_scatter | solution.py:97
Sparse Core Ops, SparseCore 0:
  16.0 22.3 reduce-scatter.4
  55.6 18.8 reduce-scatter.4
  91.9 17.9 reduce-scatter.4
  137.9 6.3 reduce-scatter.4
Sparse Core Ops, SparseCore 1:
  174.9 153.9 reduce-scatter.2
where the time goes:
time: 347 us; the launch traced here: 346 us
  waiting for transfers between devices  257 us (74%)
  other arithmetic  39.3 us (11%)
  matrix products  16.7 us (5%)
  between operations  15.2 us (4%)
  blocking collectives  8.81 us (3%)
  starting transfers between devices  5.33 us (2%)
    reduce_scatter x1, waiting for transfers between devices, on_device(): lax.psum_scatter(rounded(partial_grad), 'dp', scatter_dimension=0, tiled=...  154 us
    reduce_scatter x4, waiting for transfers between devices, section_step(): lax.psum_scatter(lax.cond(active, lambda: lax.dot_general(unit_grad, w_up...  67 us
    ppermute x4, waiting for transfers between devices, shifted(): return lax.ppermute(shard, axis, pairs)  35.6 us
    convert_element_type x1, other arithmetic, rounded(): lax.optimization_barrier(value.astype(jnp.bfloat16)).astype(jnp.float32)  11.2 us
    broadcast_in_dim x1, other arithmetic, on_device(): return (kept_dx[None], first[None], second[None], updated[None])  10.2 us
    all_gather x4, blocking collectives, section_step(): full_grad = lax.all_gather(upstream, 'tensor', axis=0, tiled=True)  8.81 us
    select_n x4, other arithmetic, section_step(): kept_dx = jnp.where(active, out_grad, kept_dx)  8.03 us
  transfers between devices with their start and end apart: 9, of which 9 were waited for; matrix products, arithmetic and copies ran while one was open for 0% of the time, Pallas kernels for 0%

commit v1 on v0

v1 whole, which is shorter than its diff:
```python
import functools
import jax
import jax.numpy as jnp
from jax import lax
from jax.experimental import pallas as pl
from jax.experimental.pallas import tpu as pltpu
from jax.sharding import PartitionSpec as P

EPS_NORM = 1e-05
EPS_ADAM = 1e-08
BETA_ONE = 0.9
BETA_TWO = 0.95
RATE = 0.01
DECAY = 0.1
CORRECT_ONE = 1.0 - 0.9**10
CORRECT_TWO = 1.0 - 0.95**10

MIB = 2**20
VMEM = pl.BlockSpec(memory_space=pltpu.VMEM)
F32 = jnp.float32
BF16 = jnp.bfloat16


def tile_of(extent, most):
    tile = min(extent, most)
    while extent % tile:
        tile //= 2
    return tile


def step_kernel(layer, sizes, own_ref, *refs):
    parts, share, width, units = sizes
    peer_refs = refs[: parts - 1]
    down_ref, up_ref, gate_ref, kept_ref = refs[parts - 1 : parts + 3]
    sent_refs = refs[parts + 3 : 2 * parts + 2]
    rows_ref, unit_ref = refs[2 * parts + 2 :]
    me = lax.axis_index("tensor")

    @pl.when(lax.axis_index("pipe") == layer)
    def _():
        rows_ref[0:share, :] = own_ref[...]
        for k in range(1, parts):
            rows_ref[k * share : (k + 1) * share, :] = peer_refs[k - 1][...]
        tile = tile_of(units, 1024)

        @pl.loop(0, units // tile)
        def _(j):
            cols = pl.ds(pl.multiple_of(j * tile, tile), tile)
            term = jnp.dot(rows_ref[...], down_ref[:, cols], preferred_element_type=F32)
            for k in range(parts):
                at = pl.multiple_of(lax.rem(me + k, parts) * share, share)
                gates = gate_ref[pl.ds(at, share), cols].astype(F32)
                unit_ref[k * share : (k + 1) * share, cols] = (
                    term[k * share : (k + 1) * share] * gates
                ).astype(BF16)

        tile = tile_of(width, 1024)

        @pl.loop(0, width // tile)
        def _(j):
            cols = pl.ds(pl.multiple_of(j * tile, tile), tile)
            term = lax.dot_general(
                unit_ref[...], up_ref[cols, :], (((1,), (1,)), ((), ())), preferred_element_type=F32
            )
            kept_ref[:, cols] = term[0:share]
            for k in range(1, parts):
                sent_refs[k - 1][:, cols] = term[k * share : (k + 1) * share].astype(BF16)


def section_step(layer, own, peers, w_down, w_up, gates):
    share, width = own.shape
    units = w_down.shape[1]
    parts = len(peers) + 1
    rows = share * parts
    outs = pl.pallas_call(
        functools.partial(step_kernel, layer, (parts, share, width, units)),
        out_shape=[jax.ShapeDtypeStruct((share, width), F32)]
        + [jax.ShapeDtypeStruct((share, width), BF16)] * (parts - 1),
        in_specs=[VMEM] * (parts + 3),
        out_specs=[VMEM] * parts,
        scratch_shapes=[pltpu.VMEM((rows, width), BF16), pltpu.VMEM((rows, units), BF16)],
        compiler_params=pltpu.CompilerParams(vmem_limit_bytes=8 * MIB),
        cost_estimate=pl.CostEstimate(
            flops=4 * rows * width * units, bytes_accessed=4 * width * units, transcendentals=0
        ),
        name="section_step",
    )(own, *peers, w_down, w_up, gates)
    return outs[0], outs[1:]


def norm_kernel(layer, parts, kept_ref, *refs):
    arrived = refs[: parts - 1]
    up_ref, in_ref, gain_ref = refs[parts - 1 : parts + 2]
    earlier = refs[parts + 2 : -1]
    out_ref = refs[-1]
    segment = lax.axis_index("pipe")

    @pl.when(segment == layer)
    def _():
        normed = kept_ref[...]
        for ref in arrived:
            normed = normed + ref[...].astype(F32)
        rows_in = in_ref[...].astype(F32)
        inverse_rms = lax.rsqrt(jnp.mean(rows_in * rows_in, axis=-1, keepdims=True) + EPS_NORM)
        scaled = normed * gain_ref[...]
        mean_term = jnp.mean(rows_in * scaled, axis=-1, keepdims=True)
        out_ref[...] = (
            up_ref[...].astype(F32)
            + inverse_rms * scaled
            - rows_in * (inverse_rms * inverse_rms * inverse_rms * mean_term)
        ).astype(BF16)

    for above, ref in enumerate(earlier):

        @pl.when(segment == layer + len(earlier) - above)
        def _(ref=ref):
            out_ref[...] = ref[...]


def norm_step(layer, kept, arrived, upstream, rows_in, gain, earlier=()):
    parts = len(arrived) + 1
    return pl.pallas_call(
        functools.partial(norm_kernel, layer, parts),
        out_shape=jax.ShapeDtypeStruct(upstream.shape, BF16),
        in_specs=[VMEM] * (parts + 3 + len(earlier)),
        out_specs=VMEM,
        compiler_params=pltpu.CompilerParams(vmem_limit_bytes=8 * MIB),
        name="norm_step",
    )(kept, *arrived, upstream, rows_in, gain, *earlier)


def split_kernel(owners, *refs):
    sections = len(refs) - owners
    share = refs[sections].shape[1]
    me = lax.axis_index("dp")
    for s in range(sections):

        @pl.when(lax.axis_index("pipe") == sections - 1 - s)
        def _(s=s):
            for k in range(owners):
                at = pl.multiple_of((me ^ k) * share, share)
                refs[sections + k][...] = refs[s][:, pl.ds(at, share)]


def split_for_owners(upstreams, owners):
    tokens, width = upstreams[0].shape
    return pl.pallas_call(
        functools.partial(split_kernel, owners),
        out_shape=[jax.ShapeDtypeStruct((tokens, width // owners), BF16)] * owners,
        in_specs=[VMEM] * len(upstreams),
        out_specs=[VMEM] * owners,
        compiler_params=pltpu.CompilerParams(vmem_limit_bytes=4 * MIB),
        name="split_for_owners",
    )(*upstreams)


def adam_update(gradient, current, moment_one, moment_two):
    first = BETA_ONE * moment_one + (1.0 - BETA_ONE) * gradient
    second = BETA_TWO * moment_two + (1.0 - BETA_TWO) * gradient * gradient
    direction = (first / CORRECT_ONE) / (jnp.sqrt(second / CORRECT_TWO) + EPS_ADAM) + DECAY * current
    return first, second, current - RATE * direction


def adam_kernel(grad_refs, sizes, *refs):
    owners, parts, share, rows, tile = sizes
    up_refs = refs[:grad_refs]
    hidden_ref, down_ref, one_ref, two_ref, first_ref, second_ref, updated_ref, turned_ref = refs[grad_refs:]
    me = lax.axis_index("dp")
    part = lax.axis_index("tensor")

    @pl.when(pl.program_id(0) == 0)
    def _():
        for p in range(parts):
            for k in range(owners):
                at = (me ^ k) * parts + lax.rem(part + p, parts)
                turned_ref[pl.ds(pl.multiple_of(at * share, share), share), :] = up_refs[p * owners + k][...]

    gradient = lax.dot_general(
        turned_ref[...], hidden_ref[...], (((0,), (0,)), ((), ())), preferred_element_type=F32
    )
    cols = pl.ds(pl.multiple_of(pl.program_id(0) * tile, tile), tile)
    current = down_ref[pl.ds(pl.multiple_of(me * rows, rows), rows), cols].astype(F32)
    first_ref[...], second_ref[...], updated_ref[...] = adam_update(
        gradient, current, one_ref[:, cols], two_ref[:, cols]
    )


def adam_step(blocks, hidden_all, w_down, moment_one, moment_two, owners, parts):
    rows, units = moment_one.shape
    share = blocks[0].shape[0]
    tokens = hidden_all.shape[0]
    tile = tile_of(units, 256)
    out = pl.BlockSpec((rows, tile), lambda j: (0, j))
    return pl.pallas_call(
        functools.partial(adam_kernel, len(blocks), (owners, parts, share, rows, tile)),
        out_shape=[jax.ShapeDtypeStruct((rows, units), F32)] * 3,
        grid=(units // tile,),
        in_specs=[VMEM] * len(blocks)
        + [pl.BlockSpec((tokens, tile), lambda j: (0, j)), VMEM, VMEM, VMEM],
        out_specs=[out] * 3,
        scratch_shapes=[pltpu.VMEM((tokens, rows), BF16)],
        compiler_params=pltpu.CompilerParams(vmem_limit_bytes=24 * MIB),
        name="adam_step",
    )(*blocks, hidden_all, w_down, moment_one, moment_two)


def adam_general(upstreams, hidden_all, w_down, moment_one, moment_two):
    owners = lax.axis_size("dp")
    sections = len(upstreams)
    segment = lax.axis_index("pipe")
    own = upstreams[0]
    for s in range(1, sections):
        own = jnp.where(segment == sections - 1 - s, upstreams[s], own)
    mine = lax.all_to_all(own, "dp", split_axis=1, concat_axis=0, tiled=True)
    share, rows = own.shape[0], mine.shape[1]
    turned = lax.all_gather(mine.reshape(owners, share, rows), "tensor", axis=1, tiled=True)
    gradient = lax.dot_general(
        turned.reshape(-1, rows), hidden_all, (((0,), (0,)), ((), ())), preferred_element_type=F32
    )
    at = lax.axis_index("dp") * rows
    current = lax.dynamic_slice_in_dim(w_down, at, rows, 0).astype(F32)
    return adam_update(gradient, current, moment_one, moment_two)


def from_peers(value, axis):
    size = lax.axis_size(axis)
    return [lax.ppermute(value, axis, [((i + k) % size, i) for i in range(size)]) for k in range(1, size)]


def to_peers(values, axis):
    size = lax.axis_size(axis)
    return [
        lax.ppermute(value, axis, [(i, (i + k) % size) for i in range(size)])
        for k, value in enumerate(values, 1)
    ]


def on_device(
    up_weight,
    down_weight,
    gate_act,
    hidden,
    block_input,
    norm_gain,
    loss_grad,
    moment_one,
    moment_two,
):
    w_up, w_down, gates, rows_in = up_weight[0], down_weight[0], gate_act[0], block_input[0]
    sections = lax.axis_size("pipe")
    owners = lax.axis_size("dp")
    parts = lax.axis_size("tensor")
    hidden_all = lax.all_gather(hidden[0], "dp", axis=0, tiled=True)
    by_blocks = owners <= 8 and owners & (owners - 1) == 0 and rows_in.shape[1] // owners % 128 == 0
    upstreams = [loss_grad]
    grads = []
    for layer in reversed(range(sections)):
        upstream = upstreams[-1]
        peers = from_peers(upstream, "tensor")
        if layer == 0 and by_blocks:
            blocks = split_for_owners(upstreams, owners)
            blocks = [blocks[0]] + [
                lax.ppermute(blocks[k], "dp", [(i, i ^ k) for i in range(owners)])
                for k in range(1, owners)
            ]
            blocks = blocks + [
                block for turn in zip(*[from_peers(b, "tensor") for b in blocks]) for block in turn
            ]
        kept, sent = section_step(layer, upstream, peers, w_down, w_up, gates)
        arrived = to_peers(sent, "tensor")
        grad = norm_step(
            layer, kept, arrived, upstream, rows_in, norm_gain, grads if layer == 0 else ()
        )
        grads.append(grad)
        if layer:
            upstreams.append(lax.ppermute(grad, "pipe", [(layer, layer - 1)]))
    if by_blocks:
        first, second, updated = adam_step(
            blocks, hidden_all, w_down, moment_one[0], moment_two[0], owners, parts
        )
    else:
        first, second, updated = adam_general(
            upstreams, hidden_all, w_down, moment_one[0], moment_two[0]
        )
    return (grads[-1][None], first[None], second[None], updated[None])


def solution(mesh):
    in_specs = (
        P("pipe", None, "tensor"),
        P("pipe", None, "tensor"),
        P("pipe", "dp", "tensor"),
        P("pipe", "dp", "tensor"),
        P("pipe", ("dp", "tensor"), None),
        P("pipe", None),
        P(("dp", "tensor"), None),
        P("pipe", "dp", "tensor"),
        P("pipe", "dp", "tensor"),
    )
    out_specs = (
        P("pipe", ("dp", "tensor"), None),
        P("pipe", "dp", "tensor"),
        P("pipe", "dp", "tensor"),
        P("pipe", "dp", "tensor"),
    )
    return jax.shard_map(
        on_device, mesh=mesh, in_specs=in_specs, out_specs=out_specs, check_vma=False
    )
```

time: 347 us -> 118 us (0.34)
  waiting for transfers between devices: 257 us -> 55 us
  other arithmetic: 39.3 us -> 0 us
  local copies, waits for them, and re-layouts: 3.46 us -> 24.9 us
  matrix products: 16.7 us -> 0 us
  Pallas kernels: 0 us -> 13.9 us
  blocking collectives: 8.81 us -> 0 us
  starting transfers between devices: 5.33 us -> 9.15 us
    reduce_scatter x5 -> x0, waiting for transfers between devices: 221 us -> none  [the longest x1 154 us: on_device(): lax.psum_scatter(rounded(partial_grad), 'dp', scatter_dimension=0, tiled=...]
    unnamed x2 -> x30, local copies, waits for them, and re-layouts: 0.01 us -> 24.9 us
    ppermute x4 -> x18, waiting for transfers between devices: 35.6 us -> 55 us  [the longest x3 41.4 us: on_device(): upstreams.append(lax.ppermute(grad, 'pipe', [(layer, layer - 1)]))]
    dot_general x3 -> x0, matrix products: 16.7 us -> none  [the longest x1 6.27 us: section_step(): lax.dot_general(unit_grad, w_up, (((1,), (1,)), ((), ())), preferred_elem...]
    convert_element_type x3 -> x0, other arithmetic: 14.3 us -> none  [the longest x1 11.2 us: rounded(): lax.optimization_barrier(value.astype(jnp.bfloat16)).astype(jnp.float32)]
    pallas_call x0 -> x10, Pallas kernels: none -> 13.9 us  [the longest x1 8.28 us: adam_step(): pl.pallas_call(functools.partial(adam_kernel, len(blocks), (owners, parts...]
    broadcast_in_dim x1 -> x0, other arithmetic: 10.2 us -> none  [on_device(): return (kept_dx[None], first[None], second[None], updated[None])]
    select_n x13 -> x0, other arithmetic: 9.16 us -> none  [the longest x4 8.03 us: section_step(): kept_dx = jnp.where(active, out_grad, kept_dx)]
  transfers between devices with their start and end apart: 9 -> 19, of which waited for: 9 -> 12; matrix products, arithmetic and copies ran while one was open for 0% -> 0% of each run, Pallas kernels for 0% -> 5%
where the time goes in v1:
time: 118 us; the launch traced here: 117 us
  waiting for transfers between devices  55 us (47%)
  local copies, waits for them, and re-layouts  24.9 us (21%)
  between operations  14.1 us (12%)
  Pallas kernels  13.9 us (12%)
  starting transfers between devices  9.15 us (8%)
    ppermute x3, waiting for transfers between devices, on_device(): upstreams.append(lax.ppermute(grad, 'pipe', [(layer, layer - 1)]))  41.4 us
    unnamed x30, local copies, waits for them, and re-layouts  24.9 us
    pallas_call x1, Pallas kernels, adam_step(): pl.pallas_call(functools.partial(adam_kernel, len(blocks), (owners, parts...  8.28 us
    ppermute x8, waiting for transfers between devices, from_peers(): lax.ppermute(value, axis, [((i + k) % size, i) for i in range(size)])  5.46 us
    ppermute x3, waiting for transfers between devices, on_device(): lax.ppermute(blocks[k], 'dp', [(i, i ^ k) for i in range(owners)])  4.67 us
    pallas_call x4, Pallas kernels, section_step(): pl.pallas_call(functools.partial(step_kernel, layer, (parts, share, width...  4.52 us
    ppermute x3, starting transfers between devices, on_device(): lax.ppermute(blocks[k], 'dp', [(i, i ^ k) for i in range(owners)])  3.57 us
    ppermute x4, waiting for transfers between devices, to_peers(): lax.ppermute(value, axis, [(i, (i + k) % size) for i in range(size)])  3.46 us
  transfers between devices with their start and end apart: 19, of which 12 were waited for; matrix products, arithmetic and copies ran while one was open for 0% of the time, Pallas kernels for 5%

profile of v1, /device:TPU:0, one launch (start us, length us, event | category | flops | bytes accessed | tf_op | source)
XLA Modules:
  0.0 117.0 jit_solution(3933977823051572156)
XLA Ops:
  7.2 0.0 all-gather.3.cloned.1.call-start
  7.2 0.5 collective-permute-start
  7.7 1.4 %collective-permute-done.refs_0_ = bf16[64,2048]{1,0:T(8,128)(2,1)S(1)} collective-permute-done((bf16[64,2048]{1,0:T(8,128)(2,1)}, bf16[64,2048]{1,0:T(8,128)(2,1)S(1)}, u32[]{:S(2)}, u32[]{:S(2)}) %collective-permute-start) | collective-permute-done | bytes 262176 | tf_op jit(solution)/shard_map/ppermute | solution.py:227
  9.1 0.0 copy-start
  9.1 3.4 %copy-done = bf16[1,2048,2048]{2,1,0:T(8,128)(2,1)S(1)} copy-done((bf16[1,2048,2048]{2,1,0:T(8,128)(2,1)S(1)}, bf16[1,2048,2048]{2,1,0:T(8,128)(2,1)}, u32[]{:S(2)}) %copy-start) | copy-done | bytes 8388632
  12.5 0.0 copy-start.4
  12.5 3.4 %copy-done.4 = bf16[1,2048,2048]{2,1,0:T(8,128)(2,1)S(1)} copy-done((bf16[1,2048,2048]{2,1,0:T(8,128)(2,1)S(1)}, bf16[1,2048,2048]{2,1,0:T(8,128)(2,1)}, u32[]{:S(2)}) %copy-start.4) | copy-done | bytes 8388632
  15.9 0.0 copy-start.6
  15.9 1.0 copy-done.6
  16.9 0.0 copy-start.11
  16.9 0.9 copy-done.11
  17.9 0.0 copy-start.12
  17.9 0.0 copy-start.14
  17.9 0.0 copy-start.7
  17.9 0.4 collective-permute-start.1
  18.3 0.0 all-gather.3.cloned.1.call-update
  18.4 1.1 collective-permute-done.1.refs_0_
  19.5 0.0 copy-done.10
  19.5 0.0 copy-done.12
  19.5 0.0 copy-done.14
  19.5 0.7 collective-permute-start.2
  20.2 0.0 collective-permute-done.2.own_ref.refs_1_
  20.2 0.4 collective-permute-start.3
  20.7 1.2 collective-permute-done.3.refs_0_
  21.8 0.0 copy-done.7
  21.8 0.0 copy-start.1
  21.8 3.4 %copy-done.1 = bf16[1,2048,2048]{2,1,0:T(8,128)(2,1)S(1)} copy-done((bf16[1,2048,2048]{2,1,0:T(8,128)(2,1)S(1)}, bf16[1,2048,2048]{2,1,0:T(8,128)(2,1)}, u32[]{:S(2)}) %copy-start.1) | copy-done | bytes 8388632
  25.2 3.4 %copy-done.5 = bf16[1,2048,2048]{2,1,0:T(8,128)(2,1)S(1)} copy-done((bf16[1,2048,2048]{2,1,0:T(8,128)(2,1)S(1)}, bf16[1,2048,2048]{2,1,0:T(8,128)(2,1)}, u32[]{:S(2)}) %copy-start.5) | copy-done | bytes 8388632
  28.6 0.4 collective-permute-start.4
  29.0 1.2 collective-permute-done.4.refs_0_
  30.1 0.8 collective-permute-start.5
  30.9 0.0 collective-permute-done.5.own_ref.refs_1_.refs_2_
  31.0 0.4 collective-permute-start.6
  31.4 1.2 collective-permute-done.6.refs_0_
  32.6 0.0 copy-done.2
  32.6 0.4 collective-permute-start.7
  32.9 1.2 collective-permute-done.7.refs_0_
  34.1 1.3 %collective-permute-start.8 = (bf16[64,2048]{1,0:T(8,128)(2,1)S(1)}, bf16[64,2048]{1,0:T(8,128)(2,1)S(1)}, u32[]{:S(2)}, u32[]{:S(2)}) collective-permute-start(bf16[64,2048]{1,0:T(8,128)(2,1)S(1)} %norm_step.6.refs_6_), channel_id=1, source_target_pairs={{8,0},{9,1},{10,2},{11,3},{12,4},{13,5},{14,6},{15,7}} | collective-permute-start | bytes 786440 | tf_op jit(solution)/shard_map/ppermute | solution.py:276
  35.4 41.4 %collective-permute-done.8.own_ref.refs_1_.refs_3_ = bf16[64,2048]{1,0:T(8,128)(2,1)S(1)} collective-permute-done((bf16[64,2048]{1,0:T(8,128)(2,1)S(1)}, bf16[64,2048]{1,0:T(8,128)(2,1)S(1)}, u32[]{:S(2)}, u32[]{:S(2)}) %collective-permute-start.8) | collective-permute-done | bytes 262176 | tf_op jit(solution)/shard_map/ppermute | solution.py:276
  76.7 0.0 collective-permute-start.9
  76.8 1.5 %collective-permute-done.9.refs_0_ = bf16[64,2048]{1,0:T(8,128)(2,1)S(1)} collective-permute-done((bf16[64,2048]{1,0:T(8,128)(2,1)S(1)}, bf16[64,2048]{1,0:T(8,128)(2,1)S(1)}, u32[]{:S(2)}, u32[]{:S(2)}) %collective-permute-start.9) | collective-permute-done | bytes 262176 | tf_op jit(solution)/shard_map/ppermute | solution.py:227
  78.3 4.5 %section_step.7 = (f32[64,2048]{1,0:T(8,128)S(1)}, bf16[64,2048]{1,0:T(8,128)(2,1)S(1)}) custom-call(bf16[64,2048]{1,0:T(8,128)(2,1)S(1)} %collective-permute-done.8.own_ref.refs_1_.refs_3_, bf16[64,2048]{1,0:T(8,128)(2,1)S(1)} %collective-permute-done.9.refs_0_, bf16[2048,2048]{1,0:T(8,128)(2,1)S(1)} %bitcast.14, bf16[2048,2048]{1,0:T(8,128)(2,1)S(1)} %bitcast.19, ...), custom_call_target="tpu_custom_call" | custom-call | flops 2147483648 | bytes 16777216 | tf_op jit(solution)/shard_map/section_step/pallas_call | solution.py:75
  82.8 0.2 collective-permute-start.10
  83.0 1.6 %collective-permute-start.11 = (bf16[64,512]{1,0:T(8,128)(2,1)S(1)}, bf16[64,512]{1,0:T(8,128)(2,1)S(1)}, u32[]{:S(2)}, u32[]{:S(2)}) collective-permute-start(bf16[64,512]{1,0:T(8,128)(2,1)S(1)} %get-tuple-element.28), channel_id=1, source_target_pairs={{0,2},{2,0},{4,6},{6,4},{1,3},{3,1},{5,7},{7,5},{8,10},{10,8},{12,... | collective-permute-start | bytes 196616 | tf_op jit(solution)/shard_map/ppermute | solution.py:263
  84.6 1.5 %collective-permute-start.12 = (bf16[64,512]{1,0:T(8,128)(2,1)S(1)}, bf16[64,512]{1,0:T(8,128)(2,1)S(1)}, u32[]{:S(2)}, u32[]{:S(2)}) collective-permute-start(bf16[64,512]{1,0:T(8,128)(2,1)S(1)} %get-tuple-element.29), channel_id=1, source_target_pairs={{0,4},{2,6},{4,0},{6,2},{1,5},{3,7},{5,1},{7,3},{8,12},{10,14},{12... | collective-permute-start | bytes 196616 | tf_op jit(solution)/shard_map/ppermute | solution.py:263
  86.1 0.5 collective-permute-start.13
  86.6 0.0 collective-permute-start.14
  86.6 0.9 collective-permute-done.11.refs_1_
  87.5 0.0 collective-permute-start.15
  87.5 1.4 %collective-permute-done.12.refs_2_ = bf16[64,512]{1,0:T(8,128)(2,1)S(1)} collective-permute-done((bf16[64,512]{1,0:T(8,128)(2,1)S(1)}, bf16[64,512]{1,0:T(8,128)(2,1)S(1)}, u32[]{:S(2)}, u32[]{:S(2)}) %collective-permute-start.12) | collective-permute-done | bytes 65568 | tf_op jit(solution)/shard_map/ppermute | solution.py:263
  88.9 0.0 collective-permute-start.16
  88.9 2.4 %collective-permute-done.13.refs_3_ = bf16[64,512]{1,0:T(8,128)(2,1)S(1)} collective-permute-done((bf16[64,512]{1,0:T(8,128)(2,1)S(1)}, bf16[64,512]{1,0:T(8,128)(2,1)S(1)}, u32[]{:S(2)}, u32[]{:S(2)}) %collective-permute-start.13) | collective-permute-done | bytes 65568 | tf_op jit(solution)/shard_map/ppermute | solution.py:263
  91.3 0.0 collective-permute-start.17
  91.3 0.0 collective-permute-done.10.refs_0_
  91.3 1.0 norm_step.7
  92.3 0.0 collective-permute-done.14.refs_4_
  92.3 0.0 collective-permute-done.15.refs_5_
  92.3 0.0 collective-permute-done.16.refs_6_
  92.3 0.2 collective-permute-done.17.refs_7_
  92.5 3.4 %copy-done.3 = bf16[1,2048,2048]{2,1,0:T(8,128)(2,1)S(1)} copy-done((bf16[1,2048,2048]{2,1,0:T(8,128)(2,1)S(1)}, bf16[1,2048,2048]{2,1,0:T(8,128)(2,1)}, u32[]{:S(2)}) %copy-start.3) | copy-done | bytes 8388632
  95.9 2.2 %copy-done.8 = f32[1,512,2048]{2,1,0:T(8,128)S(1)} copy-done((f32[1,512,2048]{2,1,0:T(8,128)S(1)}, f32[1,512,2048]{2,1,0:T(8,128)}, u32[]{:S(2)}) %copy-start.8) | copy-done | bytes 4194328
  98.1 2.2 %copy-done.9 = f32[1,512,2048]{2,1,0:T(8,128)S(1)} copy-done((f32[1,512,2048]{2,1,0:T(8,128)S(1)}, f32[1,512,2048]{2,1,0:T(8,128)}, u32[]{:S(2)}) %copy-start.9) | copy-done | bytes 4194328
  100.3 1.6 %copy-done.13 = bf16[1,512,2048]{2,1,0:T(8,128)(2,1)S(1)} copy-done((bf16[1,512,2048]{2,1,0:T(8,128)(2,1)S(1)}, bf16[1,512,2048]{2,1,0:T(8,128)(2,1)}, u32[]{:S(2)}) %copy-start.13) | copy-done | bytes 2097176
  101.9 8.3 %adam_step.1 = (f32[512,2048]{1,0:T(8,128)}, f32[512,2048]{1,0:T(8,128)}, f32[512,2048]{1,0:T(8,128)}) custom-call(bf16[64,512]{1,0:T(8,128)(2,1)S(1)} %get-tuple-element.27.refs_0_, bf16[64,512]{1,0:T(8,128)(2,1)S(1)} %collective-permute-done.11.refs_1_, bf16[64,512]{1,0:T(8,128)(2,1)S(1)} %collective-permute-done.12.refs_2_, ...), custom_call_target="tpu_custom_call" | custom-call | tf_op jit(solution)/shard_map/adam_step/pallas_call | solution.py:194
  (15 shorter events, 0.1 us)
Async XLA Ops:
  7.2 85.4 %all-gather.3.cloned.1.call-start = ((), (), s32[]{:S(2)}) async-start(), calls=%async_computation | async-start | bytes 2621440 | tf_op jit(solution)/shard_map/all_gather | solution.py:253
  7.2 1.9 %collective-permute-start = (bf16[64,2048]{1,0:T(8,128)(2,1)}, bf16[64,2048]{1,0:T(8,128)(2,1)S(1)}, u32[]{:S(2)}, u32[]{:S(2)}) collective-permute-start(bf16[64,2048]{1,0:T(8,128)(2,1)} %refs_0_.1), channel_id=1, source_target_pairs={{1,0},{0,1},{3,2},{2,3},{5,4},{4,5},{7,6},{6,7},{9,8},{8,9},{11,10... | collective-permute-start | bytes 786440 | tf_op jit(solution)/shard_map/ppermute | solution.py:227
  9.1 3.4 %copy-start = (bf16[1,2048,2048]{2,1,0:T(8,128)(2,1)S(1)}, bf16[1,2048,2048]{2,1,0:T(8,128)(2,1)}, u32[]{:S(2)}) copy-start(bf16[1,2048,2048]{2,1,0:T(8,128)(2,1)} %param.10) | copy-start | bytes 25165828
  12.5 3.4 %copy-start.4 = (bf16[1,2048,2048]{2,1,0:T(8,128)(2,1)S(1)}, bf16[1,2048,2048]{2,1,0:T(8,128)(2,1)}, u32[]{:S(2)}) copy-start(bf16[1,2048,2048]{2,1,0:T(8,128)(2,1)} %param.9) | copy-start | bytes 25165828
  15.9 1.0 copy-start.6
  16.9 0.9 copy-start.11
  17.9 1.6 %copy-start.10 = (bf16[1,64,2048]{2,1,0:T(8,128)(2,1)S(1)}, bf16[1,64,2048]{2,1,0:T(8,128)(2,1)}, u32[]{:S(2)}) copy-start(bf16[1,64,2048]{2,1,0:T(8,128)(2,1)} %param.13) | copy-start | bytes 786436
  17.9 1.6 %copy-start.12 = (bf16[64,2048]{1,0:T(8,128)(2,1)S(1)}, bf16[64,2048]{1,0:T(8,128)(2,1)}, u32[]{:S(2)}) copy-start(bf16[64,2048]{1,0:T(8,128)(2,1)} %refs_0_.1) | copy-start | bytes 786436
  17.9 1.6 %copy-start.14 = (f32[1,2048]{1,0:T(1,128)S(1)}, f32[1,2048]{1,0:T(1,128)}, u32[]{:S(2)}) copy-start(f32[1,2048]{1,0:T(1,128)} %refs_3_.7) | copy-start | bytes 24580
  17.9 4.0 %copy-start.7 = (bf16[1,128,2048]{2,1,0:T(8,128)(2,1)S(1)}, bf16[1,128,2048]{2,1,0:T(8,128)(2,1)}, u32[]{:S(2)}) copy-start(bf16[1,128,2048]{2,1,0:T(8,128)(2,1)} %param.11) | copy-start | bytes 1572868
  17.9 1.6 %collective-permute-start.1 = (bf16[64,2048]{1,0:T(8,128)(2,1)S(1)}, bf16[64,2048]{1,0:T(8,128)(2,1)S(1)}, u32[]{:S(2)}, u32[]{:S(2)}) collective-permute-start(bf16[64,2048]{1,0:T(8,128)(2,1)S(1)} %get-tuple-element.20), channel_id=1, source_target_pairs={{0,1},{1,0},{2,3},{3,2},{4,5},{5,4},{6,7},{7,6},{8,9},{9,8},{10,11... | collective-permute-start | bytes 786440 | tf_op jit(solution)/shard_map/ppermute | solution.py:233
  19.5 0.7 collective-permute-start.2
  20.2 1.6 %collective-permute-start.3 = (bf16[64,2048]{1,0:T(8,128)(2,1)S(1)}, bf16[64,2048]{1,0:T(8,128)(2,1)S(1)}, u32[]{:S(2)}, u32[]{:S(2)}) collective-permute-start(bf16[64,2048]{1,0:T(8,128)(2,1)S(1)} %collective-permute-done.2.own_ref.refs_1_), channel_id=1, source_target_pairs={{1,0},{0,1},{3,2},{2,3},{5,4},{4,5},{7,6},{6,7},{9,8},{8,9},{11,10... | collective-permute-start | bytes 786440 | tf_op jit(solution)/shard_map/ppermute | solution.py:227
  21.8 3.4 %copy-start.1 = (bf16[1,2048,2048]{2,1,0:T(8,128)(2,1)S(1)}, bf16[1,2048,2048]{2,1,0:T(8,128)(2,1)}, u32[]{:S(2)}) copy-start(bf16[1,2048,2048]{2,1,0:T(8,128)(2,1)} %param.10) | copy-start | bytes 25165828
  25.2 3.4 %copy-start.5 = (bf16[1,2048,2048]{2,1,0:T(8,128)(2,1)S(1)}, bf16[1,2048,2048]{2,1,0:T(8,128)(2,1)}, u32[]{:S(2)}) copy-start(bf16[1,2048,2048]{2,1,0:T(8,128)(2,1)} %param.9) | copy-start | bytes 25165828
  28.6 4.0 %copy-start.2 = (bf16[1,2048,2048]{2,1,0:T(8,128)(2,1)S(1)}, bf16[1,2048,2048]{2,1,0:T(8,128)(2,1)}, u32[]{:S(2)}) copy-start(bf16[1,2048,2048]{2,1,0:T(8,128)(2,1)} %param.10) | copy-start | bytes 25165828
  28.6 1.5 %collective-permute-start.4 = (bf16[64,2048]{1,0:T(8,128)(2,1)S(1)}, bf16[64,2048]{1,0:T(8,128)(2,1)S(1)}, u32[]{:S(2)}, u32[]{:S(2)}) collective-permute-start(bf16[64,2048]{1,0:T(8,128)(2,1)S(1)} %get-tuple-element.22), channel_id=1, source_target_pairs={{0,1},{1,0},{2,3},{3,2},{4,5},{5,4},{6,7},{7,6},{8,9},{9,8},{10,11... | collective-permute-start | bytes 786440 | tf_op jit(solution)/shard_map/ppermute | solution.py:233
  30.1 0.8 collective-permute-start.5
  31.0 1.6 %collective-permute-start.6 = (bf16[64,2048]{1,0:T(8,128)(2,1)S(1)}, bf16[64,2048]{1,0:T(8,128)(2,1)S(1)}, u32[]{:S(2)}, u32[]{:S(2)}) collective-permute-start(bf16[64,2048]{1,0:T(8,128)(2,1)S(1)} %collective-permute-done.5.own_ref.refs_1_.refs_2_), channel_id=1, source_target_pairs={{1,0},{0,1},{3,2},{2,3},{5,4},{4,5},{7,6},{6,7},{9,8},{8,9},{11,10... | collective-permute-start | bytes 786440 | tf_op jit(solution)/shard_map/ppermute | solution.py:227
  32.6 1.5 %collective-permute-start.7 = (bf16[64,2048]{1,0:T(8,128)(2,1)S(1)}, bf16[64,2048]{1,0:T(8,128)(2,1)S(1)}, u32[]{:S(2)}, u32[]{:S(2)}) collective-permute-start(bf16[64,2048]{1,0:T(8,128)(2,1)S(1)} %get-tuple-element.24), channel_id=1, source_target_pairs={{0,1},{1,0},{2,3},{3,2},{4,5},{5,4},{6,7},{7,6},{8,9},{9,8},{10,11... | collective-permute-start | bytes 786440 | tf_op jit(solution)/shard_map/ppermute | solution.py:233
  34.1 42.7 %collective-permute-start.8 = (bf16[64,2048]{1,0:T(8,128)(2,1)S(1)}, bf16[64,2048]{1,0:T(8,128)(2,1)S(1)}, u32[]{:S(2)}, u32[]{:S(2)}) collective-permute-start(bf16[64,2048]{1,0:T(8,128)(2,1)S(1)} %norm_step.6.refs_6_), channel_id=1, source_target_pairs={{8,0},{9,1},{10,2},{11,3},{12,4},{13,5},{14,6},{15,7}} | collective-permute-start | bytes 786440 | tf_op jit(solution)/shard_map/ppermute | solution.py:276
  76.7 1.5 %collective-permute-start.9 = (bf16[64,2048]{1,0:T(8,128)(2,1)S(1)}, bf16[64,2048]{1,0:T(8,128)(2,1)S(1)}, u32[]{:S(2)}, u32[]{:S(2)}) collective-permute-start(bf16[64,2048]{1,0:T(8,128)(2,1)S(1)} %collective-permute-done.8.own_ref.refs_1_.refs_3_), channel_id=1, source_target_pairs={{1,0},{0,1},{3,2},{2,3},{5,4},{4,5},{7,6},{6,7},{9,8},{8,9},{11,10... | collective-permute-start | bytes 786440 | tf_op jit(solution)/shard_map/ppermute | solution.py:227
  82.8 8.5 %collective-permute-start.10 = (bf16[64,2048]{1,0:T(8,128)(2,1)S(1)}, bf16[64,2048]{1,0:T(8,128)(2,1)S(1)}, u32[]{:S(2)}, u32[]{:S(2)}) collective-permute-start(bf16[64,2048]{1,0:T(8,128)(2,1)S(1)} %get-tuple-element.26), channel_id=1, source_target_pairs={{0,1},{1,0},{2,3},{3,2},{4,5},{5,4},{6,7},{7,6},{8,9},{9,8},{10,11... | collective-permute-start | bytes 786440 | tf_op jit(solution)/shard_map/ppermute | solution.py:233
  83.0 4.4 %collective-permute-start.11 = (bf16[64,512]{1,0:T(8,128)(2,1)S(1)}, bf16[64,512]{1,0:T(8,128)(2,1)S(1)}, u32[]{:S(2)}, u32[]{:S(2)}) collective-permute-start(bf16[64,512]{1,0:T(8,128)(2,1)S(1)} %get-tuple-element.28), channel_id=1, source_target_pairs={{0,2},{2,0},{4,6},{6,4},{1,3},{3,1},{5,7},{7,5},{8,10},{10,8},{12,... | collective-permute-start | bytes 196616 | tf_op jit(solution)/shard_map/ppermute | solution.py:263
  84.6 4.3 %collective-permute-start.12 = (bf16[64,512]{1,0:T(8,128)(2,1)S(1)}, bf16[64,512]{1,0:T(8,128)(2,1)S(1)}, u32[]{:S(2)}, u32[]{:S(2)}) collective-permute-start(bf16[64,512]{1,0:T(8,128)(2,1)S(1)} %get-tuple-element.29), channel_id=1, source_target_pairs={{0,4},{2,6},{4,0},{6,2},{1,5},{3,7},{5,1},{7,3},{8,12},{10,14},{12... | collective-permute-start | bytes 196616 | tf_op jit(solution)/shard_map/ppermute | solution.py:263
  86.1 5.2 %collective-permute-start.13 = (bf16[64,512]{1,0:T(8,128)(2,1)S(1)}, bf16[64,512]{1,0:T(8,128)(2,1)S(1)}, u32[]{:S(2)}, u32[]{:S(2)}) collective-permute-start(bf16[64,512]{1,0:T(8,128)(2,1)S(1)} %get-tuple-element.30), channel_id=1, source_target_pairs={{0,6},{2,4},{4,2},{6,0},{1,7},{3,5},{5,3},{7,1},{8,14},{10,12},{12... | collective-permute-start | bytes 196616 | tf_op jit(solution)/shard_map/ppermute | solution.py:263
  86.6 5.7 %collective-permute-start.14 = (bf16[64,512]{1,0:T(8,128)(2,1)S(1)}, bf16[64,512]{1,0:T(8,128)(2,1)S(1)}, u32[]{:S(2)}, u32[]{:S(2)}) collective-permute-start(bf16[64,512]{1,0:T(8,128)(2,1)S(1)} %get-tuple-element.27.refs_0_), channel_id=1, source_target_pairs={{1,0},{0,1},{3,2},{2,3},{5,4},{4,5},{7,6},{6,7},{9,8},{8,9},{11,10... | collective-permute-start | bytes 196616 | tf_op jit(solution)/shard_map/ppermute | solution.py:227
  87.5 4.8 %collective-permute-start.15 = (bf16[64,512]{1,0:T(8,128)(2,1)S(1)}, bf16[64,512]{1,0:T(8,128)(2,1)S(1)}, u32[]{:S(2)}, u32[]{:S(2)}) collective-permute-start(bf16[64,512]{1,0:T(8,128)(2,1)S(1)} %collective-permute-done.11.refs_1_), channel_id=1, source_target_pairs={{1,0},{0,1},{3,2},{2,3},{5,4},{4,5},{7,6},{6,7},{9,8},{8,9},{11,10... | collective-permute-start | bytes 196616 | tf_op jit(solution)/shard_map/ppermute | solution.py:227
  88.9 3.4 %collective-permute-start.16 = (bf16[64,512]{1,0:T(8,128)(2,1)S(1)}, bf16[64,512]{1,0:T(8,128)(2,1)S(1)}, u32[]{:S(2)}, u32[]{:S(2)}) collective-permute-start(bf16[64,512]{1,0:T(8,128)(2,1)S(1)} %collective-permute-done.12.refs_2_), channel_id=1, source_target_pairs={{1,0},{0,1},{3,2},{2,3},{5,4},{4,5},{7,6},{6,7},{9,8},{8,9},{11,10... | collective-permute-start | bytes 196616 | tf_op jit(solution)/shard_map/ppermute | solution.py:227
  91.3 1.3 %collective-permute-start.17 = (bf16[64,512]{1,0:T(8,128)(2,1)S(1)}, bf16[64,512]{1,0:T(8,128)(2,1)S(1)}, u32[]{:S(2)}, u32[]{:S(2)}) collective-permute-start(bf16[64,512]{1,0:T(8,128)(2,1)S(1)} %collective-permute-done.13.refs_3_), channel_id=1, source_target_pairs={{1,0},{0,1},{3,2},{2,3},{5,4},{4,5},{7,6},{6,7},{9,8},{8,9},{11,10... | collective-permute-start | bytes 196616 | tf_op jit(solution)/shard_map/ppermute | solution.py:227
  92.5 3.4 %copy-start.3 = (bf16[1,2048,2048]{2,1,0:T(8,128)(2,1)S(1)}, bf16[1,2048,2048]{2,1,0:T(8,128)(2,1)}, u32[]{:S(2)}) copy-start(bf16[1,2048,2048]{2,1,0:T(8,128)(2,1)} %param.10) | copy-start | bytes 25165828
  95.9 2.2 %copy-start.8 = (f32[1,512,2048]{2,1,0:T(8,128)S(1)}, f32[1,512,2048]{2,1,0:T(8,128)}, u32[]{:S(2)}) copy-start(f32[1,512,2048]{2,1,0:T(8,128)} %param.16) | copy-start | bytes 12582916
  98.1 2.2 %copy-start.9 = (f32[1,512,2048]{2,1,0:T(8,128)S(1)}, f32[1,512,2048]{2,1,0:T(8,128)}, u32[]{:S(2)}) copy-start(f32[1,512,2048]{2,1,0:T(8,128)} %param.17) | copy-start | bytes 12582916
  100.3 1.6 %copy-start.13 = (bf16[1,512,2048]{2,1,0:T(8,128)(2,1)S(1)}, bf16[1,512,2048]{2,1,0:T(8,128)(2,1)}, u32[]{:S(2)}) copy-start(bf16[1,512,2048]{2,1,0:T(8,128)(2,1)} %all-gather.3.cloned.1.call-done) | copy-start | bytes 6291460
Sparse Core Ops, SparseCore 0:
  18.5 42.2 all-gather.2

commit v2 on v1

v2 whole, which is shorter than its diff:
```python
import functools
import jax
import jax.numpy as jnp
from jax import lax
from jax.experimental import pallas as pl
from jax.experimental.pallas import tpu as pltpu
from jax.sharding import PartitionSpec as P

EPS_NORM = 1e-05
EPS_ADAM = 1e-08
BETA_ONE = 0.9
BETA_TWO = 0.95
RATE = 0.01
DECAY = 0.1
CORRECT_ONE = 1.0 - 0.9**10
CORRECT_TWO = 1.0 - 0.95**10

MIB = 2**20
VMEM = pl.BlockSpec(memory_space=pltpu.VMEM)
CHEAP = pl.CostEstimate(flops=0, bytes_accessed=0, transcendentals=0)
F32 = jnp.float32
BF16 = jnp.bfloat16


def tile_of(extent, most):
    tile = min(extent, most)
    while extent % tile:
        tile //= 2
    return tile


def copies(pairs, sem, chunks):
    started = []
    for n, (source, target) in enumerate(pairs):
        rows = source.shape[0] // chunks
        cut = [slice(c * rows, (c + 1) * rows) for c in range(chunks)]
        started.append(
            [pltpu.make_async_copy(source.at[r], target.at[r], sem.at[n, c]) for c, r in enumerate(cut)]
        )
    for array in started:
        for copy in array:
            copy.start()
    return started


def stage(arrays, split=(), after=()):
    pieces = [(n, slice(None)) for n in range(len(arrays))]
    for n, array in enumerate(split, len(arrays)):
        half = array.shape[0] // 2
        pieces += [(n, slice(0, half)), (n, slice(half, 2 * half))]
    arrays = [*arrays, *split]
    shapes = [(arrays[n][rows].shape if rows.start is not None else arrays[n].shape) for n, rows in pieces]
    count = len(arrays)

    def kernel(*refs):
        sources, targets, sem = refs[:count], refs[count + len(after) : -1], refs[-1]
        pairs = [(sources[n].at[rows], target) for (n, rows), target in zip(pieces, targets)]
        for array in copies(pairs, sem, 2):
            for copy in array:
                copy.wait()

    return pl.pallas_call(
        kernel,
        out_shape=[pltpu.VMEM(shape, arrays[n].dtype) for (n, _), shape in zip(pieces, shapes)],
        in_specs=[pl.BlockSpec(memory_space=pltpu.HBM)] * count
        + [pl.BlockSpec(memory_space=pl.ANY)] * len(after),
        out_specs=[VMEM] * len(pieces),
        scratch_shapes=[pltpu.SemaphoreType.DMA((len(pieces), 2))],
        compiler_params=pltpu.CompilerParams(vmem_limit_bytes=4 * MIB),
        cost_estimate=pl.CostEstimate(
            flops=0, bytes_accessed=sum(2 * a.size * a.dtype.itemsize for a in arrays), transcendentals=0
        ),
        name="stage",
    )(*[pltpu.with_memory_space_constraint(a, pltpu.HBM) for a in arrays], *after)


def stage_in_section(arrays, wanted, held, after):
    count = len(arrays)

    def kernel(*refs):
        sources, targets, sem = refs[:count], refs[count + len(held) + len(after) : -1], refs[-1]

        @pl.when(wanted(lax.axis_index("pipe")))
        def _():
            for array in copies(list(zip(sources, targets)), sem, 2):
                for copy in array:
                    copy.wait()

    return pl.pallas_call(
        kernel,
        out_shape=[pltpu.VMEM(a.shape, a.dtype) for a in arrays],
        in_specs=[pl.BlockSpec(memory_space=pltpu.HBM)] * count
        + [VMEM] * len(held)
        + [pl.BlockSpec(memory_space=pl.ANY)] * len(after),
        out_specs=[VMEM] * count,
        input_output_aliases={count + n: n for n in range(len(held))},
        scratch_shapes=[pltpu.SemaphoreType.DMA((count, 2))],
        compiler_params=pltpu.CompilerParams(vmem_limit_bytes=4 * MIB),
        cost_estimate=CHEAP,
        name="stage_in_section",
    )(*[pltpu.with_memory_space_constraint(a, pltpu.HBM) for a in arrays], *held, *after)


def unit_grads(parts, share, rows_ref, down_ref, gate_ref, unit_ref):
    me = lax.axis_index("tensor")
    term = jnp.dot(rows_ref[...], down_ref[...], preferred_element_type=F32)
    for k in range(parts):
        at = pl.multiple_of(lax.rem(me + k, parts) * share, share)
        gates = gate_ref[pl.ds(at, share), :].astype(F32)
        unit_ref[k * share : (k + 1) * share, :] = (term[k * share : (k + 1) * share] * gates).astype(BF16)


def hand_out(share, term, cols, kept_ref, sent_refs):
    kept_ref[:, cols] = term[0:share]
    for k, ref in enumerate(sent_refs, 1):
        ref[:, cols] = term[k * share : (k + 1) * share].astype(BF16)


def fill_rows(share, rows_ref, own_ref, peer_refs):
    rows_ref[0:share, :] = own_ref[...]
    at, row = 0, share
    for ref in peer_refs:
        rows_ref[row : row + share, at : at + ref.shape[1]] = ref[...]
        at += ref.shape[1]
        if at == rows_ref.shape[1]:
            at, row = 0, row + share


def step_kernel(layer, parts, pieces, own_ref, *refs):
    peer_refs, refs = refs[:pieces], refs[pieces:]
    down_ref, turned_ref, gate_ref, kept_ref = refs[:4]
    sent_refs = refs[4 : parts + 3]
    rows_ref, unit_ref = refs[parts + 3 :]
    share = own_ref.shape[0]

    @pl.when(lax.axis_index("pipe") == layer)
    def _():
        fill_rows(share, rows_ref, own_ref, peer_refs)
        unit_grads(parts, share, rows_ref, down_ref, gate_ref, unit_ref)
        term = jnp.dot(unit_ref[...], turned_ref[...], preferred_element_type=F32)
        hand_out(share, term, slice(None), kept_ref, sent_refs)


def first_kernel(layer, parts, pieces, own_ref, *refs):
    peer_refs, refs = refs[:pieces], refs[pieces:]
    down_ref, up_ref, gate_ref, turned_ref, kept_ref = refs[:5]
    sent_refs = refs[5 : parts + 4]
    rows_ref, unit_ref, held_ref, sem = refs[parts + 4 :]
    share = own_ref.shape[0]
    chunks = sem.shape[1]
    size = held_ref.shape[0] // chunks
    (arriving,) = copies([(up_ref, held_ref)], sem, chunks)
    starts = lax.axis_index("pipe") == layer

    @pl.when(starts)
    def _():
        fill_rows(share, rows_ref, own_ref, peer_refs)
        unit_grads(parts, share, rows_ref, down_ref, gate_ref, unit_ref)

    for c in range(chunks):
        cols = slice(c * size, (c + 1) * size)
        arriving[c].wait()

        @pl.when(starts)
        def _(cols=cols):
            term = lax.dot_general(
                unit_ref[...], held_ref[cols, :], (((1,), (1,)), ((), ())), preferred_element_type=F32
            )
            hand_out(share, term, cols, kept_ref, sent_refs)

        @pl.when(jnp.logical_not(starts))
        def _(cols=cols):
            turned_ref[:, cols] = held_ref[cols, :].T


def section_step(layer, own, peers, w_down, turned, gates, w_up=None, after=()):
    share, width = own.shape
    units = w_down.shape[1]
    pieces = len(peers)
    parts = sum(p.size for p in peers) // own.size + 1
    rows = share * parts
    first = w_up is not None
    out_shape = [jax.ShapeDtypeStruct((share, width), F32)]
    out_shape += [jax.ShapeDtypeStruct((share, width), BF16)] * (parts - 1)
    scratch = [pltpu.VMEM((rows, width), BF16), pltpu.VMEM((rows, units), BF16)]
    in_specs = [VMEM] * (pieces + 4) + [pl.BlockSpec(memory_space=pl.ANY)] * len(after)
    body = functools.partial(first_kernel if first else step_kernel, layer, parts, pieces)

    def kernel(*refs):
        body(*refs[: pieces + 4], *refs[pieces + 4 + len(after) :])

    if first:
        out_shape = [pltpu.VMEM((units, width), BF16)] + out_shape
        scratch += [pltpu.VMEM((width, units), BF16), pltpu.SemaphoreType.DMA((1, 4))]
        in_specs[pieces + 2] = pl.BlockSpec(memory_space=pltpu.HBM)
        operand = pltpu.with_memory_space_constraint(w_up, pltpu.HBM)
    else:
        operand = turned
    outs = pl.pallas_call(
        kernel,
        out_shape=out_shape,
        in_specs=in_specs,
        out_specs=[VMEM] * len(out_shape),
        scratch_shapes=scratch,
        compiler_params=pltpu.CompilerParams(vmem_limit_bytes=(20 if first else 12) * MIB),
        cost_estimate=CHEAP,
        name="section_step",
    )(own, *peers, w_down, operand, gates, *after)
    return outs


def norm_kernel(layer, parts, earlier, owners, passed, handed, kept_ref, *refs):
    arrived = refs[: parts - 1]
    up_ref, in_ref, gain_ref = refs[parts - 1 : parts + 2]
    refs = refs[parts + 2 :]
    earlier_refs, refs = refs[:earlier], refs[earlier:]
    first_ref, pass_refs, refs = refs[0], refs[1 : 1 + passed], refs[1 + passed :]
    out_ref, block_refs, handed_refs = refs[0], refs[1 : len(refs) - handed], refs[len(refs) - handed :]
    segment = lax.axis_index("pipe")

    def cut(source):
        size = source.shape[1] // owners
        for k, ref in enumerate(block_refs, 1):
            at = pl.multiple_of((lax.axis_index("dp") ^ k) * size, size)
            ref[...] = source[:, pl.ds(at, size)]

    @pl.when(segment == layer)
    def _():
        normed = kept_ref[...]
        for ref in arrived:
            normed = normed + ref[...].astype(F32)
        rows_in = in_ref[...].astype(F32)
        inverse_rms = lax.rsqrt(jnp.mean(rows_in * rows_in, axis=-1, keepdims=True) + EPS_NORM)
        scaled = normed * gain_ref[...]
        mean_term = jnp.mean(rows_in * scaled, axis=-1, keepdims=True)
        out_ref[...] = (
            up_ref[...].astype(F32)
            + inverse_rms * scaled
            - rows_in * (inverse_rms * inverse_rms * inverse_rms * mean_term)
        ).astype(BF16)
        cut(out_ref)

    for above, ref in enumerate(earlier_refs):

        @pl.when(segment == layer + earlier - above)
        def _(ref=ref):
            cut(ref)
            if layer == 0:
                out_ref[...] = ref[...]

    if block_refs:

        @pl.when(segment == 0)
        def _():
            cut(first_ref)

    sources = list(pass_refs)
    for target in handed_refs:
        at = 0
        while at < target.shape[0]:
            source = sources.pop(0)
            target[at : at + source.shape[0], :] = source[...]
            at += source.shape[0]


def norm_step(layer, kept, arrived, upstream, rows_in, gain, first, earlier=(), owners=1, passed=()):
    parts = len(arrived) + 1
    share, width = upstream.shape
    block = jax.ShapeDtypeStruct((share, width // owners), BF16)
    handed = [
        jax.ShapeDtypeStruct((sum(p.shape[0] for p in group), group[0].shape[1]), BF16) for group in passed
    ]
    passed = [p for group in passed for p in group]
    outs = pl.pallas_call(
        functools.partial(norm_kernel, layer, parts, len(earlier), owners, len(passed), len(handed)),
        out_shape=[jax.ShapeDtypeStruct(upstream.shape, BF16)]
        + [block] * (owners - 1)
        + handed,
        in_specs=[VMEM] * (parts + 4 + len(earlier) + len(passed)),
        out_specs=[VMEM] * (owners + len(handed)),
        compiler_params=pltpu.CompilerParams(vmem_limit_bytes=8 * MIB),
        cost_estimate=CHEAP,
        name="norm_step",
    )(kept, *arrived, upstream, rows_in, gain, *earlier, first, *passed)
    return outs[0], outs[1:owners], outs[owners:]


def collect_kernel(sections, *refs):
    upstream_refs, block_refs, out_ref = refs[:sections], refs[sections:-1], refs[-1]
    share, size = block_refs[0].shape
    at = pl.multiple_of(lax.axis_index("dp") * size, size)
    for s, ref in enumerate(upstream_refs):

        @pl.when(lax.axis_index("pipe") == sections - 1 - s)
        def _(ref=ref):
            out_ref[0:share, :] = ref[:, pl.ds(at, size)]

    for k, ref in enumerate(block_refs, 1):
        out_ref[k * share : (k + 1) * share, :] = ref[...]


def collect(upstreams, blocks, after):
    sections = len(upstreams)
    owners = len(blocks) + 1
    share, size = blocks[0].shape
    count = sections + len(blocks)

    def kernel(*refs):
        collect_kernel(sections, *refs[:count], refs[-1])

    return pl.pallas_call(
        kernel,
        out_shape=jax.ShapeDtypeStruct((owners * share, size), BF16),
        in_specs=[VMEM] * count + [pl.BlockSpec(memory_space=pl.ANY)] * len(after),
        out_specs=VMEM,
        compiler_params=pltpu.CompilerParams(vmem_limit_bytes=4 * MIB),
        cost_estimate=CHEAP,
        name="collect",
    )(*upstreams, *blocks, *after)


def adam_update(gradient, current, moment_one, moment_two):
    first = BETA_ONE * moment_one + (1.0 - BETA_ONE) * gradient
    second = BETA_TWO * moment_two + (1.0 - BETA_TWO) * gradient * gradient
    scaled = second * (1.0 / CORRECT_TWO)
    root = scaled * lax.rsqrt(scaled)
    step = (first * (RATE / CORRECT_ONE)) / (root + EPS_ADAM)
    return first, second, (1.0 - RATE * DECAY) * current - step


def adam_kernel(sizes, *refs):
    owners, parts, share, tile = sizes
    up_refs = refs[:parts]
    hidden_ref, down_ref, one_ref, two_ref = refs[parts : parts + 4]
    outs = refs[parts + 4 : parts + 7]
    rows_ref, turned_ref, *results, sem = refs[parts + 7 :]
    rows = turned_ref.shape[0]
    me = lax.axis_index("dp")
    part = lax.axis_index("tensor")
    for p in range(parts):
        for k in range(owners):
            at = k * parts + lax.rem(part + p, parts)
            rows_ref[pl.ds(pl.multiple_of(at * share, share), share), :] = up_refs[p][
                k * share : (k + 1) * share, :
            ]
    turned_ref[...] = rows_ref[...].T
    writes = []
    for i in range(rows // tile):
        cut = slice(i * tile, (i + 1) * tile)
        gradient = jnp.dot(turned_ref[cut, :], hidden_ref[...], preferred_element_type=F32)
        current = down_ref[pl.ds(pl.multiple_of(me * rows + i * tile, tile), tile), :].astype(F32)
        updates = adam_update(gradient, current, one_ref[cut, :], two_ref[cut, :])
        for q, update in enumerate(updates):
            results[q][cut, :] = update
            writes.append(pltpu.make_async_copy(results[q].at[cut], outs[q].at[cut], sem.at[i, q]))
            writes[-1].start()
    for write in writes:
        write.wait()


def adam_step(blocks, hidden_all, w_down, moment_one, moment_two, owners, parts):
    rows, units = moment_one.shape
    tokens = hidden_all.shape[0]
    tile = tile_of(rows, 128)
    return pl.pallas_call(
        functools.partial(adam_kernel, (owners, parts, blocks[0].shape[0] // owners, tile)),
        out_shape=[jax.ShapeDtypeStruct((rows, units), F32)] * 3,
        in_specs=[VMEM] * (len(blocks) + 4),
        out_specs=[pl.BlockSpec(memory_space=pl.ANY)] * 3,
        scratch_shapes=[pltpu.VMEM((tokens, rows), BF16), pltpu.VMEM((rows, tokens), BF16)]
        + [pltpu.VMEM((rows, units), F32)] * 3
        + [pltpu.SemaphoreType.DMA((rows // tile, 3))],
        compiler_params=pltpu.CompilerParams(vmem_limit_bytes=18 * MIB),
        cost_estimate=CHEAP,
        name="adam_step",
    )(*blocks, hidden_all, w_down, moment_one, moment_two)


def columns(array, count):
    rows, cols = array.shape
    size = cols // count

    def kernel(source, *targets):
        for n, target in enumerate(targets):
            target[...] = source[:, n * size : (n + 1) * size]

    return pl.pallas_call(
        kernel,
        out_shape=[jax.ShapeDtypeStruct((rows, size), array.dtype)] * count,
        in_specs=[VMEM],
        out_specs=[VMEM] * count,
        compiler_params=pltpu.CompilerParams(vmem_limit_bytes=4 * MIB),
        cost_estimate=CHEAP,
        name="columns",
    )(array)


def stack(order, size):
    count = len(order)
    cols = order[0][0].shape[1]

    def kernel(*refs):
        out, sem = refs[-2:]
        started = [
            pltpu.make_async_copy(
                refs[n].at[at : at + size], out.at[n * size : (n + 1) * size], sem.at[n]
            )
            for n, (_, at) in enumerate(order)
        ]
        for copy in started:
            copy.start()
        for copy in started:
            copy.wait()

    return pl.pallas_call(
        kernel,
        out_shape=pltpu.VMEM((count * size, cols), BF16),
        in_specs=[pl.BlockSpec(memory_space=pl.ANY)] * count,
        out_specs=VMEM,
        scratch_shapes=[pltpu.SemaphoreType.DMA((count,))],
        compiler_params=pltpu.CompilerParams(vmem_limit_bytes=4 * MIB),
        cost_estimate=CHEAP,
        name="stack",
    )(*[array for array, _ in order])


def adam_general(upstreams, hidden_all, w_down, moment_one, moment_two):
    owners = lax.axis_size("dp")
    sections = len(upstreams)
    segment = lax.axis_index("pipe")
    own = upstreams[0]
    for s in range(1, sections):
        own = jnp.where(segment == sections - 1 - s, upstreams[s], own)
    mine = lax.all_to_all(own, "dp", split_axis=1, concat_axis=0, tiled=True)
    share, rows = own.shape[0], mine.shape[1]
    turned = lax.all_gather(mine.reshape(owners, share, rows), "tensor", axis=1, tiled=True)
    gradient = lax.dot_general(
        turned.reshape(-1, rows), hidden_all, (((0,), (0,)), ((), ())), preferred_element_type=F32
    )
    at = lax.axis_index("dp") * rows
    current = lax.dynamic_slice_in_dim(w_down, at, rows, 0).astype(F32)
    return adam_update(gradient, current, moment_one, moment_two)


def from_peers(value, axis):
    size = lax.axis_size(axis)
    return [lax.ppermute(value, axis, [((i + k) % size, i) for i in range(size)]) for k in range(1, size)]


def to_peers(values, axis):
    size = lax.axis_size(axis)
    return [
        lax.ppermute(value, axis, [(i, (i + k) % size) for i in range(size)])
        for k, value in enumerate(values, 1)
    ]


def on_device(
    up_weight,
    down_weight,
    gate_act,
    hidden,
    block_input,
    norm_gain,
    loss_grad,
    moment_one,
    moment_two,
):
    sections = lax.axis_size("pipe")
    owners = lax.axis_size("dp")
    parts = lax.axis_size("tensor")
    planned = sections == 4 and owners == 4 and block_input.shape[2] % (128 * owners) == 0
    share = loss_grad.shape[0]
    saved = hidden[0]
    w_down, gates, rows_in, loss, *halves = stage(
        [down_weight[0], gate_act[0], block_input[0], loss_grad], [saved] if planned else []
    )
    turned = None
    upstreams = [loss]
    grads = []
    blocks = []
    late = ()
    for layer in reversed(range(sections)):
        upstream = upstreams[-1]
        if planned and not layer:
            arrivals = [from_peers(piece, "tensor") for piece in columns(upstream, owners)]
            peers = [piece for peer in zip(*arrivals) for piece in peer]
        else:
            peers = from_peers(upstream if grads else loss_grad, "tensor")
        if not grads:
            turned, kept, *sent = section_step(layer, upstream, peers, w_down, None, gates, up_weight[0])
        else:
            kept, *sent = section_step(layer, upstream, peers, w_down, turned, gates, after=late)
        arrived = to_peers(sent, "tensor")
        window = len(grads)
        moving = ()
        if planned and window == 0:
            moving = [halves[:1], halves[1:]]
        elif planned and window == 1:
            moving = [(halves[1], side_lower), (halves[0], along_upper)]
        grad, cuts, handed = norm_step(
            layer,
            kept,
            arrived,
            upstream,
            rows_in,
            norm_gain,
            loss,
            earlier=grads if window >= sections - 2 else (),
            owners=owners if planned and layer == 1 else 1,
            passed=moving,
        )
        grads.append(grad)
        if layer:
            upstreams.append(lax.ppermute(grad, "pipe", [(layer, layer - 1)]))
        if planned and layer:
            for k, cut in enumerate(cuts, 1):
                pairs = [
                    (s * owners + i, (s - 1) % sections * owners + (i ^ k))
                    for s in range(sections)
                    for i in range(owners)
                ]
                blocks.append(lax.ppermute(cut, ("pipe", "dp"), pairs))
            if window < 2:
                exchange = [
                    lax.ppermute(piece, "dp", [(i, i ^ k) for i in range(owners)])
                    for k, piece in enumerate(handed, 1)
                ]
            if window == 0:
                along_upper, side_lower = exchange
                moments = stage_in_section(
                    [moment_one[0], moment_two[0]], lambda section: section != sections - 2, (), [grad]
                )
                late = [*exchange, *moments]
            elif window == 1:
                along_rest, side_rest = late = exchange
            else:
                late = moments = stage_in_section(
                    [moment_one[0], moment_two[0]], lambda section: section == sections - 2, moments, [grad]
                )
    if planned:
        half = saved.shape[0] // 2
        order = [
            (halves[0], 0),
            (halves[1], 0),
            (along_upper, 0),
            (along_rest, 0),
            (side_rest, 0),
            (side_lower, 0),
            (side_rest, half),
            (along_rest, half),
        ]
        hidden_all = stack(order, half)
        own = collect(upstreams, blocks, [kept, hidden_all])
        first, second, updated = adam_step(
            [own, *from_peers(own, "tensor")], hidden_all, w_down, *moments, owners, parts
        )
    else:
        hidden_all = lax.all_gather(saved, "dp", axis=0, tiled=True)
        first, second, updated = adam_general(
            upstreams, hidden_all, w_down, moment_one[0], moment_two[0]
        )
    return (grads[-1][None], first[None], second[None], updated[None])


def solution(mesh):
    in_specs = (
        P("pipe", None, "tensor"),
        P("pipe", None, "tensor"),
        P("pipe", "dp", "tensor"),
        P("pipe", "dp", "tensor"),
        P("pipe", ("dp", "tensor"), None),
        P("pipe", None),
        P(("dp", "tensor"), None),
        P("pipe", "dp", "tensor"),
        P("pipe", "dp", "tensor"),
    )
    out_specs = (
        P("pipe", ("dp", "tensor"), None),
        P("pipe", "dp", "tensor"),
        P("pipe", "dp", "tensor"),
        P("pipe", "dp", "tensor"),
    )
    return jax.shard_map(
        on_device, mesh=mesh, in_specs=in_specs, out_specs=out_specs, check_vma=False
    )
```

time: 118 us -> 71.2 us (0.60)
  local copies, waits for them, and re-layouts: 24.9 us -> 0.01 us
  waiting for transfers between devices: 55 us -> 34.1 us
  between operations: 14.1 us -> 0.97 us
  Pallas kernels: 13.9 us -> 21.2 us
  starting transfers between devices: 9.15 us -> 14.7 us
    ppermute x3, waiting for transfers between devices: 41.4 us -> 11.7 us  [on_device(): upstreams.append(lax.ppermute(grad, 'pipe', [(layer, layer - 1)]))]
    unnamed x30 -> x2, local copies, waits for them, and re-layouts: 24.9 us -> 0.01 us
    ppermute x3 -> x7, waiting for transfers between devices: 4.67 us -> 15.4 us  [the longest x4 13.7 us: on_device(): lax.ppermute(piece, 'dp', [(i, i ^ k) for i in range(owners)])]
    pallas_call x10 -> x15, Pallas kernels: 13.9 us -> 21.2 us  [the longest x4 6.61 us: section_step(): pl.pallas_call(kernel, out_shape=out_shape, in_specs=in_specs, out_specs=...]
    ppermute x3 -> x7, starting transfers between devices: 3.57 us -> 10.2 us  [the longest x4 6.34 us: on_device(): lax.ppermute(piece, 'dp', [(i, i ^ k) for i in range(owners)])]
    ppermute x8, waiting for transfers between devices: 5.46 us -> 2.41 us  [from_peers(): lax.ppermute(value, axis, [((i + k) % size, i) for i in range(size)])]
    ppermute x4, starting transfers between devices: 1.38 us -> 0.2 us  [to_peers(): lax.ppermute(value, axis, [(i, (i + k) % size) for i in range(size)])]
  transfers between devices with their start and end apart: 19 -> 22, of which waited for: 12 -> 14; matrix products, arithmetic and copies ran while one was open for 0% -> 0% of each run, Pallas kernels for 5% -> 16%
where the time goes in v2:
time: 71.2 us; the launch traced here: 71 us
  waiting for transfers between devices  34.1 us (48%)
  Pallas kernels  21.2 us (30%)
  starting transfers between devices  14.7 us (21%)
  between operations  0.97 us (1%)
    ppermute x4, waiting for transfers between devices, on_device(): lax.ppermute(piece, 'dp', [(i, i ^ k) for i in range(owners)])  13.7 us
    ppermute x3, waiting for transfers between devices, on_device(): upstreams.append(lax.ppermute(grad, 'pipe', [(layer, layer - 1)]))  11.7 us
    pallas_call x4, Pallas kernels, section_step(): pl.pallas_call(kernel, out_shape=out_shape, in_specs=in_specs, out_specs=...  6.61 us
    ppermute x4, starting transfers between devices, on_device(): lax.ppermute(piece, 'dp', [(i, i ^ k) for i in range(owners)])  6.34 us
    pallas_call x1, Pallas kernels, adam_step(): pl.pallas_call(functools.partial(adam_kernel, (owners, parts, blocks[0].s...  5.76 us
    ppermute x4, waiting for transfers between devices, to_peers(): lax.ppermute(value, axis, [(i, (i + k) % size) for i in range(size)])  4.55 us
    ppermute x3, starting transfers between devices, on_device(): blocks.append(lax.ppermute(cut, ('pipe', 'dp'), pairs))  3.89 us
    pallas_call x1, Pallas kernels, stage(): pl.pallas_call(kernel, out_shape=[pltpu.VMEM(shape, arrays[n].dtype) for...  3.87 us
  transfers between devices with their start and end apart: 22, of which 14 were waited for; matrix products, arithmetic and copies ran while one was open for 0% of the time, Pallas kernels for 16%

profile of v2, /device:TPU:0, one launch (start us, length us, event | category | flops | bytes accessed | tf_op | source)
XLA Modules:
  0.0 71.0 jit_solution(16628269060861851418)
XLA Ops:
  0.6 0.5 collective-permute-start
  1.2 3.9 %stage.1 = (bf16[2048,2048]{1,0:T(8,128)(2,1)S(1)}, bf16[128,2048]{1,0:T(8,128)(2,1)S(1)}, bf16[64,2048]{1,0:T(8,128)(2,1)S(1)}, bf16[64,2048]{1,0:T(8,128)(2,1)...) custom-call(bf16[2048,2048]{1,0:T(8,128)(2,1)} %bitcast.15, bf16[128,2048]{1,0:T(8,128)(2,1)} %bitcast.17, ...), custom_call_target="tpu_custom_call" | custom-call | bytes 19922944 | tf_op jit(solution)/shard_map/stage/pallas_call | solution.py:62
  5.0 0.0 collective-permute-done.refs_1_
  5.0 0.0 copy-start
  5.1 4.2 %section_step.4 = (bf16[2048,2048]{1,0:T(8,128)(2,1)S(1)}, f32[64,2048]{1,0:T(8,128)S(1)}, bf16[64,2048]{1,0:T(8,128)(2,1)S(1)}) custom-call(bf16[64,2048]{1,0:T(8,128)(2,1)S(1)} %get-tuple-element.40.refs_0_.refs_1_.refs_4_.refs_6_.refs_7_, bf16[64,2048]{1,0:T(8,128)(2,1)S(1)} %collective-permute-done.refs_1_, ...), custom_call_target="tpu_custom_call" | custom-call | tf_op jit(solution)/shard_map/section_step/pallas_call | solution.py:199
  9.3 0.1 collective-permute-start.1
  9.4 1.5 %collective-permute-done.1.refs_0_ = bf16[64,2048]{1,0:T(8,128)(2,1)S(1)} collective-permute-done((bf16[64,2048]{1,0:T(8,128)(2,1)S(1)}, bf16[64,2048]{1,0:T(8,128)(2,1)S(1)}, u32[]{:S(2)}, u32[]{:S(2)}) %collective-permute-start.1) | collective-permute-done | bytes 262176 | tf_op jit(solution)/shard_map/ppermute | solution.py:453
  10.9 0.0 copy-done
  10.9 0.7 collective-permute-start.2
  11.6 2.7 %collective-permute-start.4 = (bf16[64,2048]{1,0:T(8,128)(2,1)S(1)}, bf16[64,2048]{1,0:T(8,128)(2,1)S(1)}, u32[]{:S(2)}, u32[]{:S(2)}) collective-permute-start(bf16[64,2048]{1,0:T(8,128)(2,1)S(1)} %get-tuple-element.50), channel_id=1, source_target_pairs={{0,2},{2,0},{4,6},{6,4},{1,3},{3,1},{5,7},{7,5},{8,10},{10,8},{12,... | collective-permute-start | bytes 786440 | tf_op jit(solution)/shard_map/ppermute | solution.py:526
  14.3 1.5 %collective-permute-start.5 = (bf16[64,2048]{1,0:T(8,128)(2,1)S(1)}, bf16[64,2048]{1,0:T(8,128)(2,1)S(1)}, u32[]{:S(2)}, u32[]{:S(2)}) collective-permute-start(bf16[64,2048]{1,0:T(8,128)(2,1)S(1)} %get-tuple-element.51), channel_id=1, source_target_pairs={{0,4},{2,6},{4,0},{6,2},{1,5},{3,7},{5,1},{7,3},{8,12},{10,14},{12... | collective-permute-start | bytes 786440 | tf_op jit(solution)/shard_map/ppermute | solution.py:526
  15.9 0.0 collective-permute-done.2.refs_0_.refs_1_
  15.9 0.0 collective-permute-start.3
  15.9 3.5 %stage_in_section.2 = (f32[512,2048]{1,0:T(8,128)S(1)}, f32[512,2048]{1,0:T(8,128)S(1)}) custom-call(f32[512,2048]{1,0:T(8,128)} %bitcast.11, f32[512,2048]{1,0:T(8,128)} %bitcast.13, bf16[64,2048]{1,0:T(8,128)(2,1)S(1)} %get-tuple-element.48.refs_2_.refs_4_), custom_call_target="tpu_custom_call" | custom-call | tf_op jit(solution)/shard_map/stage_in_section/pallas_call | solution.py:89
  19.4 1.8 %collective-permute-done.4.refs_5_.refs_8_.refs_2_ = bf16[64,2048]{1,0:T(8,128)(2,1)S(1)} collective-permute-done((bf16[64,2048]{1,0:T(8,128)(2,1)S(1)}, bf16[64,2048]{1,0:T(8,128)(2,1)S(1)}, u32[]{:S(2)}, u32[]{:S(2)}) %collective-permute-start.4) | collective-permute-done | bytes 262176 | tf_op jit(solution)/shard_map/ppermute | solution.py:526
  21.2 1.5 %collective-permute-done.5.refs_6_.refs_5_ = bf16[64,2048]{1,0:T(8,128)(2,1)S(1)} collective-permute-done((bf16[64,2048]{1,0:T(8,128)(2,1)S(1)}, bf16[64,2048]{1,0:T(8,128)(2,1)S(1)}, u32[]{:S(2)}, u32[]{:S(2)}) %collective-permute-start.5) | collective-permute-done | bytes 262176 | tf_op jit(solution)/shard_map/ppermute | solution.py:526
  22.6 0.0 collective-permute-done.3.refs_1_
  22.6 0.0 collective-permute-start.6
  22.6 1.5 %collective-permute-done.6.refs_0_ = bf16[64,2048]{1,0:T(8,128)(2,1)S(1)} collective-permute-done((bf16[64,2048]{1,0:T(8,128)(2,1)S(1)}, bf16[64,2048]{1,0:T(8,128)(2,1)S(1)}, u32[]{:S(2)}, u32[]{:S(2)}) %collective-permute-start.6) | collective-permute-done | bytes 262176 | tf_op jit(solution)/shard_map/ppermute | solution.py:453
  24.2 0.1 norm_step.5
  24.2 0.7 collective-permute-start.7
  24.9 0.4 collective-permute-start.9
  25.3 1.7 %collective-permute-start.10 = (bf16[128,2048]{1,0:T(8,128)(2,1)S(1)}, bf16[128,2048]{1,0:T(8,128)(2,1)S(1)}, u32[]{:S(2)}, u32[]{:S(2)}) collective-permute-start(bf16[128,2048]{1,0:T(8,128)(2,1)S(1)} %get-tuple-element.58), channel_id=1, source_target_pairs={{0,4},{2,6},{4,0},{6,2},{1,5},{3,7},{5,1},{7,3},{8,12},{10,14},{12... | collective-permute-start | bytes 1572872 | tf_op jit(solution)/shard_map/ppermute | solution.py:526
  27.0 0.0 collective-permute-done.7.refs_0_.refs_1_.refs_2_
  27.0 0.0 collective-permute-start.8
  27.0 1.5 %collective-permute-done.8.refs_1_ = bf16[64,2048]{1,0:T(8,128)(2,1)S(1)} collective-permute-done((bf16[64,2048]{1,0:T(8,128)(2,1)S(1)}, bf16[64,2048]{1,0:T(8,128)(2,1)S(1)}, u32[]{:S(2)}, u32[]{:S(2)}) %collective-permute-start.8) | collective-permute-done | bytes 262176 | tf_op jit(solution)/shard_map/ppermute | solution.py:447
  28.6 10.4 %collective-permute-done.9.refs_5_.refs_3_.refs_7_ = bf16[128,2048]{1,0:T(8,128)(2,1)S(1)} collective-permute-done((bf16[128,2048]{1,0:T(8,128)(2,1)S(1)}, bf16[128,2048]{1,0:T(8,128)(2,1)S(1)}, u32[]{:S(2)}, u32[]{:S(2)}) %collective-permute-start.9) | collective-permute-done | bytes 524320 | tf_op jit(solution)/shard_map/ppermute | solution.py:526
  39.0 0.1 collective-permute-done.10.refs_6_.refs_4_
  39.0 0.0 collective-permute-start.11
  39.0 1.5 %collective-permute-done.11.refs_0_ = bf16[64,2048]{1,0:T(8,128)(2,1)S(1)} collective-permute-done((bf16[64,2048]{1,0:T(8,128)(2,1)S(1)}, bf16[64,2048]{1,0:T(8,128)(2,1)S(1)}, u32[]{:S(2)}, u32[]{:S(2)}) %collective-permute-start.11) | collective-permute-done | bytes 262176 | tf_op jit(solution)/shard_map/ppermute | solution.py:453
  40.6 1.3 %collective-permute-start.12 = (bf16[64,2048]{1,0:T(8,128)(2,1)S(1)}, bf16[64,2048]{1,0:T(8,128)(2,1)S(1)}, u32[]{:S(2)}, u32[]{:S(2)}) collective-permute-start(bf16[64,2048]{1,0:T(8,128)(2,1)S(1)} %get-tuple-element.61.refs_4_.refs_6_), channel_id=1, source_target_pairs={{8,0},{9,1},{10,2},{11,3},{12,4},{13,5},{14,6},{15,7}} | collective-permute-start | bytes 786440 | tf_op jit(solution)/shard_map/ppermute | solution.py:515
  41.9 11.7 %collective-permute-done.12.source.refs_0_.refs_1_.refs_3_ = bf16[64,2048]{1,0:T(8,128)(2,1)S(1)} collective-permute-done((bf16[64,2048]{1,0:T(8,128)(2,1)S(1)}, bf16[64,2048]{1,0:T(8,128)(2,1)S(1)}, u32[]{:S(2)}, u32[]{:S(2)}) %collective-permute-start.12) | collective-permute-done | bytes 262176 | tf_op jit(solution)/shard_map/ppermute | solution.py:515
  53.6 0.1 collective-permute-start.13
  53.7 0.5 collective-permute-start.14
  54.2 0.1 collective-permute-start.15
  54.3 0.4 collective-permute-start.16
  54.7 0.0 collective-permute-start.18
  54.7 0.2 collective-permute-done.13.refs_1_
  54.9 0.0 collective-permute-start.19
  54.9 0.2 collective-permute-done.14.refs_2_
  55.1 3.9 %collective-permute-start.20 = (bf16[64,512]{1,0:T(8,128)(2,1)S(1)}, bf16[64,512]{1,0:T(8,128)(2,1)S(1)}, u32[]{:S(2)}, u32[]{:S(2)}) collective-permute-start(bf16[64,512]{1,0:T(8,128)(2,1)S(1)} %get-tuple-element.72), channel_id=1, source_target_pairs={{0,30},{2,28},{4,26},{6,24},{8,6},{10,4},{12,2},{14,0},{16,14},{18... | collective-permute-start | bytes 196616 | tf_op jit(solution)/shard_map/ppermute | solution.py:523
  59.0 0.2 stack.1.refs_8_.refs_2_
  59.2 0.1 stage_in_section.3
  59.3 0.0 collective-permute-done.15.refs_3_
  59.3 0.0 collective-permute-done.16.refs_4_
  59.3 2.4 %section_step.7 = (f32[64,2048]{1,0:T(8,128)S(1)}, bf16[64,2048]{1,0:T(8,128)(2,1)S(1)}) custom-call(bf16[64,2048]{1,0:T(8,128)(2,1)S(1)} %collective-permute-done.12.source.refs_0_.refs_1_.refs_3_, bf16[64,512]{1,0:T(8,128)(2,1)S(1)} %collective-permute-done.13.refs_1_, bf16[64,512]{1,0:T(8,128)(2,1)S(1)} %collective-permute-done.14.refs_2_, ...), custom_call_target="tpu_custom_call" | custom-call | tf_op jit(solution)/shard_map/section_step/pallas_call | solution.py:199
  61.7 0.1 collective-permute-start.17
  61.8 0.0 collective-permute-done.18.refs_4_
  61.8 1.0 %collective-permute-done.19.refs_5_ = bf16[64,512]{1,0:T(8,128)(2,1)S(1)} collective-permute-done((bf16[64,512]{1,0:T(8,128)(2,1)S(1)}, bf16[64,512]{1,0:T(8,128)(2,1)S(1)}, u32[]{:S(2)}, u32[]{:S(2)}) %collective-permute-start.19) | collective-permute-done | bytes 65568 | tf_op jit(solution)/shard_map/ppermute | solution.py:523
  62.8 0.7 collective-permute-done.20.refs_6_
  63.5 0.1 collective-permute-start.21
  63.6 0.0 collective-permute-done.17.refs_0_
  63.6 1.0 %norm_step.7 = bf16[64,2048]{1,0:T(8,128)(2,1)} custom-call(f32[64,2048]{1,0:T(8,128)S(1)} %get-tuple-element.68.kept_ref.refs_7_, bf16[64,2048]{1,0:T(8,128)(2,1)S(1)} %collective-permute-done.17.refs_0_, bf16[64,2048]{1,0:T(8,128)(2,1)S(1)} %collective-permute-done.12.source.refs_0_.refs_1_.refs_3_, bf16[64,2048]{1,0:T(8,128)(2,1)S(1)} %get-tuple-element.45.refs_2_, ...), custom_call_target="tpu_custom_call" | custom-call | tf_op jit(solution)/shard_map/norm_step/pallas_call | solution.py:274
  64.6 0.5 collective-permute-done.21.refs_1_
  65.1 5.8 %adam_step.1 = (f32[512,2048]{1,0:T(8,128)}, f32[512,2048]{1,0:T(8,128)}, f32[512,2048]{1,0:T(8,128)}) custom-call(bf16[256,512]{1,0:T(8,128)(2,1)S(1)} %collect.1.refs_0_, bf16[256,512]{1,0:T(8,128)(2,1)S(1)} %collective-permute-done.21.refs_1_, bf16[512,2048]{1,0:T(8,128)(2,1)S(1)} %stack.1.refs_8_.refs_2_, ...), custom_call_target="tpu_custom_call" | custom-call | tf_op jit(solution)/shard_map/adam_step/pallas_call | solution.py:365
  (6 shorter events, 0.1 us)
Async XLA Ops:
  0.6 4.4 %collective-permute-start = (bf16[64,2048]{1,0:T(8,128)(2,1)}, bf16[64,2048]{1,0:T(8,128)(2,1)S(1)}, u32[]{:S(2)}, u32[]{:S(2)}) collective-permute-start(bf16[64,2048]{1,0:T(8,128)(2,1)} %refs_3_.5), channel_id=1, source_target_pairs={{1,0},{0,1},{3,2},{2,3},{5,4},{4,5},{7,6},{6,7},{9,8},{8,9},{11,10... | collective-permute-start | bytes 786440 | tf_op jit(solution)/shard_map/ppermute | solution.py:447
  5.0 5.9 %copy-start = (f32[1,2048]{1,0:T(1,128)S(1)}, f32[1,2048]{1,0:T(1,128)}, u32[]{:S(2)}) copy-start(f32[1,2048]{1,0:T(1,128)} %refs_3_.9) | copy-start | bytes 24580
  9.3 1.6 %collective-permute-start.1 = (bf16[64,2048]{1,0:T(8,128)(2,1)S(1)}, bf16[64,2048]{1,0:T(8,128)(2,1)S(1)}, u32[]{:S(2)}, u32[]{:S(2)}) collective-permute-start(bf16[64,2048]{1,0:T(8,128)(2,1)S(1)} %get-tuple-element.44), channel_id=1, source_target_pairs={{0,1},{1,0},{2,3},{3,2},{4,5},{5,4},{6,7},{7,6},{8,9},{9,8},{10,11... | collective-permute-start | bytes 786440 | tf_op jit(solution)/shard_map/ppermute | solution.py:453
  10.9 4.9 %collective-permute-start.2 = (bf16[64,2048]{1,0:T(8,128)(2,1)S(1)}, bf16[64,2048]{1,0:T(8,128)(2,1)S(1)}, u32[]{:S(2)}, u32[]{:S(2)}) collective-permute-start(bf16[64,2048]{1,0:T(8,128)(2,1)S(1)} %get-tuple-element.48.refs_2_.refs_4_), channel_id=1, source_target_pairs={{24,16},{25,17},{26,18},{27,19},{28,20},{29,21},{30,22},{31,23}} | collective-permute-start | bytes 786440 | tf_op jit(solution)/shard_map/ppermute | solution.py:515
  11.6 9.5 %collective-permute-start.4 = (bf16[64,2048]{1,0:T(8,128)(2,1)S(1)}, bf16[64,2048]{1,0:T(8,128)(2,1)S(1)}, u32[]{:S(2)}, u32[]{:S(2)}) collective-permute-start(bf16[64,2048]{1,0:T(8,128)(2,1)S(1)} %get-tuple-element.50), channel_id=1, source_target_pairs={{0,2},{2,0},{4,6},{6,4},{1,3},{3,1},{5,7},{7,5},{8,10},{10,8},{12,... | collective-permute-start | bytes 786440 | tf_op jit(solution)/shard_map/ppermute | solution.py:526
  14.3 8.3 %collective-permute-start.5 = (bf16[64,2048]{1,0:T(8,128)(2,1)S(1)}, bf16[64,2048]{1,0:T(8,128)(2,1)S(1)}, u32[]{:S(2)}, u32[]{:S(2)}) collective-permute-start(bf16[64,2048]{1,0:T(8,128)(2,1)S(1)} %get-tuple-element.51), channel_id=1, source_target_pairs={{0,4},{2,6},{4,0},{6,2},{1,5},{3,7},{5,1},{7,3},{8,12},{10,14},{12... | collective-permute-start | bytes 786440 | tf_op jit(solution)/shard_map/ppermute | solution.py:526
  15.9 6.8 %collective-permute-start.3 = (bf16[64,2048]{1,0:T(8,128)(2,1)S(1)}, bf16[64,2048]{1,0:T(8,128)(2,1)S(1)}, u32[]{:S(2)}, u32[]{:S(2)}) collective-permute-start(bf16[64,2048]{1,0:T(8,128)(2,1)S(1)} %collective-permute-done.2.refs_0_.refs_1_), channel_id=1, source_target_pairs={{1,0},{0,1},{3,2},{2,3},{5,4},{4,5},{7,6},{6,7},{9,8},{8,9},{11,10... | collective-permute-start | bytes 786440 | tf_op jit(solution)/shard_map/ppermute | solution.py:447
  22.6 1.5 %collective-permute-start.6 = (bf16[64,2048]{1,0:T(8,128)(2,1)S(1)}, bf16[64,2048]{1,0:T(8,128)(2,1)S(1)}, u32[]{:S(2)}, u32[]{:S(2)}) collective-permute-start(bf16[64,2048]{1,0:T(8,128)(2,1)S(1)} %get-tuple-element.55), channel_id=1, source_target_pairs={{0,1},{1,0},{2,3},{3,2},{4,5},{5,4},{6,7},{7,6},{8,9},{9,8},{10,11... | collective-permute-start | bytes 786440 | tf_op jit(solution)/shard_map/ppermute | solution.py:453
  24.2 2.8 %collective-permute-start.7 = (bf16[64,2048]{1,0:T(8,128)(2,1)S(1)}, bf16[64,2048]{1,0:T(8,128)(2,1)S(1)}, u32[]{:S(2)}, u32[]{:S(2)}) collective-permute-start(bf16[64,2048]{1,0:T(8,128)(2,1)S(1)} %get-tuple-element.56.refs_5_), channel_id=1, source_target_pairs={{16,8},{17,9},{18,10},{19,11},{20,12},{21,13},{22,14},{23,15}} | collective-permute-start | bytes 786440 | tf_op jit(solution)/shard_map/ppermute | solution.py:515
  24.9 14.0 %collective-permute-start.9 = (bf16[128,2048]{1,0:T(8,128)(2,1)S(1)}, bf16[128,2048]{1,0:T(8,128)(2,1)S(1)}, u32[]{:S(2)}, u32[]{:S(2)}) collective-permute-start(bf16[128,2048]{1,0:T(8,128)(2,1)S(1)} %get-tuple-element.57), channel_id=1, source_target_pairs={{0,2},{2,0},{4,6},{6,4},{1,3},{3,1},{5,7},{7,5},{8,10},{10,8},{12,... | collective-permute-start | bytes 1572872 | tf_op jit(solution)/shard_map/ppermute | solution.py:526
  25.3 13.7 %collective-permute-start.10 = (bf16[128,2048]{1,0:T(8,128)(2,1)S(1)}, bf16[128,2048]{1,0:T(8,128)(2,1)S(1)}, u32[]{:S(2)}, u32[]{:S(2)}) collective-permute-start(bf16[128,2048]{1,0:T(8,128)(2,1)S(1)} %get-tuple-element.58), channel_id=1, source_target_pairs={{0,4},{2,6},{4,0},{6,2},{1,5},{3,7},{5,1},{7,3},{8,12},{10,14},{12... | collective-permute-start | bytes 1572872 | tf_op jit(solution)/shard_map/ppermute | solution.py:526
  27.0 1.5 %collective-permute-start.8 = (bf16[64,2048]{1,0:T(8,128)(2,1)S(1)}, bf16[64,2048]{1,0:T(8,128)(2,1)S(1)}, u32[]{:S(2)}, u32[]{:S(2)}) collective-permute-start(bf16[64,2048]{1,0:T(8,128)(2,1)S(1)} %collective-permute-done.7.refs_0_.refs_1_.refs_2_), channel_id=1, source_target_pairs={{1,0},{0,1},{3,2},{2,3},{5,4},{4,5},{7,6},{6,7},{9,8},{8,9},{11,10... | collective-permute-start | bytes 786440 | tf_op jit(solution)/shard_map/ppermute | solution.py:447
  39.0 1.5 %collective-permute-start.11 = (bf16[64,2048]{1,0:T(8,128)(2,1)S(1)}, bf16[64,2048]{1,0:T(8,128)(2,1)S(1)}, u32[]{:S(2)}, u32[]{:S(2)}) collective-permute-start(bf16[64,2048]{1,0:T(8,128)(2,1)S(1)} %get-tuple-element.60), channel_id=1, source_target_pairs={{0,1},{1,0},{2,3},{3,2},{4,5},{5,4},{6,7},{7,6},{8,9},{9,8},{10,11... | collective-permute-start | bytes 786440 | tf_op jit(solution)/shard_map/ppermute | solution.py:453
  40.6 13.0 %collective-permute-start.12 = (bf16[64,2048]{1,0:T(8,128)(2,1)S(1)}, bf16[64,2048]{1,0:T(8,128)(2,1)S(1)}, u32[]{:S(2)}, u32[]{:S(2)}) collective-permute-start(bf16[64,2048]{1,0:T(8,128)(2,1)S(1)} %get-tuple-element.61.refs_4_.refs_6_), channel_id=1, source_target_pairs={{8,0},{9,1},{10,2},{11,3},{12,4},{13,5},{14,6},{15,7}} | collective-permute-start | bytes 786440 | tf_op jit(solution)/shard_map/ppermute | solution.py:515
  53.6 1.3 %collective-permute-start.13 = (bf16[64,512]{1,0:T(8,128)(2,1)S(1)}, bf16[64,512]{1,0:T(8,128)(2,1)S(1)}, u32[]{:S(2)}, u32[]{:S(2)}) collective-permute-start(bf16[64,512]{1,0:T(8,128)(2,1)S(1)} %get-tuple-element.62), channel_id=1, source_target_pairs={{1,0},{0,1},{3,2},{2,3},{5,4},{4,5},{7,6},{6,7},{9,8},{8,9},{11,10... | collective-permute-start | bytes 196616 | tf_op jit(solution)/shard_map/ppermute | solution.py:447
  53.7 1.4 %collective-permute-start.14 = (bf16[64,512]{1,0:T(8,128)(2,1)S(1)}, bf16[64,512]{1,0:T(8,128)(2,1)S(1)}, u32[]{:S(2)}, u32[]{:S(2)}) collective-permute-start(bf16[64,512]{1,0:T(8,128)(2,1)S(1)} %get-tuple-element.63), channel_id=1, source_target_pairs={{1,0},{0,1},{3,2},{2,3},{5,4},{4,5},{7,6},{6,7},{9,8},{8,9},{11,10... | collective-permute-start | bytes 196616 | tf_op jit(solution)/shard_map/ppermute | solution.py:447
  54.2 5.1 %collective-permute-start.15 = (bf16[64,512]{1,0:T(8,128)(2,1)S(1)}, bf16[64,512]{1,0:T(8,128)(2,1)S(1)}, u32[]{:S(2)}, u32[]{:S(2)}) collective-permute-start(bf16[64,512]{1,0:T(8,128)(2,1)S(1)} %get-tuple-element.64), channel_id=1, source_target_pairs={{1,0},{0,1},{3,2},{2,3},{5,4},{4,5},{7,6},{6,7},{9,8},{8,9},{11,10... | collective-permute-start | bytes 196616 | tf_op jit(solution)/shard_map/ppermute | solution.py:447
  54.3 5.0 %collective-permute-start.16 = (bf16[64,512]{1,0:T(8,128)(2,1)S(1)}, bf16[64,512]{1,0:T(8,128)(2,1)S(1)}, u32[]{:S(2)}, u32[]{:S(2)}) collective-permute-start(bf16[64,512]{1,0:T(8,128)(2,1)S(1)} %get-tuple-element.65), channel_id=1, source_target_pairs={{1,0},{0,1},{3,2},{2,3},{5,4},{4,5},{7,6},{6,7},{9,8},{8,9},{11,10... | collective-permute-start | bytes 196616 | tf_op jit(solution)/shard_map/ppermute | solution.py:447
  54.7 7.1 %collective-permute-start.18 = (bf16[64,512]{1,0:T(8,128)(2,1)S(1)}, bf16[64,512]{1,0:T(8,128)(2,1)S(1)}, u32[]{:S(2)}, u32[]{:S(2)}) collective-permute-start(bf16[64,512]{1,0:T(8,128)(2,1)S(1)} %get-tuple-element.70), channel_id=1, source_target_pairs={{0,26},{2,24},{4,30},{6,28},{8,2},{10,0},{12,6},{14,4},{16,10},{18... | collective-permute-start | bytes 196616 | tf_op jit(solution)/shard_map/ppermute | solution.py:523
  54.9 7.9 %collective-permute-start.19 = (bf16[64,512]{1,0:T(8,128)(2,1)S(1)}, bf16[64,512]{1,0:T(8,128)(2,1)S(1)}, u32[]{:S(2)}, u32[]{:S(2)}) collective-permute-start(bf16[64,512]{1,0:T(8,128)(2,1)S(1)} %get-tuple-element.71), channel_id=1, source_target_pairs={{0,28},{2,30},{4,24},{6,26},{8,4},{10,6},{12,0},{14,2},{16,12},{18... | collective-permute-start | bytes 196616 | tf_op jit(solution)/shard_map/ppermute | solution.py:523
  55.1 8.4 %collective-permute-start.20 = (bf16[64,512]{1,0:T(8,128)(2,1)S(1)}, bf16[64,512]{1,0:T(8,128)(2,1)S(1)}, u32[]{:S(2)}, u32[]{:S(2)}) collective-permute-start(bf16[64,512]{1,0:T(8,128)(2,1)S(1)} %get-tuple-element.72), channel_id=1, source_target_pairs={{0,30},{2,28},{4,26},{6,24},{8,6},{10,4},{12,2},{14,0},{16,14},{18... | collective-permute-start | bytes 196616 | tf_op jit(solution)/shard_map/ppermute | solution.py:523
  61.7 1.9 %collective-permute-start.17 = (bf16[64,2048]{1,0:T(8,128)(2,1)S(1)}, bf16[64,2048]{1,0:T(8,128)(2,1)S(1)}, u32[]{:S(2)}, u32[]{:S(2)}) collective-permute-start(bf16[64,2048]{1,0:T(8,128)(2,1)S(1)} %get-tuple-element.69), channel_id=1, source_target_pairs={{0,1},{1,0},{2,3},{3,2},{4,5},{5,4},{6,7},{7,6},{8,9},{9,8},{10,11... | collective-permute-start | bytes 786440 | tf_op jit(solution)/shard_map/ppermute | solution.py:453
  63.5 1.6 %collective-permute-start.21 = (bf16[256,512]{1,0:T(8,128)(2,1)S(1)}, bf16[256,512]{1,0:T(8,128)(2,1)S(1)}, u32[]{:S(2)}, u32[]{:S(2)}) collective-permute-start(bf16[256,512]{1,0:T(8,128)(2,1)S(1)} %collect.1.refs_0_), channel_id=1, source_target_pairs={{1,0},{0,1},{3,2},{2,3},{5,4},{4,5},{7,6},{6,7},{9,8},{8,9},{11,10... | collective-permute-start | bytes 786440 | tf_op jit(solution)/shard_map/ppermute | solution.py:447

commit v3 on v2

--- a/solution.py
+++ b/solution.py
@@ -1,4 +1,5 @@
 import functools
+import math
 import jax
 import jax.numpy as jnp
 from jax import lax
@@ -118,12 +119,14 @@
 
 def fill_rows(share, rows_ref, own_ref, peer_refs):
     rows_ref[0:share, :] = own_ref[...]
-    at, row = 0, share
-    for ref in peer_refs:
-        rows_ref[row : row + share, at : at + ref.shape[1]] = ref[...]
-        at += ref.shape[1]
-        if at == rows_ref.shape[1]:
-            at, row = 0, row + share
+    parts = rows_ref.shape[0] // share
+    me = lax.axis_index("tensor")
+    for k in range(1, parts):
+        if peer_refs[0].shape[0] > share:
+            at = pl.multiple_of(lax.rem(me + k, parts) * share, share)
+            rows_ref[k * share : (k + 1) * share, :] = peer_refs[0][pl.ds(at, share), :]
+        else:
+            rows_ref[k * share : (k + 1) * share, :] = peer_refs[k - 1][...]
 
 
 def step_kernel(layer, parts, pieces, own_ref, *refs):
@@ -139,6 +142,56 @@
         unit_grads(parts, share, rows_ref, down_ref, gate_ref, unit_ref)
         term = jnp.dot(unit_ref[...], turned_ref[...], preferred_element_type=F32)
         hand_out(share, term, slice(None), kept_ref, sent_refs)
+
+
+def unit_kernel(layer, parts, own_ref, *refs):
+    peer_refs = refs[: parts - 1]
+    down_ref, gate_ref, unit_ref, rows_ref = refs[parts - 1 :]
+    share = own_ref.shape[0]
+
+    @pl.when(lax.axis_index("pipe") == layer)
+    def _():
+        fill_rows(share, rows_ref, own_ref, peer_refs)
+        unit_grads(parts, share, rows_ref, down_ref, gate_ref, unit_ref)
+
+
+def unit_step(layer, own, peers, w_down, gates):
+    parts = len(peers) + 1
+    rows = own.shape[0] * parts
+    return pl.pallas_call(
+        functools.partial(unit_kernel, layer, parts),
+        out_shape=jax.ShapeDtypeStruct((rows, w_down.shape[1]), BF16),
+        in_specs=[VMEM] * (parts + 2),
+        out_specs=VMEM,
+        scratch_shapes=[pltpu.VMEM((rows, own.shape[1]), BF16)],
+        compiler_params=pltpu.CompilerParams(vmem_limit_bytes=12 * MIB),
+        cost_estimate=CHEAP,
+        name="unit_step",
+    )(own, *peers, w_down, gates)
+
+
+def width_step(layer, unit_grad, turned, share, after):
+    width = turned.shape[1]
+    parts = unit_grad.shape[0] // share
+
+    def kernel(unit_ref, turned_ref, *refs):
+        kept_ref, *sent_refs = refs[len(after) :]
+
+        @pl.when(lax.axis_index("pipe") == layer)
+        def _():
+            term = jnp.dot(unit_ref[...], turned_ref[...], preferred_element_type=F32)
+            hand_out(share, term, slice(None), kept_ref, sent_refs)
+
+    return pl.pallas_call(
+        kernel,
+        out_shape=[jax.ShapeDtypeStruct((share, width), F32)]
+        + [jax.ShapeDtypeStruct((share, width), BF16)] * (parts - 1),
+        in_specs=[VMEM, VMEM] + [pl.BlockSpec(memory_space=pl.ANY)] * len(after),
+        out_specs=[VMEM] * parts,
+        compiler_params=pltpu.CompilerParams(vmem_limit_bytes=12 * MIB),
+        cost_estimate=CHEAP,
+        name="width_step",
+    )(unit_grad, turned, *after)
 
 
 def first_kernel(layer, parts, pieces, own_ref, *refs):
@@ -177,7 +230,7 @@
     share, width = own.shape
     units = w_down.shape[1]
     pieces = len(peers)
-    parts = sum(p.size for p in peers) // own.size + 1
+    parts = lax.axis_size("tensor")
     rows = share * parts
     first = w_up is not None
     out_shape = [jax.ShapeDtypeStruct((share, width), F32)]
@@ -209,13 +262,26 @@
     return outs
 
 
+def pack_block(source, k, target, at):
+    owners = lax.axis_size("dp")
+    tokens, width = source.shape
+    size = width // owners
+    rows = tokens * size // target.shape[1]
+    column = pl.multiple_of((lax.axis_index("dp") ^ k) * size, size)
+    for q in range(tokens // rows):
+        target[at : at + rows, q * size : (q + 1) * size] = source[
+            q * rows : (q + 1) * rows, pl.ds(column, size)
+        ]
+    return rows
+
+
 def norm_kernel(layer, parts, earlier, owners, passed, handed, kept_ref, *refs):
     arrived = refs[: parts - 1]
     up_ref, in_ref, gain_ref = refs[parts - 1 : parts + 2]
     refs = refs[parts + 2 :]
     earlier_refs, refs = refs[:earlier], refs[earlier:]
     first_ref, pass_refs, refs = refs[0], refs[1 : 1 + passed], refs[1 + passed :]
-    out_ref, block_refs, handed_refs = refs[0], refs[1 : len(refs) - handed], refs[len(refs) - handed :]
+    out_ref, block_refs, handed_refs = refs[0], refs[1 : len(refs) - len(handed)], refs[len(refs) - len(handed) :]
     segment = lax.axis_index("pipe")
 
     def cut(source):
@@ -248,31 +314,32 @@
             if layer == 0:
                 out_ref[...] = ref[...]
 
-    if block_refs:
-
-        @pl.when(segment == 0)
-        def _():
-            cut(first_ref)
-
-    sources = list(pass_refs)
-    for target in handed_refs:
+    sources = iter(pass_refs)
+    for recipe, target in zip(handed, handed_refs):
         at = 0
-        while at < target.shape[0]:
-            source = sources.pop(0)
-            target[at : at + source.shape[0], :] = source[...]
-            at += source.shape[0]
+        for piece in recipe:
+            if isinstance(piece, int):
+                at += pack_block(first_ref, piece, target, at)
+            else:
+                start, rows = piece
+                target[at : at + rows, :] = next(sources)[start : start + rows, :]
+                at += rows
 
 
 def norm_step(layer, kept, arrived, upstream, rows_in, gain, first, earlier=(), owners=1, passed=()):
     parts = len(arrived) + 1
     share, width = upstream.shape
     block = jax.ShapeDtypeStruct((share, width // owners), BF16)
-    handed = [
-        jax.ShapeDtypeStruct((sum(p.shape[0] for p in group), group[0].shape[1]), BF16) for group in passed
-    ]
-    passed = [p for group in passed for p in group]
+    recipes = [[p if isinstance(p, int) else p[1:] for p in group] for group in passed]
+    handed = []
+    for group in passed:
+        units = passed[0][0][0].shape[1]
+        block_rows = share * (width // lax.axis_size("dp")) // units
+        rows = sum(block_rows if isinstance(p, int) else p[2] for p in group)
+        handed.append(jax.ShapeDtypeStruct((rows, units), BF16))
+    passed = [p[0] for group in passed for p in group if not isinstance(p, int)]
     outs = pl.pallas_call(
-        functools.partial(norm_kernel, layer, parts, len(earlier), owners, len(passed), len(handed)),
+        functools.partial(norm_kernel, layer, parts, len(earlier), owners, len(passed), recipes),
         out_shape=[jax.ShapeDtypeStruct(upstream.shape, BF16)]
         + [block] * (owners - 1)
         + handed,
@@ -285,28 +352,37 @@
     return outs[0], outs[1:owners], outs[owners:]
 
 
-def collect_kernel(sections, *refs):
-    upstream_refs, block_refs, out_ref = refs[:sections], refs[sections:-1], refs[-1]
-    share, size = block_refs[0].shape
-    at = pl.multiple_of(lax.axis_index("dp") * size, size)
-    for s, ref in enumerate(upstream_refs):
-
-        @pl.when(lax.axis_index("pipe") == sections - 1 - s)
-        def _(ref=ref):
-            out_ref[0:share, :] = ref[:, pl.ds(at, size)]
-
-    for k, ref in enumerate(block_refs, 1):
-        out_ref[k * share : (k + 1) * share, :] = ref[...]
-
-
-def collect(upstreams, blocks, after):
+def collect(upstreams, blocks, packed, after):
     sections = len(upstreams)
     owners = len(blocks) + 1
     share, size = blocks[0].shape
-    count = sections + len(blocks)
+    count = sections + 2 * len(blocks)
 
     def kernel(*refs):
-        collect_kernel(sections, *refs[:count], refs[-1])
+        out_ref = refs[-1]
+        segment = lax.axis_index("pipe")
+        at = pl.multiple_of(lax.axis_index("dp") * size, size)
+        for s in range(sections):
+
+            @pl.when(segment == sections - 1 - s)
+            def _(s=s):
+                out_ref[0:share, :] = refs[s][:, pl.ds(at, size)]
+
+        @pl.when(segment < sections - 1)
+        def _():
+            for k in range(1, owners):
+                out_ref[k * share : (k + 1) * share, :] = refs[sections + k - 1][...]
+
+        @pl.when(segment == sections - 1)
+        def _():
+            for k in range(1, owners):
+                source, start = refs[sections + owners + k - 2], packed[k - 1][1]
+                pieces = source.shape[1] // size
+                rows = share // pieces
+                for q in range(pieces):
+                    out_ref[k * share + q * rows : k * share + (q + 1) * rows, :] = source[
+                        start : start + rows, q * size : (q + 1) * size
+                    ]
 
     return pl.pallas_call(
         kernel,
@@ -316,25 +392,25 @@
         compiler_params=pltpu.CompilerParams(vmem_limit_bytes=4 * MIB),
         cost_estimate=CHEAP,
         name="collect",
-    )(*upstreams, *blocks, *after)
+    )(*upstreams, *blocks, *[array for array, _ in packed], *after)
 
 
 def adam_update(gradient, current, moment_one, moment_two):
     first = BETA_ONE * moment_one + (1.0 - BETA_ONE) * gradient
     second = BETA_TWO * moment_two + (1.0 - BETA_TWO) * gradient * gradient
-    scaled = second * (1.0 / CORRECT_TWO)
-    root = scaled * lax.rsqrt(scaled)
-    step = (first * (RATE / CORRECT_ONE)) / (root + EPS_ADAM)
+    root = second * lax.rsqrt(second)
+    scale = math.sqrt(CORRECT_TWO)
+    step = (first * (RATE * scale / CORRECT_ONE)) / (root + EPS_ADAM * scale)
     return first, second, (1.0 - RATE * DECAY) * current - step
 
 
 def adam_kernel(sizes, *refs):
-    owners, parts, share, tile = sizes
+    owners, parts, share, tile, part_rows = sizes
     up_refs = refs[:parts]
     hidden_ref, down_ref, one_ref, two_ref = refs[parts : parts + 4]
     outs = refs[parts + 4 : parts + 7]
-    rows_ref, turned_ref, *results, sem = refs[parts + 7 :]
-    rows = turned_ref.shape[0]
+    rows_ref, *results, sem = refs[parts + 7 :]
+    rows = rows_ref.shape[1]
     me = lax.axis_index("dp")
     part = lax.axis_index("tensor")
     for p in range(parts):
@@ -343,17 +419,23 @@
             rows_ref[pl.ds(pl.multiple_of(at * share, share), share), :] = up_refs[p][
                 k * share : (k + 1) * share, :
             ]
-    turned_ref[...] = rows_ref[...].T
     writes = []
     for i in range(rows // tile):
-        cut = slice(i * tile, (i + 1) * tile)
-        gradient = jnp.dot(turned_ref[cut, :], hidden_ref[...], preferred_element_type=F32)
-        current = down_ref[pl.ds(pl.multiple_of(me * rows + i * tile, tile), tile), :].astype(F32)
-        updates = adam_update(gradient, current, one_ref[cut, :], two_ref[cut, :])
-        for q, update in enumerate(updates):
-            results[q][cut, :] = update
-            writes.append(pltpu.make_async_copy(results[q].at[cut], outs[q].at[cut], sem.at[i, q]))
-            writes[-1].start()
+        turned = rows_ref[:, i * tile : (i + 1) * tile].T
+        gradient = jnp.dot(turned, hidden_ref[...], preferred_element_type=F32)
+        for j in range(tile // part_rows):
+            at = i * tile + j * part_rows
+            cut = slice(at, at + part_rows)
+            current = down_ref[pl.ds(pl.multiple_of(me * rows + at, part_rows), part_rows), :].astype(F32)
+            updates = adam_update(
+                gradient[j * part_rows : (j + 1) * part_rows], current, one_ref[cut, :], two_ref[cut, :]
+            )
+            for q, update in enumerate(updates):
+                results[q][cut, :] = update
+                writes.append(
+                    pltpu.make_async_copy(results[q].at[cut], outs[q].at[cut], sem.at[at // part_rows, q])
+                )
+                writes[-1].start()
     for write in writes:
         write.wait()
 
@@ -362,51 +444,36 @@
     rows, units = moment_one.shape
     tokens = hidden_all.shape[0]
     tile = tile_of(rows, 128)
+    part_rows = tile_of(tile, 32)
     return pl.pallas_call(
-        functools.partial(adam_kernel, (owners, parts, blocks[0].shape[0] // owners, tile)),
+        functools.partial(adam_kernel, (owners, parts, blocks[0].shape[0] // owners, tile, part_rows)),
         out_shape=[jax.ShapeDtypeStruct((rows, units), F32)] * 3,
         in_specs=[VMEM] * (len(blocks) + 4),
         out_specs=[pl.BlockSpec(memory_space=pl.ANY)] * 3,
-        scratch_shapes=[pltpu.VMEM((tokens, rows), BF16), pltpu.VMEM((rows, tokens), BF16)]
+        scratch_shapes=[pltpu.VMEM((tokens, rows), BF16)]
         + [pltpu.VMEM((rows, units), F32)] * 3
-        + [pltpu.SemaphoreType.DMA((rows // tile, 3))],
+        + [pltpu.SemaphoreType.DMA((rows // part_rows, 3))],
         compiler_params=pltpu.CompilerParams(vmem_limit_bytes=18 * MIB),
         cost_estimate=CHEAP,
         name="adam_step",
     )(*blocks, hidden_all, w_down, moment_one, moment_two)
 
 
-def columns(array, count):
-    rows, cols = array.shape
-    size = cols // count
-
-    def kernel(source, *targets):
-        for n, target in enumerate(targets):
-            target[...] = source[:, n * size : (n + 1) * size]
-
-    return pl.pallas_call(
-        kernel,
-        out_shape=[jax.ShapeDtypeStruct((rows, size), array.dtype)] * count,
-        in_specs=[VMEM],
-        out_specs=[VMEM] * count,
-        compiler_params=pltpu.CompilerParams(vmem_limit_bytes=4 * MIB),
-        cost_estimate=CHEAP,
-        name="columns",
-    )(array)
-
-
-def stack(order, size):
+def stack(order):
     count = len(order)
-    cols = order[0][0].shape[1]
+    total = sum(rows for _, _, rows in order)
 
     def kernel(*refs):
         out, sem = refs[-2:]
-        started = [
-            pltpu.make_async_copy(
-                refs[n].at[at : at + size], out.at[n * size : (n + 1) * size], sem.at[n]
+        started = []
+        place = 0
+        for n, (_, at, rows) in enumerate(order):
+            started.append(
+                pltpu.make_async_copy(
+                    refs[n].at[at : at + rows], out.at[place : place + rows], sem.at[n]
+                )
             )
-            for n, (_, at) in enumerate(order)
-        ]
+            place += rows
         for copy in started:
             copy.start()
         for copy in started:
@@ -414,14 +481,14 @@
 
     return pl.pallas_call(
         kernel,
-        out_shape=pltpu.VMEM((count * size, cols), BF16),
+        out_shape=pltpu.VMEM((total, order[0][0].shape[1]), BF16),
         in_specs=[pl.BlockSpec(memory_space=pl.ANY)] * count,
         out_specs=VMEM,
         scratch_shapes=[pltpu.SemaphoreType.DMA((count,))],
         compiler_params=pltpu.CompilerParams(vmem_limit_bytes=4 * MIB),
         cost_estimate=CHEAP,
         name="stack",
-    )(*[array for array, _ in order])
+    )(*[array for array, _, _ in order])
 
 
 def adam_general(upstreams, hidden_all, w_down, moment_one, moment_two):
@@ -469,35 +536,58 @@
     sections = lax.axis_size("pipe")
     owners = lax.axis_size("dp")
     parts = lax.axis_size("tensor")
-    planned = sections == 4 and owners == 4 and block_input.shape[2] % (128 * owners) == 0
+    width, units = down_weight.shape[1:]
+    planned = sections == 4 and owners == 4 and width % (128 * owners) == 0 and units % (width // owners) == 0
+    planned = planned and loss_grad.shape[0] * (width // owners) % (16 * units) == 0 and parts == 2
     share = loss_grad.shape[0]
     saved = hidden[0]
+    half = saved.shape[0] // 2
     w_down, gates, rows_in, loss, *halves = stage(
         [down_weight[0], gate_act[0], block_input[0], loss_grad], [saved] if planned else []
     )
     turned = None
     upstreams = [loss]
     grads = []
-    blocks = []
     late = ()
     for layer in reversed(range(sections)):
         upstream = upstreams[-1]
         if planned and not layer:
-            arrivals = [from_peers(piece, "tensor") for piece in columns(upstream, owners)]
-            peers = [piece for peer in zip(*arrivals) for piece in peer]
+            peers = [lax.all_gather(upstream, "tensor", axis=0, tiled=True)]
         else:
             peers = from_peers(upstream if grads else loss_grad, "tensor")
         if not grads:
             turned, kept, *sent = section_step(layer, upstream, peers, w_down, None, gates, up_weight[0])
+        elif planned and len(grads) == 2:
+            unit_grad = unit_step(layer, upstream, peers, w_down, gates)
+            kept, *sent = width_step(layer, unit_grad, turned, loss_grad.shape[0], late)
         else:
             kept, *sent = section_step(layer, upstream, peers, w_down, turned, gates, after=late)
+        if planned and not layer:
+            hidden_all = stack(
+                [
+                    (halves[0], 0, half),
+                    (halves[1], 0, half),
+                    (along_upper, 0, half),
+                    (along_rest, 0, half),
+                    (side_rest, 0, half),
+                    (side_lower, 0, half),
+                    (side_rest, half, half),
+                    (along_rest, half, half),
+                ]
+            )
+            packed = [(along_upper, half), (side_lower, half), (corner, 0)]
+            own = collect(upstreams, blocks, packed, [kept, hidden_all])
         arrived = to_peers(sent, "tensor")
         window = len(grads)
         moving = ()
         if planned and window == 0:
-            moving = [halves[:1], halves[1:]]
+            moving = [[(halves[0], 0, half), 1], [(halves[1], 0, half), 2]]
         elif planned and window == 1:
-            moving = [(halves[1], side_lower), (halves[0], along_upper)]
+            moving = [
+                [(halves[1], 0, half), (side_lower, 0, half)],
+                [(halves[0], 0, half), (along_upper, 0, half)],
+                [3],
+            ]
         grad, cuts, handed = norm_step(
             layer,
             kept,
@@ -507,24 +597,30 @@
             norm_gain,
             loss,
             earlier=grads if window >= sections - 2 else (),
-            owners=owners if planned and layer == 1 else 1,
+            owners=owners if planned and window == 2 else 1,
             passed=moving,
         )
         grads.append(grad)
         if layer:
             upstreams.append(lax.ppermute(grad, "pipe", [(layer, layer - 1)]))
         if planned and layer:
-            for k, cut in enumerate(cuts, 1):
-                pairs = [
-                    (s * owners + i, (s - 1) % sections * owners + (i ^ k))
-                    for s in range(sections)
-                    for i in range(owners)
+            if window == 2:
+                blocks = [
+                    lax.ppermute(
+                        cut,
+                        ("pipe", "dp"),
+                        [
+                            (s * owners + i, (s - 1) * owners + (i ^ k))
+                            for s in range(1, sections)
+                            for i in range(owners)
+                        ],
+                    )
+                    for k, cut in enumerate(cuts, 1)
                 ]
-                blocks.append(lax.ppermute(cut, ("pipe", "dp"), pairs))
             if window < 2:
                 exchange = [
                     lax.ppermute(piece, "dp", [(i, i ^ k) for i in range(owners)])
-                    for k, piece in enumerate(handed, 1)
+                    for k, piece in enumerate(handed[:2], 1)
                 ]
             if window == 0:
                 along_upper, side_lower = exchange
@@ -533,25 +629,18 @@
                 )
                 late = [*exchange, *moments]
             elif window == 1:
-                along_rest, side_rest = late = exchange
-            else:
-                late = moments = stage_in_section(
+                along_rest, side_rest = exchange
+                start = (sections - 1) * owners
+                corner = lax.ppermute(
+                    handed[2], ("pipe", "dp"), [(start + i, start + (i ^ 3)) for i in range(owners)]
+                )
+                moments = stage_in_section(
                     [moment_one[0], moment_two[0]], lambda section: section == sections - 2, moments, [grad]
                 )
+                late = [*exchange, *moments]
+            else:
+                late = ()
     if planned:
-        half = saved.shape[0] // 2
-        order = [
-            (halves[0], 0),
-            (halves[1], 0),
-            (along_upper, 0),
-            (along_rest, 0),
-            (side_rest, 0),
-            (side_lower, 0),
-            (side_rest, half),
-            (along_rest, half),
-        ]
-        hidden_all = stack(order, half)
-        own = collect(upstreams, blocks, [kept, hidden_all])
         first, second, updated = adam_step(
             [own, *from_peers(own, "tensor")], hidden_all, w_down, *moments, owners, parts
         )

time: 71.2 us -> 67.8 us (0.952)
  waiting for transfers between devices: 34.1 us -> 28.8 us
  blocking collectives: 0 us -> 2.17 us
    ppermute x3, waiting for transfers between devices: 11.7 us -> 6.39 us  [on_device(): upstreams.append(lax.ppermute(grad, 'pipe', [(layer, layer - 1)]))]
    all_gather x0 -> x1, blocking collectives: none -> 2.17 us  [on_device(): peers = [lax.all_gather(upstream, 'tensor', axis=0, tiled=True)]]
    ppermute x4, waiting for transfers between devices: 13.7 us -> 15.1 us  [on_device(): lax.ppermute(piece, 'dp', [(i, i ^ k) for i in range(owners)])]
    ppermute x8 -> x4, starting transfers between devices: 1.67 us -> 0.59 us  [from_peers(): lax.ppermute(value, axis, [((i + k) % size, i) for i in range(size)])]
    ppermute x3 -> x4, waiting for transfers between devices: 1.71 us -> 0.79 us  [the longest x3 0.78 us: on_device(): lax.ppermute(cut, ('pipe', 'dp'), [(s * owners + i, (s - 1) * owners + (i...]
    ppermute x8 -> x4, waiting for transfers between devices: 2.41 us -> 1.5 us  [from_peers(): lax.ppermute(value, axis, [((i + k) % size, i) for i in range(size)])]
    ppermute x3 -> x4, starting transfers between devices: 3.89 us -> 4.54 us  [the longest x3 3.88 us: on_device(): lax.ppermute(cut, ('pipe', 'dp'), [(s * owners + i, (s - 1) * owners + (i...]
    pallas_call x4 -> x3, Pallas kernels: 6.61 us -> 6.6 us  [section_step(): pl.pallas_call(kernel, out_shape=out_shape, in_specs=in_specs, out_specs=...]
  transfers between devices with their start and end apart: 22 -> 19, of which waited for: 14 -> 11; matrix products, arithmetic and copies ran while one was open for 0% -> 0% of each run, Pallas kernels for 16% -> 16%
where the time goes in v3:
time: 67.8 us; the launch traced here: 67.6 us
  waiting for transfers between devices  28.8 us (42%)
  Pallas kernels  21.2 us (31%)
  starting transfers between devices  14.4 us (21%)
  blocking collectives  2.17 us (3%)
  between operations  0.96 us (1%)
    ppermute x4, waiting for transfers between devices, on_device(): lax.ppermute(piece, 'dp', [(i, i ^ k) for i in range(owners)])  15.1 us
    pallas_call x3, Pallas kernels, section_step(): pl.pallas_call(kernel, out_shape=out_shape, in_specs=in_specs, out_specs=...  6.6 us
    ppermute x3, waiting for transfers between devices, on_device(): upstreams.append(lax.ppermute(grad, 'pipe', [(layer, layer - 1)]))  6.39 us
    ppermute x4, starting transfers between devices, on_device(): lax.ppermute(piece, 'dp', [(i, i ^ k) for i in range(owners)])  6.34 us
    pallas_call x1, Pallas kernels, adam_step(): pl.pallas_call(functools.partial(adam_kernel, (owners, parts, blocks[0].s...  5.81 us
    ppermute x4, waiting for transfers between devices, to_peers(): lax.ppermute(value, axis, [(i, (i + k) % size) for i in range(size)])  5.04 us
    ppermute x3, starting transfers between devices, on_device(): lax.ppermute(cut, ('pipe', 'dp'), [(s * owners + i, (s - 1) * owners + (i...  3.88 us
    pallas_call x1, Pallas kernels, stage(): pl.pallas_call(kernel, out_shape=[pltpu.VMEM(shape, arrays[n].dtype) for...  3.87 us
  transfers between devices with their start and end apart: 19, of which 11 were waited for; matrix products, arithmetic and copies ran while one was open for 0% of the time, Pallas kernels for 16%

profile of v3, /device:TPU:0, one launch (start us, length us, event | category | flops | bytes accessed | tf_op | source)
XLA Modules:
  0.0 67.6 jit_solution(1283064344630325069)
XLA Ops:
  0.6 0.5 collective-permute-start
  1.2 3.9 %stage.1 = (bf16[2048,2048]{1,0:T(8,128)(2,1)S(1)}, bf16[128,2048]{1,0:T(8,128)(2,1)S(1)}, bf16[64,2048]{1,0:T(8,128)(2,1)S(1)}, bf16[64,2048]{1,0:T(8,128)(2,1)...) custom-call(bf16[2048,2048]{1,0:T(8,128)(2,1)} %bitcast.15, bf16[128,2048]{1,0:T(8,128)(2,1)} %bitcast.17, ...), custom_call_target="tpu_custom_call" | custom-call | bytes 19922944 | tf_op jit(solution)/shard_map/stage/pallas_call | solution.py:63
  5.0 0.0 collective-permute-done.refs_1_
  5.0 0.0 copy-start
  5.1 4.2 %section_step.3 = (bf16[2048,2048]{1,0:T(8,128)(2,1)S(1)}, f32[64,2048]{1,0:T(8,128)S(1)}, bf16[64,2048]{1,0:T(8,128)(2,1)S(1)}) custom-call(bf16[64,2048]{1,0:T(8,128)(2,1)S(1)} %get-tuple-element.37.refs_0_.refs_1_.refs_4_.refs_6_.refs_7_, bf16[64,2048]{1,0:T(8,128)(2,1)S(1)} %collective-permute-done.refs_1_, ...), custom_call_target="tpu_custom_call" | custom-call | tf_op jit(solution)/shard_map/section_step/pallas_call | solution.py:252
  9.3 0.1 collective-permute-start.1
  9.4 1.5 %collective-permute-done.1.refs_0_ = bf16[64,2048]{1,0:T(8,128)(2,1)S(1)} collective-permute-done((bf16[64,2048]{1,0:T(8,128)(2,1)S(1)}, bf16[64,2048]{1,0:T(8,128)(2,1)S(1)}, u32[]{:S(2)}, u32[]{:S(2)}) %collective-permute-start.1) | collective-permute-done | bytes 262176 | tf_op jit(solution)/shard_map/ppermute | solution.py:520
  10.9 0.0 copy-done
  11.0 0.7 %collective-permute-start.2 = (bf16[64,2048]{1,0:T(8,128)(2,1)S(1)}, bf16[64,2048]{1,0:T(8,128)(2,1)S(1)}, u32[]{:S(2)}, u32[]{:S(2)}) collective-permute-start(bf16[64,2048]{1,0:T(8,128)(2,1)S(1)} %get-tuple-element.45.refs_2_.refs_4_), channel_id=1, source_target_pairs={{24,16},{25,17},{26,18},{27,19},{28,20},{29,21},{30,22},{31,23}} | collective-permute-start | bytes 786440 | tf_op jit(solution)/shard_map/ppermute | solution.py:605
  11.6 2.7 %collective-permute-start.4 = (bf16[80,2048]{1,0:T(8,128)(2,1)S(1)}, bf16[80,2048]{1,0:T(8,128)(2,1)S(1)}, u32[]{:S(2)}, u32[]{:S(2)}) collective-permute-start(bf16[80,2048]{1,0:T(8,128)(2,1)S(1)} %get-tuple-element.47), channel_id=1, source_target_pairs={{0,2},{2,0},{4,6},{6,4},{1,3},{3,1},{5,7},{7,5},{8,10},{10,8},{12,... | collective-permute-start | bytes 983048 | tf_op jit(solution)/shard_map/ppermute | solution.py:622
  14.3 1.5 %collective-permute-start.5 = (bf16[80,2048]{1,0:T(8,128)(2,1)S(1)}, bf16[80,2048]{1,0:T(8,128)(2,1)S(1)}, u32[]{:S(2)}, u32[]{:S(2)}) collective-permute-start(bf16[80,2048]{1,0:T(8,128)(2,1)S(1)} %get-tuple-element.48), channel_id=1, source_target_pairs={{0,4},{2,6},{4,0},{6,2},{1,5},{3,7},{5,1},{7,3},{8,12},{10,14},{12... | collective-permute-start | bytes 983048 | tf_op jit(solution)/shard_map/ppermute | solution.py:622
  15.9 0.0 collective-permute-done.2.refs_0_.refs_1_
  15.9 0.0 collective-permute-start.3
  15.9 3.5 %stage_in_section.2 = (f32[512,2048]{1,0:T(8,128)S(1)}, f32[512,2048]{1,0:T(8,128)S(1)}) custom-call(f32[512,2048]{1,0:T(8,128)} %bitcast.11, f32[512,2048]{1,0:T(8,128)} %bitcast.13, bf16[64,2048]{1,0:T(8,128)(2,1)S(1)} %get-tuple-element.45.refs_2_.refs_4_), custom_call_target="tpu_custom_call" | custom-call | tf_op jit(solution)/shard_map/stage_in_section/pallas_call | solution.py:90
  19.4 3.2 %collective-permute-done.4.refs_5_.refs_8_.refs_2_.refs_7_ = bf16[80,2048]{1,0:T(8,128)(2,1)S(1)} collective-permute-done((bf16[80,2048]{1,0:T(8,128)(2,1)S(1)}, bf16[80,2048]{1,0:T(8,128)(2,1)S(1)}, u32[]{:S(2)}, u32[]{:S(2)}) %collective-permute-start.4) | collective-permute-done | bytes 327712 | tf_op jit(solution)/shard_map/ppermute | solution.py:622
  22.6 1.5 %collective-permute-done.5.refs_6_.refs_5_.refs_8_ = bf16[80,2048]{1,0:T(8,128)(2,1)S(1)} collective-permute-done((bf16[80,2048]{1,0:T(8,128)(2,1)S(1)}, bf16[80,2048]{1,0:T(8,128)(2,1)S(1)}, u32[]{:S(2)}, u32[]{:S(2)}) %collective-permute-start.5) | collective-permute-done | bytes 327712 | tf_op jit(solution)/shard_map/ppermute | solution.py:622
  24.0 0.0 collective-permute-done.3.refs_1_
  24.0 0.0 collective-permute-start.6
  24.0 1.5 %collective-permute-done.6.refs_0_ = bf16[64,2048]{1,0:T(8,128)(2,1)S(1)} collective-permute-done((bf16[64,2048]{1,0:T(8,128)(2,1)S(1)}, bf16[64,2048]{1,0:T(8,128)(2,1)S(1)}, u32[]{:S(2)}, u32[]{:S(2)}) %collective-permute-start.6) | collective-permute-done | bytes 262176 | tf_op jit(solution)/shard_map/ppermute | solution.py:520
  25.6 0.1 norm_step.5
  25.7 0.7 %collective-permute-start.7 = (bf16[64,2048]{1,0:T(8,128)(2,1)S(1)}, bf16[64,2048]{1,0:T(8,128)(2,1)S(1)}, u32[]{:S(2)}, u32[]{:S(2)}) collective-permute-start(bf16[64,2048]{1,0:T(8,128)(2,1)S(1)} %get-tuple-element.53.refs_4_.refs_5_), channel_id=1, source_target_pairs={{16,8},{17,9},{18,10},{19,11},{20,12},{21,13},{22,14},{23,15}} | collective-permute-start | bytes 786440 | tf_op jit(solution)/shard_map/ppermute | solution.py:605
  26.3 0.4 collective-permute-start.9
  26.8 1.7 %collective-permute-start.10 = (bf16[128,2048]{1,0:T(8,128)(2,1)S(1)}, bf16[128,2048]{1,0:T(8,128)(2,1)S(1)}, u32[]{:S(2)}, u32[]{:S(2)}) collective-permute-start(bf16[128,2048]{1,0:T(8,128)(2,1)S(1)} %get-tuple-element.55), channel_id=1, source_target_pairs={{0,4},{2,6},{4,0},{6,2},{1,5},{3,7},{5,1},{7,3},{8,12},{10,14},{12... | collective-permute-start | bytes 1572872 | tf_op jit(solution)/shard_map/ppermute | solution.py:622
  28.5 0.0 collective-permute-done.7.own_ref.refs_1_.refs_2_
  28.5 0.0 collective-permute-start.8
  28.5 1.5 %collective-permute-done.8.refs_0_ = bf16[64,2048]{1,0:T(8,128)(2,1)S(1)} collective-permute-done((bf16[64,2048]{1,0:T(8,128)(2,1)S(1)}, bf16[64,2048]{1,0:T(8,128)(2,1)S(1)}, u32[]{:S(2)}, u32[]{:S(2)}) %collective-permute-start.8) | collective-permute-done | bytes 262176 | tf_op jit(solution)/shard_map/ppermute | solution.py:514
  30.0 10.4 %collective-permute-done.9.refs_0_.refs_3_.refs_7_ = bf16[128,2048]{1,0:T(8,128)(2,1)S(1)} collective-permute-done((bf16[128,2048]{1,0:T(8,128)(2,1)S(1)}, bf16[128,2048]{1,0:T(8,128)(2,1)S(1)}, u32[]{:S(2)}, u32[]{:S(2)}) %collective-permute-start.9) | collective-permute-done | bytes 524320 | tf_op jit(solution)/shard_map/ppermute | solution.py:622
  40.4 0.1 collective-permute-done.10.refs_1_.refs_4_.refs_6_
  40.4 0.0 collective-permute-start.11
  40.5 1.5 %collective-permute-done.11.refs_0_ = bf16[64,2048]{1,0:T(8,128)(2,1)S(1)} collective-permute-done((bf16[64,2048]{1,0:T(8,128)(2,1)S(1)}, bf16[64,2048]{1,0:T(8,128)(2,1)S(1)}, u32[]{:S(2)}, u32[]{:S(2)}) %collective-permute-start.11) | collective-permute-done | bytes 262176 | tf_op jit(solution)/shard_map/ppermute | solution.py:520
  42.0 1.3 %collective-permute-start.12 = (bf16[64,2048]{1,0:T(8,128)(2,1)S(1)}, bf16[64,2048]{1,0:T(8,128)(2,1)S(1)}, u32[]{:S(2)}, u32[]{:S(2)}) collective-permute-start(bf16[64,2048]{1,0:T(8,128)(2,1)S(1)} %get-tuple-element.60.refs_6_), channel_id=1, source_target_pairs={{8,0},{9,1},{10,2},{11,3},{12,4},{13,5},{14,6},{15,7}} | collective-permute-start | bytes 786440 | tf_op jit(solution)/shard_map/ppermute | solution.py:605
  43.3 0.7 collective-permute-start.17
  43.9 0.2 stack.1.refs_11_.refs_2_
  44.2 1.3 %collective-permute-start.14 = (bf16[64,512]{1,0:T(8,128)(2,1)S(1)}, bf16[64,512]{1,0:T(8,128)(2,1)S(1)}, u32[]{:S(2)}, u32[]{:S(2)}) collective-permute-start(bf16[64,512]{1,0:T(8,128)(2,1)S(1)} %get-tuple-element.63), channel_id=1, source_target_pairs={{8,2},{10,0},{12,6},{14,4},{16,10},{18,8},{20,14},{22,12},{24,18},... | collective-permute-start | bytes 196616 | tf_op jit(solution)/shard_map/ppermute | solution.py:609
  45.5 1.3 %collective-permute-start.15 = (bf16[64,512]{1,0:T(8,128)(2,1)S(1)}, bf16[64,512]{1,0:T(8,128)(2,1)S(1)}, u32[]{:S(2)}, u32[]{:S(2)}) collective-permute-start(bf16[64,512]{1,0:T(8,128)(2,1)S(1)} %get-tuple-element.64), channel_id=1, source_target_pairs={{8,4},{10,6},{12,0},{14,2},{16,12},{18,14},{20,8},{22,10},{24,20},... | collective-permute-start | bytes 196616 | tf_op jit(solution)/shard_map/ppermute | solution.py:609
  46.8 1.3 %collective-permute-start.16 = (bf16[64,512]{1,0:T(8,128)(2,1)S(1)}, bf16[64,512]{1,0:T(8,128)(2,1)S(1)}, u32[]{:S(2)}, u32[]{:S(2)}) collective-permute-start(bf16[64,512]{1,0:T(8,128)(2,1)S(1)} %get-tuple-element.65), channel_id=1, source_target_pairs={{8,6},{10,4},{12,2},{14,0},{16,14},{18,12},{20,10},{22,8},{24,22},... | collective-permute-start | bytes 196616 | tf_op jit(solution)/shard_map/ppermute | solution.py:609
  48.1 6.4 %collective-permute-done.12.refs_0_.refs_1_.refs_3_ = bf16[64,2048]{1,0:T(8,128)(2,1)S(1)} collective-permute-done((bf16[64,2048]{1,0:T(8,128)(2,1)S(1)}, bf16[64,2048]{1,0:T(8,128)(2,1)S(1)}, u32[]{:S(2)}, u32[]{:S(2)}) %collective-permute-start.12) | collective-permute-done | bytes 262176 | tf_op jit(solution)/shard_map/ppermute | solution.py:605
  54.5 2.2 %all_gather.3.refs_1_ = bf16[128,2048]{1,0:T(8,128)(2,1)S(1)} all-gather(bf16[64,2048]{1,0:T(8,128)(2,1)S(1)} %collective-permute-done.12.refs_0_.refs_1_.refs_3_), channel_id=1, replica_groups=mesh['pipe'=4,'dp'=4,'tensor'=2] {'tensor'}, dimensions={0}, use_global_device_ids=true | all-gather | bytes 786432 | tf_op jit(solution)/shard_map/all_gather | solution.py:555
  56.6 2.4 %section_step.5 = (f32[64,2048]{1,0:T(8,128)S(1)}, bf16[64,2048]{1,0:T(8,128)(2,1)S(1)}) custom-call(bf16[64,2048]{1,0:T(8,128)(2,1)S(1)} %collective-permute-done.12.refs_0_.refs_1_.refs_3_, bf16[128,2048]{1,0:T(8,128)(2,1)S(1)} %all_gather.3.refs_1_, bf16[2048,2048]{1,0:T(8,128)(2,1)S(1)} %get-tuple-element.38.refs_2_.refs_1_.refs_3_, ...), custom_call_target="tpu_custom_call" | custom-call | tf_op jit(solution)/shard_map/section_step/pallas_call | solution.py:252
  59.0 0.2 collective-permute-start.13
  59.2 0.0 collective-permute-done.17.refs_9_
  59.2 0.0 collective-permute-done.14.refs_4_
  59.2 0.0 collective-permute-done.15.refs_5_
  59.2 0.8 %collective-permute-done.16.refs_6_ = bf16[64,512]{1,0:T(8,128)(2,1)S(1)} collective-permute-done((bf16[64,512]{1,0:T(8,128)(2,1)S(1)}, bf16[64,512]{1,0:T(8,128)(2,1)S(1)}, u32[]{:S(2)}, u32[]{:S(2)}) %collective-permute-start.16) | collective-permute-done | bytes 65568 | tf_op jit(solution)/shard_map/ppermute | solution.py:609
  60.0 0.1 collective-permute-start.18
  60.1 0.5 collective-permute-done.13.refs_0_
  60.6 1.0 %norm_step.7 = bf16[64,2048]{1,0:T(8,128)(2,1)} custom-call(f32[64,2048]{1,0:T(8,128)S(1)} %get-tuple-element.61.kept_ref.refs_10_, bf16[64,2048]{1,0:T(8,128)(2,1)S(1)} %collective-permute-done.13.refs_0_, bf16[64,2048]{1,0:T(8,128)(2,1)S(1)} %collective-permute-done.12.refs_0_.refs_1_.refs_3_, bf16[64,2048]{1,0:T(8,128)(2,1)S(1)} %get-tuple-element.42.refs_2_, ...), custom_call_target="tpu_custom_call" | custom-call | tf_op jit(solution)/shard_map/norm_step/pallas_call | solution.py:341
  61.6 0.0 collective-permute-done.18.refs_1_
  61.6 5.8 %adam_step.1 = (f32[512,2048]{1,0:T(8,128)}, f32[512,2048]{1,0:T(8,128)}, f32[512,2048]{1,0:T(8,128)}) custom-call(bf16[256,512]{1,0:T(8,128)(2,1)S(1)} %collect.1.refs_0_, bf16[256,512]{1,0:T(8,128)(2,1)S(1)} %collective-permute-done.18.refs_1_, bf16[512,2048]{1,0:T(8,128)(2,1)S(1)} %stack.1.refs_11_.refs_2_, ...), custom_call_target="tpu_custom_call" | custom-call | tf_op jit(solution)/shard_map/adam_step/pallas_call | solution.py:448
  (7 shorter events, 0.1 us)
Async XLA Ops:
  0.6 4.4 %collective-permute-start = (bf16[64,2048]{1,0:T(8,128)(2,1)}, bf16[64,2048]{1,0:T(8,128)(2,1)S(1)}, u32[]{:S(2)}, u32[]{:S(2)}) collective-permute-start(bf16[64,2048]{1,0:T(8,128)(2,1)} %refs_3_.5), channel_id=1, source_target_pairs={{1,0},{0,1},{3,2},{2,3},{5,4},{4,5},{7,6},{6,7},{9,8},{8,9},{11,10... | collective-permute-start | bytes 786440 | tf_op jit(solution)/shard_map/ppermute | solution.py:514
  5.0 5.9 %copy-start = (f32[1,2048]{1,0:T(1,128)S(1)}, f32[1,2048]{1,0:T(1,128)}, u32[]{:S(2)}) copy-start(f32[1,2048]{1,0:T(1,128)} %refs_3_.9) | copy-start | bytes 24580
  9.3 1.6 %collective-permute-start.1 = (bf16[64,2048]{1,0:T(8,128)(2,1)S(1)}, bf16[64,2048]{1,0:T(8,128)(2,1)S(1)}, u32[]{:S(2)}, u32[]{:S(2)}) collective-permute-start(bf16[64,2048]{1,0:T(8,128)(2,1)S(1)} %get-tuple-element.41), channel_id=1, source_target_pairs={{0,1},{1,0},{2,3},{3,2},{4,5},{5,4},{6,7},{7,6},{8,9},{9,8},{10,11... | collective-permute-start | bytes 786440 | tf_op jit(solution)/shard_map/ppermute | solution.py:520
  11.0 4.9 %collective-permute-start.2 = (bf16[64,2048]{1,0:T(8,128)(2,1)S(1)}, bf16[64,2048]{1,0:T(8,128)(2,1)S(1)}, u32[]{:S(2)}, u32[]{:S(2)}) collective-permute-start(bf16[64,2048]{1,0:T(8,128)(2,1)S(1)} %get-tuple-element.45.refs_2_.refs_4_), channel_id=1, source_target_pairs={{24,16},{25,17},{26,18},{27,19},{28,20},{29,21},{30,22},{31,23}} | collective-permute-start | bytes 786440 | tf_op jit(solution)/shard_map/ppermute | solution.py:605
  11.6 10.9 %collective-permute-start.4 = (bf16[80,2048]{1,0:T(8,128)(2,1)S(1)}, bf16[80,2048]{1,0:T(8,128)(2,1)S(1)}, u32[]{:S(2)}, u32[]{:S(2)}) collective-permute-start(bf16[80,2048]{1,0:T(8,128)(2,1)S(1)} %get-tuple-element.47), channel_id=1, source_target_pairs={{0,2},{2,0},{4,6},{6,4},{1,3},{3,1},{5,7},{7,5},{8,10},{10,8},{12,... | collective-permute-start | bytes 983048 | tf_op jit(solution)/shard_map/ppermute | solution.py:622
  14.3 9.7 %collective-permute-start.5 = (bf16[80,2048]{1,0:T(8,128)(2,1)S(1)}, bf16[80,2048]{1,0:T(8,128)(2,1)S(1)}, u32[]{:S(2)}, u32[]{:S(2)}) collective-permute-start(bf16[80,2048]{1,0:T(8,128)(2,1)S(1)} %get-tuple-element.48), channel_id=1, source_target_pairs={{0,4},{2,6},{4,0},{6,2},{1,5},{3,7},{5,1},{7,3},{8,12},{10,14},{12... | collective-permute-start | bytes 983048 | tf_op jit(solution)/shard_map/ppermute | solution.py:622
  15.9 8.2 %collective-permute-start.3 = (bf16[64,2048]{1,0:T(8,128)(2,1)S(1)}, bf16[64,2048]{1,0:T(8,128)(2,1)S(1)}, u32[]{:S(2)}, u32[]{:S(2)}) collective-permute-start(bf16[64,2048]{1,0:T(8,128)(2,1)S(1)} %collective-permute-done.2.refs_0_.refs_1_), channel_id=1, source_target_pairs={{1,0},{0,1},{3,2},{2,3},{5,4},{4,5},{7,6},{6,7},{9,8},{8,9},{11,10... | collective-permute-start | bytes 786440 | tf_op jit(solution)/shard_map/ppermute | solution.py:514
  24.0 1.5 %collective-permute-start.6 = (bf16[64,2048]{1,0:T(8,128)(2,1)S(1)}, bf16[64,2048]{1,0:T(8,128)(2,1)S(1)}, u32[]{:S(2)}, u32[]{:S(2)}) collective-permute-start(bf16[64,2048]{1,0:T(8,128)(2,1)S(1)} %get-tuple-element.52), channel_id=1, source_target_pairs={{0,1},{1,0},{2,3},{3,2},{4,5},{5,4},{6,7},{7,6},{8,9},{9,8},{10,11... | collective-permute-start | bytes 786440 | tf_op jit(solution)/shard_map/ppermute | solution.py:520
  25.7 2.8 %collective-permute-start.7 = (bf16[64,2048]{1,0:T(8,128)(2,1)S(1)}, bf16[64,2048]{1,0:T(8,128)(2,1)S(1)}, u32[]{:S(2)}, u32[]{:S(2)}) collective-permute-start(bf16[64,2048]{1,0:T(8,128)(2,1)S(1)} %get-tuple-element.53.refs_4_.refs_5_), channel_id=1, source_target_pairs={{16,8},{17,9},{18,10},{19,11},{20,12},{21,13},{22,14},{23,15}} | collective-permute-start | bytes 786440 | tf_op jit(solution)/shard_map/ppermute | solution.py:605
  26.3 14.0 %collective-permute-start.9 = (bf16[128,2048]{1,0:T(8,128)(2,1)S(1)}, bf16[128,2048]{1,0:T(8,128)(2,1)S(1)}, u32[]{:S(2)}, u32[]{:S(2)}) collective-permute-start(bf16[128,2048]{1,0:T(8,128)(2,1)S(1)} %get-tuple-element.54), channel_id=1, source_target_pairs={{0,2},{2,0},{4,6},{6,4},{1,3},{3,1},{5,7},{7,5},{8,10},{10,8},{12,... | collective-permute-start | bytes 1572872 | tf_op jit(solution)/shard_map/ppermute | solution.py:622
  26.8 13.7 %collective-permute-start.10 = (bf16[128,2048]{1,0:T(8,128)(2,1)S(1)}, bf16[128,2048]{1,0:T(8,128)(2,1)S(1)}, u32[]{:S(2)}, u32[]{:S(2)}) collective-permute-start(bf16[128,2048]{1,0:T(8,128)(2,1)S(1)} %get-tuple-element.55), channel_id=1, source_target_pairs={{0,4},{2,6},{4,0},{6,2},{1,5},{3,7},{5,1},{7,3},{8,12},{10,14},{12... | collective-permute-start | bytes 1572872 | tf_op jit(solution)/shard_map/ppermute | solution.py:622
  28.5 1.5 %collective-permute-start.8 = (bf16[64,2048]{1,0:T(8,128)(2,1)S(1)}, bf16[64,2048]{1,0:T(8,128)(2,1)S(1)}, u32[]{:S(2)}, u32[]{:S(2)}) collective-permute-start(bf16[64,2048]{1,0:T(8,128)(2,1)S(1)} %collective-permute-done.7.own_ref.refs_1_.refs_2_), channel_id=1, source_target_pairs={{1,0},{0,1},{3,2},{2,3},{5,4},{4,5},{7,6},{6,7},{9,8},{8,9},{11,10... | collective-permute-start | bytes 786440 | tf_op jit(solution)/shard_map/ppermute | solution.py:514
  40.4 1.5 %collective-permute-start.11 = (bf16[64,2048]{1,0:T(8,128)(2,1)S(1)}, bf16[64,2048]{1,0:T(8,128)(2,1)S(1)}, u32[]{:S(2)}, u32[]{:S(2)}) collective-permute-start(bf16[64,2048]{1,0:T(8,128)(2,1)S(1)} %get-tuple-element.59), channel_id=1, source_target_pairs={{0,1},{1,0},{2,3},{3,2},{4,5},{5,4},{6,7},{7,6},{8,9},{9,8},{10,11... | collective-permute-start | bytes 786440 | tf_op jit(solution)/shard_map/ppermute | solution.py:520
  42.0 12.5 %collective-permute-start.12 = (bf16[64,2048]{1,0:T(8,128)(2,1)S(1)}, bf16[64,2048]{1,0:T(8,128)(2,1)S(1)}, u32[]{:S(2)}, u32[]{:S(2)}) collective-permute-start(bf16[64,2048]{1,0:T(8,128)(2,1)S(1)} %get-tuple-element.60.refs_6_), channel_id=1, source_target_pairs={{8,0},{9,1},{10,2},{11,3},{12,4},{13,5},{14,6},{15,7}} | collective-permute-start | bytes 786440 | tf_op jit(solution)/shard_map/ppermute | solution.py:605
  43.3 15.9 %collective-permute-start.17 = (bf16[16,2048]{1,0:T(8,128)(2,1)S(1)}, bf16[16,2048]{1,0:T(8,128)(2,1)S(1)}, u32[]{:S(2)}, u32[]{:S(2)}) collective-permute-start(bf16[16,2048]{1,0:T(8,128)(2,1)S(1)} %get-tuple-element.66), channel_id=1, source_target_pairs={{24,30},{26,28},{28,26},{30,24},{25,31},{27,29},{29,27},{31,25}} | collective-permute-start | bytes 196616 | tf_op jit(solution)/shard_map/ppermute | solution.py:634
  44.2 15.0 %collective-permute-start.14 = (bf16[64,512]{1,0:T(8,128)(2,1)S(1)}, bf16[64,512]{1,0:T(8,128)(2,1)S(1)}, u32[]{:S(2)}, u32[]{:S(2)}) collective-permute-start(bf16[64,512]{1,0:T(8,128)(2,1)S(1)} %get-tuple-element.63), channel_id=1, source_target_pairs={{8,2},{10,0},{12,6},{14,4},{16,10},{18,8},{20,14},{22,12},{24,18},... | collective-permute-start | bytes 196616 | tf_op jit(solution)/shard_map/ppermute | solution.py:609
  45.5 13.7 %collective-permute-start.15 = (bf16[64,512]{1,0:T(8,128)(2,1)S(1)}, bf16[64,512]{1,0:T(8,128)(2,1)S(1)}, u32[]{:S(2)}, u32[]{:S(2)}) collective-permute-start(bf16[64,512]{1,0:T(8,128)(2,1)S(1)} %get-tuple-element.64), channel_id=1, source_target_pairs={{8,4},{10,6},{12,0},{14,2},{16,12},{18,14},{20,8},{22,10},{24,20},... | collective-permute-start | bytes 196616 | tf_op jit(solution)/shard_map/ppermute | solution.py:609
  46.8 13.2 %collective-permute-start.16 = (bf16[64,512]{1,0:T(8,128)(2,1)S(1)}, bf16[64,512]{1,0:T(8,128)(2,1)S(1)}, u32[]{:S(2)}, u32[]{:S(2)}) collective-permute-start(bf16[64,512]{1,0:T(8,128)(2,1)S(1)} %get-tuple-element.65), channel_id=1, source_target_pairs={{8,6},{10,4},{12,2},{14,0},{16,14},{18,12},{20,10},{22,8},{24,22},... | collective-permute-start | bytes 196616 | tf_op jit(solution)/shard_map/ppermute | solution.py:609
  59.0 1.6 %collective-permute-start.13 = (bf16[64,2048]{1,0:T(8,128)(2,1)S(1)}, bf16[64,2048]{1,0:T(8,128)(2,1)S(1)}, u32[]{:S(2)}, u32[]{:S(2)}) collective-permute-start(bf16[64,2048]{1,0:T(8,128)(2,1)S(1)} %get-tuple-element.62), channel_id=1, source_target_pairs={{0,1},{1,0},{2,3},{3,2},{4,5},{5,4},{6,7},{7,6},{8,9},{9,8},{10,11... | collective-permute-start | bytes 786440 | tf_op jit(solution)/shard_map/ppermute | solution.py:520
  60.0 1.6 %collective-permute-start.18 = (bf16[256,512]{1,0:T(8,128)(2,1)S(1)}, bf16[256,512]{1,0:T(8,128)(2,1)S(1)}, u32[]{:S(2)}, u32[]{:S(2)}) collective-permute-start(bf16[256,512]{1,0:T(8,128)(2,1)S(1)} %collect.1.refs_0_), channel_id=1, source_target_pairs={{1,0},{0,1},{3,2},{2,3},{5,4},{4,5},{7,6},{6,7},{9,8},{8,9},{11,10... | collective-permute-start | bytes 786440 | tf_op jit(solution)/shard_map/ppermute | solution.py:514

commit v4 on v3

--- a/solution.py
+++ b/solution.py
@@ -44,35 +44,26 @@
     return started
 
 
-def stage(arrays, split=(), after=()):
-    pieces = [(n, slice(None)) for n in range(len(arrays))]
-    for n, array in enumerate(split, len(arrays)):
-        half = array.shape[0] // 2
-        pieces += [(n, slice(0, half)), (n, slice(half, 2 * half))]
-    arrays = [*arrays, *split]
-    shapes = [(arrays[n][rows].shape if rows.start is not None else arrays[n].shape) for n, rows in pieces]
+def stage(arrays):
     count = len(arrays)
 
     def kernel(*refs):
-        sources, targets, sem = refs[:count], refs[count + len(after) : -1], refs[-1]
-        pairs = [(sources[n].at[rows], target) for (n, rows), target in zip(pieces, targets)]
-        for array in copies(pairs, sem, 2):
+        for array in copies(list(zip(refs[:count], refs[count:-1])), refs[-1], 2):
             for copy in array:
                 copy.wait()
 
     return pl.pallas_call(
         kernel,
-        out_shape=[pltpu.VMEM(shape, arrays[n].dtype) for (n, _), shape in zip(pieces, shapes)],
-        in_specs=[pl.BlockSpec(memory_space=pltpu.HBM)] * count
-        + [pl.BlockSpec(memory_space=pl.ANY)] * len(after),
-        out_specs=[VMEM] * len(pieces),
-        scratch_shapes=[pltpu.SemaphoreType.DMA((len(pieces), 2))],
+        out_shape=[pltpu.VMEM(a.shape, a.dtype) for a in arrays],
+        in_specs=[pl.BlockSpec(memory_space=pltpu.HBM)] * count,
+        out_specs=[VMEM] * count,
+        scratch_shapes=[pltpu.SemaphoreType.DMA((count, 2))],
         compiler_params=pltpu.CompilerParams(vmem_limit_bytes=4 * MIB),
         cost_estimate=pl.CostEstimate(
             flops=0, bytes_accessed=sum(2 * a.size * a.dtype.itemsize for a in arrays), transcendentals=0
         ),
         name="stage",
-    )(*[pltpu.with_memory_space_constraint(a, pltpu.HBM) for a in arrays], *after)
+    )(*[pltpu.with_memory_space_constraint(a, pltpu.HBM) for a in arrays])
 
 
 def stage_in_section(arrays, wanted, held, after):
@@ -194,15 +185,21 @@
     )(unit_grad, turned, *after)
 
 
-def first_kernel(layer, parts, pieces, own_ref, *refs):
+def first_kernel(layer, parts, pieces, further, own_ref, *refs):
     peer_refs, refs = refs[:pieces], refs[pieces:]
-    down_ref, up_ref, gate_ref, turned_ref, kept_ref = refs[:5]
-    sent_refs = refs[5 : parts + 4]
-    rows_ref, unit_ref, held_ref, sem = refs[parts + 4 :]
+    down_ref, up_ref, gate_ref = refs[:3]
+    count = 1 + max((n for n, _ in further), default=-1)
+    source_refs, refs = refs[3 : 3 + count], refs[3 + count :]
+    turned_ref, kept_ref = refs[:2]
+    sent_refs = refs[2 : parts + 1]
+    staged_refs = refs[parts + 1 : parts + 1 + len(further)]
+    rows_ref, unit_ref, held_ref, sem, further_sem = refs[parts + 1 + len(further) :]
     share = own_ref.shape[0]
     chunks = sem.shape[1]
     size = held_ref.shape[0] // chunks
     (arriving,) = copies([(up_ref, held_ref)], sem, chunks)
+    pairs = [(source_refs[n].at[rows], staged) for (n, rows), staged in zip(further, staged_refs)]
+    behind = copies(pairs, further_sem, 1)
     starts = lax.axis_index("pipe") == layer
 
     @pl.when(starts)
@@ -225,41 +222,70 @@
         def _(cols=cols):
             turned_ref[:, cols] = held_ref[cols, :].T
 
-
-def section_step(layer, own, peers, w_down, turned, gates, w_up=None, after=()):
+    for (copy,) in behind:
+        copy.wait()
+
+
+def first_step(layer, own, peers, w_down, w_up, gates, arrays, split):
+    share, width = own.shape
+    units = w_down.shape[1]
+    parts = lax.axis_size("tensor")
+    rows = share * parts
+    further = [(n, slice(0, a.shape[0])) for n, a in enumerate(arrays)]
+    for n, a in enumerate(split, len(arrays)):
+        half = a.shape[0] // 2
+        further += [(n, slice(0, half)), (n, slice(half, 2 * half))]
+    sources = [*arrays, *split]
+    hbm = pl.BlockSpec(memory_space=pltpu.HBM)
+    outs = pl.pallas_call(
+        functools.partial(first_kernel, layer, parts, len(peers), further),
+        out_shape=[pltpu.VMEM((units, width), BF16), jax.ShapeDtypeStruct((share, width), F32)]
+        + [jax.ShapeDtypeStruct((share, width), BF16)] * (parts - 1)
+        + [pltpu.VMEM((rows.stop - rows.start, sources[n].shape[1]), BF16) for n, rows in further],
+        in_specs=[VMEM] * (len(peers) + 2) + [hbm, VMEM] + [hbm] * len(sources),
+        out_specs=[VMEM] * (1 + parts + len(further)),
+        scratch_shapes=[
+            pltpu.VMEM((rows, width), BF16),
+            pltpu.VMEM((rows, units), BF16),
+            pltpu.VMEM((width, units), BF16),
+            pltpu.SemaphoreType.DMA((1, 4)),
+            pltpu.SemaphoreType.DMA((len(further), 1)),
+        ],
+        compiler_params=pltpu.CompilerParams(vmem_limit_bytes=20 * MIB),
+        cost_estimate=CHEAP,
+        name="first_step",
+    )(
+        own,
+        *peers,
+        w_down,
+        pltpu.with_memory_space_constraint(w_up, pltpu.HBM),
+        gates,
+        *[pltpu.with_memory_space_constraint(a, pltpu.HBM) for a in sources],
+    )
+    return outs[0], outs[1], outs[2 : parts + 1], outs[parts + 1 :]
+
+
+def section_step(layer, own, peers, w_down, turned, gates, after=()):
     share, width = own.shape
     units = w_down.shape[1]
     pieces = len(peers)
     parts = lax.axis_size("tensor")
     rows = share * parts
-    first = w_up is not None
-    out_shape = [jax.ShapeDtypeStruct((share, width), F32)]
-    out_shape += [jax.ShapeDtypeStruct((share, width), BF16)] * (parts - 1)
-    scratch = [pltpu.VMEM((rows, width), BF16), pltpu.VMEM((rows, units), BF16)]
-    in_specs = [VMEM] * (pieces + 4) + [pl.BlockSpec(memory_space=pl.ANY)] * len(after)
-    body = functools.partial(first_kernel if first else step_kernel, layer, parts, pieces)
 
     def kernel(*refs):
-        body(*refs[: pieces + 4], *refs[pieces + 4 + len(after) :])
-
-    if first:
-        out_shape = [pltpu.VMEM((units, width), BF16)] + out_shape
-        scratch += [pltpu.VMEM((width, units), BF16), pltpu.SemaphoreType.DMA((1, 4))]
-        in_specs[pieces + 2] = pl.BlockSpec(memory_space=pltpu.HBM)
-        operand = pltpu.with_memory_space_constraint(w_up, pltpu.HBM)
-    else:
-        operand = turned
-    outs = pl.pallas_call(
+        step_kernel(layer, parts, pieces, *refs[: pieces + 4], *refs[pieces + 4 + len(after) :])
+
+    return pl.pallas_call(
         kernel,
-        out_shape=out_shape,
-        in_specs=in_specs,
-        out_specs=[VMEM] * len(out_shape),
-        scratch_shapes=scratch,
-        compiler_params=pltpu.CompilerParams(vmem_limit_bytes=(20 if first else 12) * MIB),
+        out_shape=[jax.ShapeDtypeStruct((share, width), F32)]
+        + [jax.ShapeDtypeStruct((share, width), BF16)] * (parts - 1),
+        in_specs=[VMEM] * (pieces + 4) + [pl.BlockSpec(memory_space=pl.ANY)] * len(after),
+        out_specs=[VMEM] * parts,
+        scratch_shapes=[pltpu.VMEM((rows, width), BF16), pltpu.VMEM((rows, units), BF16)],
+        compiler_params=pltpu.CompilerParams(vmem_limit_bytes=12 * MIB),
         cost_estimate=CHEAP,
         name="section_step",
-    )(own, *peers, w_down, operand, gates, *after)
-    return outs
+    )(own, *peers, w_down, turned, gates, *after)
 
 
 def pack_block(source, k, target, at):
@@ -444,7 +470,7 @@
     rows, units = moment_one.shape
     tokens = hidden_all.shape[0]
     tile = tile_of(rows, 128)
-    part_rows = tile_of(tile, 32)
+    part_rows = tile_of(tile, 64)
     return pl.pallas_call(
         functools.partial(adam_kernel, (owners, parts, blocks[0].shape[0] // owners, tile, part_rows)),
         out_shape=[jax.ShapeDtypeStruct((rows, units), F32)] * 3,
@@ -542,9 +568,7 @@
     share = loss_grad.shape[0]
     saved = hidden[0]
     half = saved.shape[0] // 2
-    w_down, gates, rows_in, loss, *halves = stage(
-        [down_weight[0], gate_act[0], block_input[0], loss_grad], [saved] if planned else []
-    )
+    w_down, gates, loss = stage([down_weight[0], gate_act[0], loss_grad])
     turned = None
     upstreams = [loss]
     grads = []
@@ -556,7 +580,16 @@
         else:
             peers = from_peers(upstream if grads else loss_grad, "tensor")
         if not grads:
-            turned, kept, *sent = section_step(layer, upstream, peers, w_down, None, gates, up_weight[0])
+            turned, kept, sent, (rows_in, *halves) = first_step(
+                layer,
+                upstream,
+                peers,
+                w_down,
+                up_weight[0],
+                gates,
+                [block_input[0]],
+                [saved] if planned else [],
+            )
         elif planned and len(grads) == 2:
             unit_grad = unit_step(layer, upstream, peers, w_down, gates)
             kept, *sent = width_step(layer, unit_grad, turned, loss_grad.shape[0], late)

time: 67.8 us -> 67.5 us (level)
  no operation moved by 1% of the time
where the time goes in v4:
time: 67.5 us; the launch traced here: 67.3 us
  waiting for transfers between devices  28.8 us (43%)
  Pallas kernels  20.9 us (31%)
  starting transfers between devices  14.4 us (21%)
  blocking collectives  2.17 us (3%)
  between operations  0.96 us (1%)
    ppermute x4, waiting for transfers between devices, on_device(): lax.ppermute(piece, 'dp', [(i, i ^ k) for i in range(owners)])  15.1 us
    ppermute x3, waiting for transfers between devices, on_device(): upstreams.append(lax.ppermute(grad, 'pipe', [(layer, layer - 1)]))  6.39 us
    ppermute x4, starting transfers between devices, on_device(): lax.ppermute(piece, 'dp', [(i, i ^ k) for i in range(owners)])  6.34 us
    pallas_call x1, Pallas kernels, adam_step(): pl.pallas_call(functools.partial(adam_kernel, (owners, parts, blocks[0].s...  5.67 us
    ppermute x4, waiting for transfers between devices, to_peers(): lax.ppermute(value, axis, [(i, (i + k) % size) for i in range(size)])  5.05 us
    pallas_call x1, Pallas kernels, first_step(): pl.pallas_call(functools.partial(first_kernel, layer, parts, len(peers),...  4.34 us
    ppermute x3, starting transfers between devices, on_device(): lax.ppermute(cut, ('pipe', 'dp'), [(s * owners + i, (s - 1) * owners + (i...  3.88 us
    pallas_call x1, Pallas kernels, stage(): pl.pallas_call(kernel, out_shape=[pltpu.VMEM(a.shape, a.dtype) for a in a...  3.6 us
  transfers between devices with their start and end apart: 19, of which 11 were waited for; matrix products, arithmetic and copies ran while one was open for 0% of the time, Pallas kernels for 16%

profile of v4, /device:TPU:0, one launch (start us, length us, event | category | flops | bytes accessed | tf_op | source)
XLA Modules:
  0.0 67.3 jit_solution(524363926774720561)
XLA Ops:
  0.6 0.5 collective-permute-start
  1.1 3.6 %stage.1 = (bf16[2048,2048]{1,0:T(8,128)(2,1)S(1)}, bf16[128,2048]{1,0:T(8,128)(2,1)S(1)}, bf16[64,2048]{1,0:T(8,128)(2,1)S(1)}) custom-call(bf16[2048,2048]{1,0:T(8,128)(2,1)} %bitcast.15, bf16[128,2048]{1,0:T(8,128)(2,1)} %bitcast.17, bf16[64,2048]{1,0:T(8,128)(2,1)} %refs_2_.1), custom_call_target="tpu_custom_call" | custom-call | bytes 18350080 | tf_op jit(solution)/shard_map/stage/pallas_call | solution.py:55
  4.8 0.0 collective-permute-done.refs_0_
  4.8 0.0 copy-start
  4.8 4.3 %first_step.1 = (bf16[2048,2048]{1,0:T(8,128)(2,1)S(1)}, f32[64,2048]{1,0:T(8,128)S(1)}, bf16[64,2048]{1,0:T(8,128)(2,1)S(1)}, bf16[64,2048]{1,0:T(8,128)(2,1)S(...) custom-call(bf16[64,2048]{1,0:T(8,128)(2,1)S(1)} %get-tuple-element.37.own_ref.refs_1_.refs_4_.refs_6_.refs_7_.refs_0_, ...), custom_call_target="tpu_custom_call" | custom-call | tf_op jit(solution)/shard_map/first_step/pallas_call | solution.py:240
  9.1 0.1 collective-permute-start.1
  9.2 1.5 %collective-permute-done.1.refs_0_ = bf16[64,2048]{1,0:T(8,128)(2,1)S(1)} collective-permute-done((bf16[64,2048]{1,0:T(8,128)(2,1)S(1)}, bf16[64,2048]{1,0:T(8,128)(2,1)S(1)}, u32[]{:S(2)}, u32[]{:S(2)}) %collective-permute-start.1) | collective-permute-done | bytes 262176 | tf_op jit(solution)/shard_map/ppermute | solution.py:546
  10.7 0.0 copy-done
  10.8 0.7 %collective-permute-start.2 = (bf16[64,2048]{1,0:T(8,128)(2,1)S(1)}, bf16[64,2048]{1,0:T(8,128)(2,1)S(1)}, u32[]{:S(2)}, u32[]{:S(2)}) collective-permute-start(bf16[64,2048]{1,0:T(8,128)(2,1)S(1)} %get-tuple-element.45.refs_2_.refs_4_), channel_id=1, source_target_pairs={{24,16},{25,17},{26,18},{27,19},{28,20},{29,21},{30,22},{31,23}} | collective-permute-start | bytes 786440 | tf_op jit(solution)/shard_map/ppermute | solution.py:638
  11.5 2.7 %collective-permute-start.4 = (bf16[80,2048]{1,0:T(8,128)(2,1)S(1)}, bf16[80,2048]{1,0:T(8,128)(2,1)S(1)}, u32[]{:S(2)}, u32[]{:S(2)}) collective-permute-start(bf16[80,2048]{1,0:T(8,128)(2,1)S(1)} %get-tuple-element.47), channel_id=1, source_target_pairs={{0,2},{2,0},{4,6},{6,4},{1,3},{3,1},{5,7},{7,5},{8,10},{10,8},{12,... | collective-permute-start | bytes 983048 | tf_op jit(solution)/shard_map/ppermute | solution.py:655
  14.2 1.5 %collective-permute-start.5 = (bf16[80,2048]{1,0:T(8,128)(2,1)S(1)}, bf16[80,2048]{1,0:T(8,128)(2,1)S(1)}, u32[]{:S(2)}, u32[]{:S(2)}) collective-permute-start(bf16[80,2048]{1,0:T(8,128)(2,1)S(1)} %get-tuple-element.48), channel_id=1, source_target_pairs={{0,4},{2,6},{4,0},{6,2},{1,5},{3,7},{5,1},{7,3},{8,12},{10,14},{12... | collective-permute-start | bytes 983048 | tf_op jit(solution)/shard_map/ppermute | solution.py:655
  15.7 0.0 collective-permute-done.2.refs_0_.refs_1_
  15.7 0.0 collective-permute-start.3
  15.7 3.5 %stage_in_section.2 = (f32[512,2048]{1,0:T(8,128)S(1)}, f32[512,2048]{1,0:T(8,128)S(1)}) custom-call(f32[512,2048]{1,0:T(8,128)} %bitcast.11, f32[512,2048]{1,0:T(8,128)} %bitcast.13, bf16[64,2048]{1,0:T(8,128)(2,1)S(1)} %get-tuple-element.45.refs_2_.refs_4_), custom_call_target="tpu_custom_call" | custom-call | tf_op jit(solution)/shard_map/stage_in_section/pallas_call | solution.py:81
  19.2 3.2 %collective-permute-done.4.refs_5_.refs_8_.refs_2_.refs_7_ = bf16[80,2048]{1,0:T(8,128)(2,1)S(1)} collective-permute-done((bf16[80,2048]{1,0:T(8,128)(2,1)S(1)}, bf16[80,2048]{1,0:T(8,128)(2,1)S(1)}, u32[]{:S(2)}, u32[]{:S(2)}) %collective-permute-start.4) | collective-permute-done | bytes 327712 | tf_op jit(solution)/shard_map/ppermute | solution.py:655
  22.4 1.5 %collective-permute-done.5.refs_6_.refs_5_.refs_8_ = bf16[80,2048]{1,0:T(8,128)(2,1)S(1)} collective-permute-done((bf16[80,2048]{1,0:T(8,128)(2,1)S(1)}, bf16[80,2048]{1,0:T(8,128)(2,1)S(1)}, u32[]{:S(2)}, u32[]{:S(2)}) %collective-permute-start.5) | collective-permute-done | bytes 327712 | tf_op jit(solution)/shard_map/ppermute | solution.py:655
  23.9 0.0 collective-permute-done.3.refs_1_
  23.9 0.0 collective-permute-start.6
  23.9 1.5 %collective-permute-done.6.refs_0_ = bf16[64,2048]{1,0:T(8,128)(2,1)S(1)} collective-permute-done((bf16[64,2048]{1,0:T(8,128)(2,1)S(1)}, bf16[64,2048]{1,0:T(8,128)(2,1)S(1)}, u32[]{:S(2)}, u32[]{:S(2)}) %collective-permute-start.6) | collective-permute-done | bytes 262176 | tf_op jit(solution)/shard_map/ppermute | solution.py:546
  25.4 0.1 norm_step.5
  25.5 0.7 %collective-permute-start.7 = (bf16[64,2048]{1,0:T(8,128)(2,1)S(1)}, bf16[64,2048]{1,0:T(8,128)(2,1)S(1)}, u32[]{:S(2)}, u32[]{:S(2)}) collective-permute-start(bf16[64,2048]{1,0:T(8,128)(2,1)S(1)} %get-tuple-element.53.refs_4_.refs_5_), channel_id=1, source_target_pairs={{16,8},{17,9},{18,10},{19,11},{20,12},{21,13},{22,14},{23,15}} | collective-permute-start | bytes 786440 | tf_op jit(solution)/shard_map/ppermute | solution.py:638
  26.2 0.4 collective-permute-start.9
  26.6 1.7 %collective-permute-start.10 = (bf16[128,2048]{1,0:T(8,128)(2,1)S(1)}, bf16[128,2048]{1,0:T(8,128)(2,1)S(1)}, u32[]{:S(2)}, u32[]{:S(2)}) collective-permute-start(bf16[128,2048]{1,0:T(8,128)(2,1)S(1)} %get-tuple-element.55), channel_id=1, source_target_pairs={{0,4},{2,6},{4,0},{6,2},{1,5},{3,7},{5,1},{7,3},{8,12},{10,14},{12... | collective-permute-start | bytes 1572872 | tf_op jit(solution)/shard_map/ppermute | solution.py:655
  28.3 0.0 collective-permute-done.7.own_ref.refs_1_.refs_2_
  28.3 0.0 collective-permute-start.8
  28.3 1.5 %collective-permute-done.8.refs_0_ = bf16[64,2048]{1,0:T(8,128)(2,1)S(1)} collective-permute-done((bf16[64,2048]{1,0:T(8,128)(2,1)S(1)}, bf16[64,2048]{1,0:T(8,128)(2,1)S(1)}, u32[]{:S(2)}, u32[]{:S(2)}) %collective-permute-start.8) | collective-permute-done | bytes 262176 | tf_op jit(solution)/shard_map/ppermute | solution.py:540
  29.8 10.4 %collective-permute-done.9.refs_0_.refs_3_.refs_7_ = bf16[128,2048]{1,0:T(8,128)(2,1)S(1)} collective-permute-done((bf16[128,2048]{1,0:T(8,128)(2,1)S(1)}, bf16[128,2048]{1,0:T(8,128)(2,1)S(1)}, u32[]{:S(2)}, u32[]{:S(2)}) %collective-permute-start.9) | collective-permute-done | bytes 524320 | tf_op jit(solution)/shard_map/ppermute | solution.py:655
  40.2 0.1 collective-permute-done.10.refs_1_.refs_4_.refs_6_
  40.3 0.0 collective-permute-start.11
  40.3 1.5 %collective-permute-done.11.refs_0_ = bf16[64,2048]{1,0:T(8,128)(2,1)S(1)} collective-permute-done((bf16[64,2048]{1,0:T(8,128)(2,1)S(1)}, bf16[64,2048]{1,0:T(8,128)(2,1)S(1)}, u32[]{:S(2)}, u32[]{:S(2)}) %collective-permute-start.11) | collective-permute-done | bytes 262176 | tf_op jit(solution)/shard_map/ppermute | solution.py:546
  41.8 1.3 %collective-permute-start.12 = (bf16[64,2048]{1,0:T(8,128)(2,1)S(1)}, bf16[64,2048]{1,0:T(8,128)(2,1)S(1)}, u32[]{:S(2)}, u32[]{:S(2)}) collective-permute-start(bf16[64,2048]{1,0:T(8,128)(2,1)S(1)} %get-tuple-element.60.refs_6_), channel_id=1, source_target_pairs={{8,0},{9,1},{10,2},{11,3},{12,4},{13,5},{14,6},{15,7}} | collective-permute-start | bytes 786440 | tf_op jit(solution)/shard_map/ppermute | solution.py:638
  43.1 0.7 collective-permute-start.17
  43.8 0.2 stack.1.refs_11_.refs_2_
  44.0 1.3 %collective-permute-start.14 = (bf16[64,512]{1,0:T(8,128)(2,1)S(1)}, bf16[64,512]{1,0:T(8,128)(2,1)S(1)}, u32[]{:S(2)}, u32[]{:S(2)}) collective-permute-start(bf16[64,512]{1,0:T(8,128)(2,1)S(1)} %get-tuple-element.63), channel_id=1, source_target_pairs={{8,2},{10,0},{12,6},{14,4},{16,10},{18,8},{20,14},{22,12},{24,18},... | collective-permute-start | bytes 196616 | tf_op jit(solution)/shard_map/ppermute | solution.py:642
  45.3 1.3 %collective-permute-start.15 = (bf16[64,512]{1,0:T(8,128)(2,1)S(1)}, bf16[64,512]{1,0:T(8,128)(2,1)S(1)}, u32[]{:S(2)}, u32[]{:S(2)}) collective-permute-start(bf16[64,512]{1,0:T(8,128)(2,1)S(1)} %get-tuple-element.64), channel_id=1, source_target_pairs={{8,4},{10,6},{12,0},{14,2},{16,12},{18,14},{20,8},{22,10},{24,20},... | collective-permute-start | bytes 196616 | tf_op jit(solution)/shard_map/ppermute | solution.py:642
  46.6 1.3 %collective-permute-start.16 = (bf16[64,512]{1,0:T(8,128)(2,1)S(1)}, bf16[64,512]{1,0:T(8,128)(2,1)S(1)}, u32[]{:S(2)}, u32[]{:S(2)}) collective-permute-start(bf16[64,512]{1,0:T(8,128)(2,1)S(1)} %get-tuple-element.65), channel_id=1, source_target_pairs={{8,6},{10,4},{12,2},{14,0},{16,14},{18,12},{20,10},{22,8},{24,22},... | collective-permute-start | bytes 196616 | tf_op jit(solution)/shard_map/ppermute | solution.py:642
  47.9 6.4 %collective-permute-done.12.refs_0_.refs_1_.refs_3_ = bf16[64,2048]{1,0:T(8,128)(2,1)S(1)} collective-permute-done((bf16[64,2048]{1,0:T(8,128)(2,1)S(1)}, bf16[64,2048]{1,0:T(8,128)(2,1)S(1)}, u32[]{:S(2)}, u32[]{:S(2)}) %collective-permute-start.12) | collective-permute-done | bytes 262176 | tf_op jit(solution)/shard_map/ppermute | solution.py:638
  54.3 2.2 %all_gather.3.refs_1_ = bf16[128,2048]{1,0:T(8,128)(2,1)S(1)} all-gather(bf16[64,2048]{1,0:T(8,128)(2,1)S(1)} %collective-permute-done.12.refs_0_.refs_1_.refs_3_), channel_id=1, replica_groups=mesh['pipe'=4,'dp'=4,'tensor'=2] {'tensor'}, dimensions={0}, use_global_device_ids=true | all-gather | bytes 786432 | tf_op jit(solution)/shard_map/all_gather | solution.py:579
  56.5 2.4 %section_step.3 = (f32[64,2048]{1,0:T(8,128)S(1)}, bf16[64,2048]{1,0:T(8,128)(2,1)S(1)}) custom-call(bf16[64,2048]{1,0:T(8,128)(2,1)S(1)} %collective-permute-done.12.refs_0_.refs_1_.refs_3_, bf16[128,2048]{1,0:T(8,128)(2,1)S(1)} %all_gather.3.refs_1_, bf16[2048,2048]{1,0:T(8,128)(2,1)S(1)} %get-tuple-element.38.refs_1_.refs_2_.refs_3_, ...), custom_call_target="tpu_custom_call" | custom-call | tf_op jit(solution)/shard_map/section_step/pallas_call | solution.py:278
  58.8 0.2 collective-permute-start.13
  59.0 0.0 collective-permute-done.17.refs_9_
  59.1 0.0 collective-permute-done.14.refs_4_
  59.1 0.0 collective-permute-done.15.refs_5_
  59.1 0.8 %collective-permute-done.16.refs_6_ = bf16[64,512]{1,0:T(8,128)(2,1)S(1)} collective-permute-done((bf16[64,512]{1,0:T(8,128)(2,1)S(1)}, bf16[64,512]{1,0:T(8,128)(2,1)S(1)}, u32[]{:S(2)}, u32[]{:S(2)}) %collective-permute-start.16) | collective-permute-done | bytes 65568 | tf_op jit(solution)/shard_map/ppermute | solution.py:642
  59.9 0.1 collective-permute-start.18
  59.9 0.5 collective-permute-done.13.refs_0_
  60.4 1.0 %norm_step.7 = bf16[64,2048]{1,0:T(8,128)(2,1)} custom-call(f32[64,2048]{1,0:T(8,128)S(1)} %get-tuple-element.61.kept_ref.refs_10_, bf16[64,2048]{1,0:T(8,128)(2,1)S(1)} %collective-permute-done.13.refs_0_, bf16[64,2048]{1,0:T(8,128)(2,1)S(1)} %collective-permute-done.12.refs_0_.refs_1_.refs_3_, bf16[64,2048]{1,0:T(8,128)(2,1)S(1)} %get-tuple-element.42.refs_2_, ...), custom_call_target="tpu_custom_call" | custom-call | tf_op jit(solution)/shard_map/norm_step/pallas_call | solution.py:367
  61.5 0.0 collective-permute-done.18.refs_1_
  61.5 5.7 %adam_step.1 = (f32[512,2048]{1,0:T(8,128)}, f32[512,2048]{1,0:T(8,128)}, f32[512,2048]{1,0:T(8,128)}) custom-call(bf16[256,512]{1,0:T(8,128)(2,1)S(1)} %collect.1.refs_0_, bf16[256,512]{1,0:T(8,128)(2,1)S(1)} %collective-permute-done.18.refs_1_, bf16[512,2048]{1,0:T(8,128)(2,1)S(1)} %stack.1.refs_11_.refs_2_, ...), custom_call_target="tpu_custom_call" | custom-call | tf_op jit(solution)/shard_map/adam_step/pallas_call | solution.py:474
  (7 shorter events, 0.1 us)
Async XLA Ops:
  0.6 4.1 %collective-permute-start = (bf16[64,2048]{1,0:T(8,128)(2,1)}, bf16[64,2048]{1,0:T(8,128)(2,1)S(1)}, u32[]{:S(2)}, u32[]{:S(2)}) collective-permute-start(bf16[64,2048]{1,0:T(8,128)(2,1)} %refs_2_.1), channel_id=1, source_target_pairs={{1,0},{0,1},{3,2},{2,3},{5,4},{4,5},{7,6},{6,7},{9,8},{8,9},{11,10... | collective-permute-start | bytes 786440 | tf_op jit(solution)/shard_map/ppermute | solution.py:540
  4.8 6.0 %copy-start = (f32[1,2048]{1,0:T(1,128)S(1)}, f32[1,2048]{1,0:T(1,128)}, u32[]{:S(2)}) copy-start(f32[1,2048]{1,0:T(1,128)} %refs_3_.7) | copy-start | bytes 24580
  9.1 1.6 %collective-permute-start.1 = (bf16[64,2048]{1,0:T(8,128)(2,1)S(1)}, bf16[64,2048]{1,0:T(8,128)(2,1)S(1)}, u32[]{:S(2)}, u32[]{:S(2)}) collective-permute-start(bf16[64,2048]{1,0:T(8,128)(2,1)S(1)} %get-tuple-element.41), channel_id=1, source_target_pairs={{0,1},{1,0},{2,3},{3,2},{4,5},{5,4},{6,7},{7,6},{8,9},{9,8},{10,11... | collective-permute-start | bytes 786440 | tf_op jit(solution)/shard_map/ppermute | solution.py:546
  10.8 4.9 %collective-permute-start.2 = (bf16[64,2048]{1,0:T(8,128)(2,1)S(1)}, bf16[64,2048]{1,0:T(8,128)(2,1)S(1)}, u32[]{:S(2)}, u32[]{:S(2)}) collective-permute-start(bf16[64,2048]{1,0:T(8,128)(2,1)S(1)} %get-tuple-element.45.refs_2_.refs_4_), channel_id=1, source_target_pairs={{24,16},{25,17},{26,18},{27,19},{28,20},{29,21},{30,22},{31,23}} | collective-permute-start | bytes 786440 | tf_op jit(solution)/shard_map/ppermute | solution.py:638
  11.5 10.9 %collective-permute-start.4 = (bf16[80,2048]{1,0:T(8,128)(2,1)S(1)}, bf16[80,2048]{1,0:T(8,128)(2,1)S(1)}, u32[]{:S(2)}, u32[]{:S(2)}) collective-permute-start(bf16[80,2048]{1,0:T(8,128)(2,1)S(1)} %get-tuple-element.47), channel_id=1, source_target_pairs={{0,2},{2,0},{4,6},{6,4},{1,3},{3,1},{5,7},{7,5},{8,10},{10,8},{12,... | collective-permute-start | bytes 983048 | tf_op jit(solution)/shard_map/ppermute | solution.py:655
  14.2 9.7 %collective-permute-start.5 = (bf16[80,2048]{1,0:T(8,128)(2,1)S(1)}, bf16[80,2048]{1,0:T(8,128)(2,1)S(1)}, u32[]{:S(2)}, u32[]{:S(2)}) collective-permute-start(bf16[80,2048]{1,0:T(8,128)(2,1)S(1)} %get-tuple-element.48), channel_id=1, source_target_pairs={{0,4},{2,6},{4,0},{6,2},{1,5},{3,7},{5,1},{7,3},{8,12},{10,14},{12... | collective-permute-start | bytes 983048 | tf_op jit(solution)/shard_map/ppermute | solution.py:655
  15.7 8.2 %collective-permute-start.3 = (bf16[64,2048]{1,0:T(8,128)(2,1)S(1)}, bf16[64,2048]{1,0:T(8,128)(2,1)S(1)}, u32[]{:S(2)}, u32[]{:S(2)}) collective-permute-start(bf16[64,2048]{1,0:T(8,128)(2,1)S(1)} %collective-permute-done.2.refs_0_.refs_1_), channel_id=1, source_target_pairs={{1,0},{0,1},{3,2},{2,3},{5,4},{4,5},{7,6},{6,7},{9,8},{8,9},{11,10... | collective-permute-start | bytes 786440 | tf_op jit(solution)/shard_map/ppermute | solution.py:540
  23.9 1.5 %collective-permute-start.6 = (bf16[64,2048]{1,0:T(8,128)(2,1)S(1)}, bf16[64,2048]{1,0:T(8,128)(2,1)S(1)}, u32[]{:S(2)}, u32[]{:S(2)}) collective-permute-start(bf16[64,2048]{1,0:T(8,128)(2,1)S(1)} %get-tuple-element.52), channel_id=1, source_target_pairs={{0,1},{1,0},{2,3},{3,2},{4,5},{5,4},{6,7},{7,6},{8,9},{9,8},{10,11... | collective-permute-start | bytes 786440 | tf_op jit(solution)/shard_map/ppermute | solution.py:546
  25.5 2.8 %collective-permute-start.7 = (bf16[64,2048]{1,0:T(8,128)(2,1)S(1)}, bf16[64,2048]{1,0:T(8,128)(2,1)S(1)}, u32[]{:S(2)}, u32[]{:S(2)}) collective-permute-start(bf16[64,2048]{1,0:T(8,128)(2,1)S(1)} %get-tuple-element.53.refs_4_.refs_5_), channel_id=1, source_target_pairs={{16,8},{17,9},{18,10},{19,11},{20,12},{21,13},{22,14},{23,15}} | collective-permute-start | bytes 786440 | tf_op jit(solution)/shard_map/ppermute | solution.py:638
  26.2 14.0 %collective-permute-start.9 = (bf16[128,2048]{1,0:T(8,128)(2,1)S(1)}, bf16[128,2048]{1,0:T(8,128)(2,1)S(1)}, u32[]{:S(2)}, u32[]{:S(2)}) collective-permute-start(bf16[128,2048]{1,0:T(8,128)(2,1)S(1)} %get-tuple-element.54), channel_id=1, source_target_pairs={{0,2},{2,0},{4,6},{6,4},{1,3},{3,1},{5,7},{7,5},{8,10},{10,8},{12,... | collective-permute-start | bytes 1572872 | tf_op jit(solution)/shard_map/ppermute | solution.py:655
  26.6 13.7 %collective-permute-start.10 = (bf16[128,2048]{1,0:T(8,128)(2,1)S(1)}, bf16[128,2048]{1,0:T(8,128)(2,1)S(1)}, u32[]{:S(2)}, u32[]{:S(2)}) collective-permute-start(bf16[128,2048]{1,0:T(8,128)(2,1)S(1)} %get-tuple-element.55), channel_id=1, source_target_pairs={{0,4},{2,6},{4,0},{6,2},{1,5},{3,7},{5,1},{7,3},{8,12},{10,14},{12... | collective-permute-start | bytes 1572872 | tf_op jit(solution)/shard_map/ppermute | solution.py:655
  28.3 1.5 %collective-permute-start.8 = (bf16[64,2048]{1,0:T(8,128)(2,1)S(1)}, bf16[64,2048]{1,0:T(8,128)(2,1)S(1)}, u32[]{:S(2)}, u32[]{:S(2)}) collective-permute-start(bf16[64,2048]{1,0:T(8,128)(2,1)S(1)} %collective-permute-done.7.own_ref.refs_1_.refs_2_), channel_id=1, source_target_pairs={{1,0},{0,1},{3,2},{2,3},{5,4},{4,5},{7,6},{6,7},{9,8},{8,9},{11,10... | collective-permute-start | bytes 786440 | tf_op jit(solution)/shard_map/ppermute | solution.py:540
  40.3 1.5 %collective-permute-start.11 = (bf16[64,2048]{1,0:T(8,128)(2,1)S(1)}, bf16[64,2048]{1,0:T(8,128)(2,1)S(1)}, u32[]{:S(2)}, u32[]{:S(2)}) collective-permute-start(bf16[64,2048]{1,0:T(8,128)(2,1)S(1)} %get-tuple-element.59), channel_id=1, source_target_pairs={{0,1},{1,0},{2,3},{3,2},{4,5},{5,4},{6,7},{7,6},{8,9},{9,8},{10,11... | collective-permute-start | bytes 786440 | tf_op jit(solution)/shard_map/ppermute | solution.py:546
  41.8 12.5 %collective-permute-start.12 = (bf16[64,2048]{1,0:T(8,128)(2,1)S(1)}, bf16[64,2048]{1,0:T(8,128)(2,1)S(1)}, u32[]{:S(2)}, u32[]{:S(2)}) collective-permute-start(bf16[64,2048]{1,0:T(8,128)(2,1)S(1)} %get-tuple-element.60.refs_6_), channel_id=1, source_target_pairs={{8,0},{9,1},{10,2},{11,3},{12,4},{13,5},{14,6},{15,7}} | collective-permute-start | bytes 786440 | tf_op jit(solution)/shard_map/ppermute | solution.py:638
  43.1 15.9 %collective-permute-start.17 = (bf16[16,2048]{1,0:T(8,128)(2,1)S(1)}, bf16[16,2048]{1,0:T(8,128)(2,1)S(1)}, u32[]{:S(2)}, u32[]{:S(2)}) collective-permute-start(bf16[16,2048]{1,0:T(8,128)(2,1)S(1)} %get-tuple-element.66), channel_id=1, source_target_pairs={{24,30},{26,28},{28,26},{30,24},{25,31},{27,29},{29,27},{31,25}} | collective-permute-start | bytes 196616 | tf_op jit(solution)/shard_map/ppermute | solution.py:667
  44.0 15.0 %collective-permute-start.14 = (bf16[64,512]{1,0:T(8,128)(2,1)S(1)}, bf16[64,512]{1,0:T(8,128)(2,1)S(1)}, u32[]{:S(2)}, u32[]{:S(2)}) collective-permute-start(bf16[64,512]{1,0:T(8,128)(2,1)S(1)} %get-tuple-element.63), channel_id=1, source_target_pairs={{8,2},{10,0},{12,6},{14,4},{16,10},{18,8},{20,14},{22,12},{24,18},... | collective-permute-start | bytes 196616 | tf_op jit(solution)/shard_map/ppermute | solution.py:642
  45.3 13.7 %collective-permute-start.15 = (bf16[64,512]{1,0:T(8,128)(2,1)S(1)}, bf16[64,512]{1,0:T(8,128)(2,1)S(1)}, u32[]{:S(2)}, u32[]{:S(2)}) collective-permute-start(bf16[64,512]{1,0:T(8,128)(2,1)S(1)} %get-tuple-element.64), channel_id=1, source_target_pairs={{8,4},{10,6},{12,0},{14,2},{16,12},{18,14},{20,8},{22,10},{24,20},... | collective-permute-start | bytes 196616 | tf_op jit(solution)/shard_map/ppermute | solution.py:642
  46.6 13.2 %collective-permute-start.16 = (bf16[64,512]{1,0:T(8,128)(2,1)S(1)}, bf16[64,512]{1,0:T(8,128)(2,1)S(1)}, u32[]{:S(2)}, u32[]{:S(2)}) collective-permute-start(bf16[64,512]{1,0:T(8,128)(2,1)S(1)} %get-tuple-element.65), channel_id=1, source_target_pairs={{8,6},{10,4},{12,2},{14,0},{16,14},{18,12},{20,10},{22,8},{24,22},... | collective-permute-start | bytes 196616 | tf_op jit(solution)/shard_map/ppermute | solution.py:642
  58.8 1.6 %collective-permute-start.13 = (bf16[64,2048]{1,0:T(8,128)(2,1)S(1)}, bf16[64,2048]{1,0:T(8,128)(2,1)S(1)}, u32[]{:S(2)}, u32[]{:S(2)}) collective-permute-start(bf16[64,2048]{1,0:T(8,128)(2,1)S(1)} %get-tuple-element.62), channel_id=1, source_target_pairs={{0,1},{1,0},{2,3},{3,2},{4,5},{5,4},{6,7},{7,6},{8,9},{9,8},{10,11... | collective-permute-start | bytes 786440 | tf_op jit(solution)/shard_map/ppermute | solution.py:546
  59.9 1.6 %collective-permute-start.18 = (bf16[256,512]{1,0:T(8,128)(2,1)S(1)}, bf16[256,512]{1,0:T(8,128)(2,1)S(1)}, u32[]{:S(2)}, u32[]{:S(2)}) collective-permute-start(bf16[256,512]{1,0:T(8,128)(2,1)S(1)} %collect.1.refs_0_), channel_id=1, source_target_pairs={{1,0},{0,1},{3,2},{2,3},{5,4},{4,5},{7,6},{6,7},{9,8},{8,9},{11,10... | collective-permute-start | bytes 786440 | tf_op jit(solution)/shard_map/ppermute | solution.py:540

commit v5 on v4

--- a/solution.py
+++ b/solution.py
@@ -202,25 +202,31 @@
     behind = copies(pairs, further_sem, 1)
     starts = lax.axis_index("pipe") == layer
 
+    def turn(first, count):
+        for c in range(first, first + count):
+            arriving[c].wait()
+        cols = slice(first * size, (first + count) * size)
+        turned_ref[:, cols] = held_ref[cols, :].T
+
+    def product(first, count):
+        cols = slice(first * size, (first + count) * size)
+        term = jnp.dot(unit_ref[...], turned_ref[:, cols], preferred_element_type=F32)
+        hand_out(share, term, cols, kept_ref, sent_refs)
+
     @pl.when(starts)
     def _():
         fill_rows(share, rows_ref, own_ref, peer_refs)
         unit_grads(parts, share, rows_ref, down_ref, gate_ref, unit_ref)
-
-    for c in range(chunks):
-        cols = slice(c * size, (c + 1) * size)
-        arriving[c].wait()
-
-        @pl.when(starts)
-        def _(cols=cols):
-            term = lax.dot_general(
-                unit_ref[...], held_ref[cols, :], (((1,), (1,)), ((), ())), preferred_element_type=F32
-            )
-            hand_out(share, term, cols, kept_ref, sent_refs)
-
-        @pl.when(jnp.logical_not(starts))
-        def _(cols=cols):
-            turned_ref[:, cols] = held_ref[cols, :].T
+        turn(0, 2)
+        for c in range(2, chunks, 2):
+            turn(c, 2)
+            product(c - 2, 2)
+        product(chunks - 2, 2)
+
+    @pl.when(jnp.logical_not(starts))
+    def _():
+        for c in range(chunks):
+            turn(c, 1)
 
     for (copy,) in behind:
         copy.wait()
@@ -248,7 +254,7 @@
             pltpu.VMEM((rows, width), BF16),
             pltpu.VMEM((rows, units), BF16),
             pltpu.VMEM((width, units), BF16),
-            pltpu.SemaphoreType.DMA((1, 4)),
+            pltpu.SemaphoreType.DMA((1, 8)),
             pltpu.SemaphoreType.DMA((len(further), 1)),
         ],
         compiler_params=pltpu.CompilerParams(vmem_limit_bytes=20 * MIB),
@@ -590,7 +596,7 @@
                 [block_input[0]],
                 [saved] if planned else [],
             )
-        elif planned and len(grads) == 2:
+        elif planned and layer:
             unit_grad = unit_step(layer, upstream, peers, w_down, gates)
             kept, *sent = width_step(layer, unit_grad, turned, loss_grad.shape[0], late)
         else:

time: 67.5 us -> 67.3 us (level)
    pallas_call x2 -> x1, Pallas kernels: 2.36 us -> 2.36 us  [section_step(): pl.pallas_call(kernel, out_shape=[jax.ShapeDtypeStruct((share, width), F3...]
  transfers between devices with their start and end apart: 19 -> 19, of which waited for: 11 -> 12; matrix products, arithmetic and copies ran while one was open for 0% -> 0% of each run, Pallas kernels for 16% -> 16%
where the time goes in v5:
time: 67.3 us; the launch traced here: 67.1 us
  waiting for transfers between devices  28.8 us (43%)
  Pallas kernels  20.7 us (31%)
  starting transfers between devices  14.4 us (21%)
  blocking collectives  2.17 us (3%)
  between operations  0.97 us (1%)
    ppermute x4, waiting for transfers between devices, on_device(): lax.ppermute(piece, 'dp', [(i, i ^ k) for i in range(owners)])  15.1 us
    ppermute x4, starting transfers between devices, on_device(): lax.ppermute(piece, 'dp', [(i, i ^ k) for i in range(owners)])  6.34 us
    ppermute x3, waiting for transfers between devices, on_device(): upstreams.append(lax.ppermute(grad, 'pipe', [(layer, layer - 1)]))  6.3 us
    pallas_call x1, Pallas kernels, adam_step(): pl.pallas_call(functools.partial(adam_kernel, (owners, parts, blocks[0].s...  5.67 us
    ppermute x4, waiting for transfers between devices, to_peers(): lax.ppermute(value, axis, [(i, (i + k) % size) for i in range(size)])  4.96 us
    pallas_call x1, Pallas kernels, first_step(): pl.pallas_call(functools.partial(first_kernel, layer, parts, len(peers),...  4.16 us
    ppermute x3, starting transfers between devices, on_device(): lax.ppermute(cut, ('pipe', 'dp'), [(s * owners + i, (s - 1) * owners + (i...  3.88 us
    pallas_call x1, Pallas kernels, stage(): pl.pallas_call(kernel, out_shape=[pltpu.VMEM(a.shape, a.dtype) for a in a...  3.6 us
  transfers between devices with their start and end apart: 19, of which 12 were waited for; matrix products, arithmetic and copies ran while one was open for 0% of the time, Pallas kernels for 16%

profile of v5, /device:TPU:0, one launch (start us, length us, event | category | flops | bytes accessed | tf_op | source)
XLA Modules:
  0.0 67.1 jit_solution(14256982654779550587)
XLA Ops:
  0.6 0.5 collective-permute-start
  1.1 3.6 %stage.1 = (bf16[2048,2048]{1,0:T(8,128)(2,1)S(1)}, bf16[128,2048]{1,0:T(8,128)(2,1)S(1)}, bf16[64,2048]{1,0:T(8,128)(2,1)S(1)}) custom-call(bf16[2048,2048]{1,0:T(8,128)(2,1)} %bitcast.15, bf16[128,2048]{1,0:T(8,128)(2,1)} %bitcast.17, bf16[64,2048]{1,0:T(8,128)(2,1)} %refs_2_.1), custom_call_target="tpu_custom_call" | custom-call | bytes 18350080 | tf_op jit(solution)/shard_map/stage/pallas_call | solution.py:55
  4.8 0.0 collective-permute-done.refs_0_
  4.8 0.0 copy-start
  4.8 4.2 %first_step.1 = (bf16[2048,2048]{1,0:T(8,128)(2,1)S(1)}, f32[64,2048]{1,0:T(8,128)S(1)}, bf16[64,2048]{1,0:T(8,128)(2,1)S(1)}, bf16[64,2048]{1,0:T(8,128)(2,1)S(...) custom-call(bf16[64,2048]{1,0:T(8,128)(2,1)S(1)} %get-tuple-element.37.own_ref.refs_1_.refs_4_.refs_6_.refs_7_.refs_0_, ...), custom_call_target="tpu_custom_call" | custom-call | tf_op jit(solution)/shard_map/first_step/pallas_call | solution.py:246
  8.9 0.1 collective-permute-start.1
  9.1 1.5 %collective-permute-done.1.refs_0_ = bf16[64,2048]{1,0:T(8,128)(2,1)S(1)} collective-permute-done((bf16[64,2048]{1,0:T(8,128)(2,1)S(1)}, bf16[64,2048]{1,0:T(8,128)(2,1)S(1)}, u32[]{:S(2)}, u32[]{:S(2)}) %collective-permute-start.1) | collective-permute-done | bytes 262176 | tf_op jit(solution)/shard_map/ppermute | solution.py:552
  10.5 0.0 copy-done
  10.6 0.7 %collective-permute-start.2 = (bf16[64,2048]{1,0:T(8,128)(2,1)S(1)}, bf16[64,2048]{1,0:T(8,128)(2,1)S(1)}, u32[]{:S(2)}, u32[]{:S(2)}) collective-permute-start(bf16[64,2048]{1,0:T(8,128)(2,1)S(1)} %get-tuple-element.45.refs_2_.refs_4_), channel_id=1, source_target_pairs={{24,16},{25,17},{26,18},{27,19},{28,20},{29,21},{30,22},{31,23}} | collective-permute-start | bytes 786440 | tf_op jit(solution)/shard_map/ppermute | solution.py:644
  11.3 2.7 %collective-permute-start.4 = (bf16[80,2048]{1,0:T(8,128)(2,1)S(1)}, bf16[80,2048]{1,0:T(8,128)(2,1)S(1)}, u32[]{:S(2)}, u32[]{:S(2)}) collective-permute-start(bf16[80,2048]{1,0:T(8,128)(2,1)S(1)} %get-tuple-element.47), channel_id=1, source_target_pairs={{0,2},{2,0},{4,6},{6,4},{1,3},{3,1},{5,7},{7,5},{8,10},{10,8},{12,... | collective-permute-start | bytes 983048 | tf_op jit(solution)/shard_map/ppermute | solution.py:661
  14.0 1.5 %collective-permute-start.5 = (bf16[80,2048]{1,0:T(8,128)(2,1)S(1)}, bf16[80,2048]{1,0:T(8,128)(2,1)S(1)}, u32[]{:S(2)}, u32[]{:S(2)}) collective-permute-start(bf16[80,2048]{1,0:T(8,128)(2,1)S(1)} %get-tuple-element.48), channel_id=1, source_target_pairs={{0,4},{2,6},{4,0},{6,2},{1,5},{3,7},{5,1},{7,3},{8,12},{10,14},{12... | collective-permute-start | bytes 983048 | tf_op jit(solution)/shard_map/ppermute | solution.py:661
  15.5 0.0 collective-permute-done.2.own_ref.refs_1_
  15.5 0.0 collective-permute-start.3
  15.5 3.5 %stage_in_section.2 = (f32[512,2048]{1,0:T(8,128)S(1)}, f32[512,2048]{1,0:T(8,128)S(1)}) custom-call(f32[512,2048]{1,0:T(8,128)} %bitcast.11, f32[512,2048]{1,0:T(8,128)} %bitcast.13, bf16[64,2048]{1,0:T(8,128)(2,1)S(1)} %get-tuple-element.45.refs_2_.refs_4_), custom_call_target="tpu_custom_call" | custom-call | tf_op jit(solution)/shard_map/stage_in_section/pallas_call | solution.py:81
  19.0 0.0 collective-permute-done.3.refs_0_
  19.0 3.2 %collective-permute-done.4.refs_0_.refs_8_.refs_2_.refs_7_ = bf16[80,2048]{1,0:T(8,128)(2,1)S(1)} collective-permute-done((bf16[80,2048]{1,0:T(8,128)(2,1)S(1)}, bf16[80,2048]{1,0:T(8,128)(2,1)S(1)}, u32[]{:S(2)}, u32[]{:S(2)}) %collective-permute-start.4) | collective-permute-done | bytes 327712 | tf_op jit(solution)/shard_map/ppermute | solution.py:661
  22.2 1.5 %collective-permute-done.5.refs_1_.refs_6_.refs_5_.refs_8_ = bf16[80,2048]{1,0:T(8,128)(2,1)S(1)} collective-permute-done((bf16[80,2048]{1,0:T(8,128)(2,1)S(1)}, bf16[80,2048]{1,0:T(8,128)(2,1)S(1)}, u32[]{:S(2)}, u32[]{:S(2)}) %collective-permute-start.5) | collective-permute-done | bytes 327712 | tf_op jit(solution)/shard_map/ppermute | solution.py:661
  23.7 0.0 collective-permute-start.6
  23.7 1.5 %collective-permute-done.6.refs_0_ = bf16[64,2048]{1,0:T(8,128)(2,1)S(1)} collective-permute-done((bf16[64,2048]{1,0:T(8,128)(2,1)S(1)}, bf16[64,2048]{1,0:T(8,128)(2,1)S(1)}, u32[]{:S(2)}, u32[]{:S(2)}) %collective-permute-start.6) | collective-permute-done | bytes 262176 | tf_op jit(solution)/shard_map/ppermute | solution.py:552
  25.2 0.1 norm_step.5
  25.3 0.7 %collective-permute-start.7 = (bf16[64,2048]{1,0:T(8,128)(2,1)S(1)}, bf16[64,2048]{1,0:T(8,128)(2,1)S(1)}, u32[]{:S(2)}, u32[]{:S(2)}) collective-permute-start(bf16[64,2048]{1,0:T(8,128)(2,1)S(1)} %get-tuple-element.53.refs_4_.refs_5_), channel_id=1, source_target_pairs={{16,8},{17,9},{18,10},{19,11},{20,12},{21,13},{22,14},{23,15}} | collective-permute-start | bytes 786440 | tf_op jit(solution)/shard_map/ppermute | solution.py:644
  26.0 0.4 collective-permute-start.9
  26.4 1.7 %collective-permute-start.10 = (bf16[128,2048]{1,0:T(8,128)(2,1)S(1)}, bf16[128,2048]{1,0:T(8,128)(2,1)S(1)}, u32[]{:S(2)}, u32[]{:S(2)}) collective-permute-start(bf16[128,2048]{1,0:T(8,128)(2,1)S(1)} %get-tuple-element.55), channel_id=1, source_target_pairs={{0,4},{2,6},{4,0},{6,2},{1,5},{3,7},{5,1},{7,3},{8,12},{10,14},{12... | collective-permute-start | bytes 1572872 | tf_op jit(solution)/shard_map/ppermute | solution.py:661
  28.1 0.0 collective-permute-done.7.own_ref.refs_1_.refs_2_
  28.1 0.0 collective-permute-start.8
  28.1 1.5 %collective-permute-done.8.refs_0_ = bf16[64,2048]{1,0:T(8,128)(2,1)S(1)} collective-permute-done((bf16[64,2048]{1,0:T(8,128)(2,1)S(1)}, bf16[64,2048]{1,0:T(8,128)(2,1)S(1)}, u32[]{:S(2)}, u32[]{:S(2)}) %collective-permute-start.8) | collective-permute-done | bytes 262176 | tf_op jit(solution)/shard_map/ppermute | solution.py:546
  29.6 10.4 %collective-permute-done.9.refs_0_.refs_3_.refs_7_ = bf16[128,2048]{1,0:T(8,128)(2,1)S(1)} collective-permute-done((bf16[128,2048]{1,0:T(8,128)(2,1)S(1)}, bf16[128,2048]{1,0:T(8,128)(2,1)S(1)}, u32[]{:S(2)}, u32[]{:S(2)}) %collective-permute-start.9) | collective-permute-done | bytes 524320 | tf_op jit(solution)/shard_map/ppermute | solution.py:661
  40.0 0.1 collective-permute-done.10.refs_1_.refs_4_.refs_6_
  40.1 0.0 collective-permute-start.11
  40.1 1.5 %collective-permute-done.11.refs_0_ = bf16[64,2048]{1,0:T(8,128)(2,1)S(1)} collective-permute-done((bf16[64,2048]{1,0:T(8,128)(2,1)S(1)}, bf16[64,2048]{1,0:T(8,128)(2,1)S(1)}, u32[]{:S(2)}, u32[]{:S(2)}) %collective-permute-start.11) | collective-permute-done | bytes 262176 | tf_op jit(solution)/shard_map/ppermute | solution.py:552
  41.6 1.3 %collective-permute-start.12 = (bf16[64,2048]{1,0:T(8,128)(2,1)S(1)}, bf16[64,2048]{1,0:T(8,128)(2,1)S(1)}, u32[]{:S(2)}, u32[]{:S(2)}) collective-permute-start(bf16[64,2048]{1,0:T(8,128)(2,1)S(1)} %get-tuple-element.60.refs_6_), channel_id=1, source_target_pairs={{8,0},{9,1},{10,2},{11,3},{12,4},{13,5},{14,6},{15,7}} | collective-permute-start | bytes 786440 | tf_op jit(solution)/shard_map/ppermute | solution.py:644
  42.9 0.7 collective-permute-start.17
  43.6 0.2 stack.1.refs_11_.refs_2_
  43.8 1.3 %collective-permute-start.14 = (bf16[64,512]{1,0:T(8,128)(2,1)S(1)}, bf16[64,512]{1,0:T(8,128)(2,1)S(1)}, u32[]{:S(2)}, u32[]{:S(2)}) collective-permute-start(bf16[64,512]{1,0:T(8,128)(2,1)S(1)} %get-tuple-element.63), channel_id=1, source_target_pairs={{8,2},{10,0},{12,6},{14,4},{16,10},{18,8},{20,14},{22,12},{24,18},... | collective-permute-start | bytes 196616 | tf_op jit(solution)/shard_map/ppermute | solution.py:648
  45.1 1.3 %collective-permute-start.15 = (bf16[64,512]{1,0:T(8,128)(2,1)S(1)}, bf16[64,512]{1,0:T(8,128)(2,1)S(1)}, u32[]{:S(2)}, u32[]{:S(2)}) collective-permute-start(bf16[64,512]{1,0:T(8,128)(2,1)S(1)} %get-tuple-element.64), channel_id=1, source_target_pairs={{8,4},{10,6},{12,0},{14,2},{16,12},{18,14},{20,8},{22,10},{24,20},... | collective-permute-start | bytes 196616 | tf_op jit(solution)/shard_map/ppermute | solution.py:648
  46.4 1.3 %collective-permute-start.16 = (bf16[64,512]{1,0:T(8,128)(2,1)S(1)}, bf16[64,512]{1,0:T(8,128)(2,1)S(1)}, u32[]{:S(2)}, u32[]{:S(2)}) collective-permute-start(bf16[64,512]{1,0:T(8,128)(2,1)S(1)} %get-tuple-element.65), channel_id=1, source_target_pairs={{8,6},{10,4},{12,2},{14,0},{16,14},{18,12},{20,10},{22,8},{24,22},... | collective-permute-start | bytes 196616 | tf_op jit(solution)/shard_map/ppermute | solution.py:648
  47.7 6.3 %collective-permute-done.12.refs_0_.refs_1_.refs_3_ = bf16[64,2048]{1,0:T(8,128)(2,1)S(1)} collective-permute-done((bf16[64,2048]{1,0:T(8,128)(2,1)S(1)}, bf16[64,2048]{1,0:T(8,128)(2,1)S(1)}, u32[]{:S(2)}, u32[]{:S(2)}) %collective-permute-start.12) | collective-permute-done | bytes 262176 | tf_op jit(solution)/shard_map/ppermute | solution.py:644
  54.0 2.2 %all_gather.3.refs_1_ = bf16[128,2048]{1,0:T(8,128)(2,1)S(1)} all-gather(bf16[64,2048]{1,0:T(8,128)(2,1)S(1)} %collective-permute-done.12.refs_0_.refs_1_.refs_3_), channel_id=1, replica_groups=mesh['pipe'=4,'dp'=4,'tensor'=2] {'tensor'}, dimensions={0}, use_global_device_ids=true | all-gather | bytes 786432 | tf_op jit(solution)/shard_map/all_gather | solution.py:585
  56.2 2.4 %section_step.1 = (f32[64,2048]{1,0:T(8,128)S(1)}, bf16[64,2048]{1,0:T(8,128)(2,1)S(1)}) custom-call(bf16[64,2048]{1,0:T(8,128)(2,1)S(1)} %collective-permute-done.12.refs_0_.refs_1_.refs_3_, bf16[128,2048]{1,0:T(8,128)(2,1)S(1)} %all_gather.3.refs_1_, bf16[2048,2048]{1,0:T(8,128)(2,1)S(1)} %get-tuple-element.38.refs_1_.refs_2_.refs_3_, ...), custom_call_target="tpu_custom_call" | custom-call | tf_op jit(solution)/shard_map/section_step/pallas_call | solution.py:284
  58.6 0.2 collective-permute-start.13
  58.8 0.0 collective-permute-done.17.refs_9_
  58.8 0.0 collective-permute-done.14.refs_4_
  58.8 0.0 collective-permute-done.15.refs_5_
  58.8 0.9 %collective-permute-done.16.refs_6_ = bf16[64,512]{1,0:T(8,128)(2,1)S(1)} collective-permute-done((bf16[64,512]{1,0:T(8,128)(2,1)S(1)}, bf16[64,512]{1,0:T(8,128)(2,1)S(1)}, u32[]{:S(2)}, u32[]{:S(2)}) %collective-permute-start.16) | collective-permute-done | bytes 65568 | tf_op jit(solution)/shard_map/ppermute | solution.py:648
  59.7 0.1 collective-permute-start.18
  59.7 0.4 collective-permute-done.13.refs_0_
  60.2 1.0 %norm_step.7 = bf16[64,2048]{1,0:T(8,128)(2,1)} custom-call(f32[64,2048]{1,0:T(8,128)S(1)} %get-tuple-element.61.kept_ref.refs_10_, bf16[64,2048]{1,0:T(8,128)(2,1)S(1)} %collective-permute-done.13.refs_0_, bf16[64,2048]{1,0:T(8,128)(2,1)S(1)} %collective-permute-done.12.refs_0_.refs_1_.refs_3_, bf16[64,2048]{1,0:T(8,128)(2,1)S(1)} %get-tuple-element.42.refs_2_, ...), custom_call_target="tpu_custom_call" | custom-call | tf_op jit(solution)/shard_map/norm_step/pallas_call | solution.py:373
  61.2 0.1 collective-permute-done.18.refs_1_
  61.3 5.7 %adam_step.1 = (f32[512,2048]{1,0:T(8,128)}, f32[512,2048]{1,0:T(8,128)}, f32[512,2048]{1,0:T(8,128)}) custom-call(bf16[256,512]{1,0:T(8,128)(2,1)S(1)} %collect.1.refs_0_, bf16[256,512]{1,0:T(8,128)(2,1)S(1)} %collective-permute-done.18.refs_1_, bf16[512,2048]{1,0:T(8,128)(2,1)S(1)} %stack.1.refs_11_.refs_2_, ...), custom_call_target="tpu_custom_call" | custom-call | tf_op jit(solution)/shard_map/adam_step/pallas_call | solution.py:480
  (8 shorter events, 0.1 us)
Async XLA Ops:
  0.6 4.1 %collective-permute-start = (bf16[64,2048]{1,0:T(8,128)(2,1)}, bf16[64,2048]{1,0:T(8,128)(2,1)S(1)}, u32[]{:S(2)}, u32[]{:S(2)}) collective-permute-start(bf16[64,2048]{1,0:T(8,128)(2,1)} %refs_2_.1), channel_id=1, source_target_pairs={{1,0},{0,1},{3,2},{2,3},{5,4},{4,5},{7,6},{6,7},{9,8},{8,9},{11,10... | collective-permute-start | bytes 786440 | tf_op jit(solution)/shard_map/ppermute | solution.py:546
  4.8 5.8 %copy-start = (f32[1,2048]{1,0:T(1,128)S(1)}, f32[1,2048]{1,0:T(1,128)}, u32[]{:S(2)}) copy-start(f32[1,2048]{1,0:T(1,128)} %refs_3_.7) | copy-start | bytes 24580
  8.9 1.6 %collective-permute-start.1 = (bf16[64,2048]{1,0:T(8,128)(2,1)S(1)}, bf16[64,2048]{1,0:T(8,128)(2,1)S(1)}, u32[]{:S(2)}, u32[]{:S(2)}) collective-permute-start(bf16[64,2048]{1,0:T(8,128)(2,1)S(1)} %get-tuple-element.41), channel_id=1, source_target_pairs={{0,1},{1,0},{2,3},{3,2},{4,5},{5,4},{6,7},{7,6},{8,9},{9,8},{10,11... | collective-permute-start | bytes 786440 | tf_op jit(solution)/shard_map/ppermute | solution.py:552
  10.6 4.9 %collective-permute-start.2 = (bf16[64,2048]{1,0:T(8,128)(2,1)S(1)}, bf16[64,2048]{1,0:T(8,128)(2,1)S(1)}, u32[]{:S(2)}, u32[]{:S(2)}) collective-permute-start(bf16[64,2048]{1,0:T(8,128)(2,1)S(1)} %get-tuple-element.45.refs_2_.refs_4_), channel_id=1, source_target_pairs={{24,16},{25,17},{26,18},{27,19},{28,20},{29,21},{30,22},{31,23}} | collective-permute-start | bytes 786440 | tf_op jit(solution)/shard_map/ppermute | solution.py:644
  11.3 10.9 %collective-permute-start.4 = (bf16[80,2048]{1,0:T(8,128)(2,1)S(1)}, bf16[80,2048]{1,0:T(8,128)(2,1)S(1)}, u32[]{:S(2)}, u32[]{:S(2)}) collective-permute-start(bf16[80,2048]{1,0:T(8,128)(2,1)S(1)} %get-tuple-element.47), channel_id=1, source_target_pairs={{0,2},{2,0},{4,6},{6,4},{1,3},{3,1},{5,7},{7,5},{8,10},{10,8},{12,... | collective-permute-start | bytes 983048 | tf_op jit(solution)/shard_map/ppermute | solution.py:661
  14.0 9.7 %collective-permute-start.5 = (bf16[80,2048]{1,0:T(8,128)(2,1)S(1)}, bf16[80,2048]{1,0:T(8,128)(2,1)S(1)}, u32[]{:S(2)}, u32[]{:S(2)}) collective-permute-start(bf16[80,2048]{1,0:T(8,128)(2,1)S(1)} %get-tuple-element.48), channel_id=1, source_target_pairs={{0,4},{2,6},{4,0},{6,2},{1,5},{3,7},{5,1},{7,3},{8,12},{10,14},{12... | collective-permute-start | bytes 983048 | tf_op jit(solution)/shard_map/ppermute | solution.py:661
  15.5 3.5 %collective-permute-start.3 = (bf16[64,2048]{1,0:T(8,128)(2,1)S(1)}, bf16[64,2048]{1,0:T(8,128)(2,1)S(1)}, u32[]{:S(2)}, u32[]{:S(2)}) collective-permute-start(bf16[64,2048]{1,0:T(8,128)(2,1)S(1)} %collective-permute-done.2.own_ref.refs_1_), channel_id=1, source_target_pairs={{1,0},{0,1},{3,2},{2,3},{5,4},{4,5},{7,6},{6,7},{9,8},{8,9},{11,10... | collective-permute-start | bytes 786440 | tf_op jit(solution)/shard_map/ppermute | solution.py:546
  23.7 1.5 %collective-permute-start.6 = (bf16[64,2048]{1,0:T(8,128)(2,1)S(1)}, bf16[64,2048]{1,0:T(8,128)(2,1)S(1)}, u32[]{:S(2)}, u32[]{:S(2)}) collective-permute-start(bf16[64,2048]{1,0:T(8,128)(2,1)S(1)} %get-tuple-element.52), channel_id=1, source_target_pairs={{0,1},{1,0},{2,3},{3,2},{4,5},{5,4},{6,7},{7,6},{8,9},{9,8},{10,11... | collective-permute-start | bytes 786440 | tf_op jit(solution)/shard_map/ppermute | solution.py:552
  25.3 2.8 %collective-permute-start.7 = (bf16[64,2048]{1,0:T(8,128)(2,1)S(1)}, bf16[64,2048]{1,0:T(8,128)(2,1)S(1)}, u32[]{:S(2)}, u32[]{:S(2)}) collective-permute-start(bf16[64,2048]{1,0:T(8,128)(2,1)S(1)} %get-tuple-element.53.refs_4_.refs_5_), channel_id=1, source_target_pairs={{16,8},{17,9},{18,10},{19,11},{20,12},{21,13},{22,14},{23,15}} | collective-permute-start | bytes 786440 | tf_op jit(solution)/shard_map/ppermute | solution.py:644
  26.0 14.0 %collective-permute-start.9 = (bf16[128,2048]{1,0:T(8,128)(2,1)S(1)}, bf16[128,2048]{1,0:T(8,128)(2,1)S(1)}, u32[]{:S(2)}, u32[]{:S(2)}) collective-permute-start(bf16[128,2048]{1,0:T(8,128)(2,1)S(1)} %get-tuple-element.54), channel_id=1, source_target_pairs={{0,2},{2,0},{4,6},{6,4},{1,3},{3,1},{5,7},{7,5},{8,10},{10,8},{12,... | collective-permute-start | bytes 1572872 | tf_op jit(solution)/shard_map/ppermute | solution.py:661
  26.4 13.7 %collective-permute-start.10 = (bf16[128,2048]{1,0:T(8,128)(2,1)S(1)}, bf16[128,2048]{1,0:T(8,128)(2,1)S(1)}, u32[]{:S(2)}, u32[]{:S(2)}) collective-permute-start(bf16[128,2048]{1,0:T(8,128)(2,1)S(1)} %get-tuple-element.55), channel_id=1, source_target_pairs={{0,4},{2,6},{4,0},{6,2},{1,5},{3,7},{5,1},{7,3},{8,12},{10,14},{12... | collective-permute-start | bytes 1572872 | tf_op jit(solution)/shard_map/ppermute | solution.py:661
  28.1 1.5 %collective-permute-start.8 = (bf16[64,2048]{1,0:T(8,128)(2,1)S(1)}, bf16[64,2048]{1,0:T(8,128)(2,1)S(1)}, u32[]{:S(2)}, u32[]{:S(2)}) collective-permute-start(bf16[64,2048]{1,0:T(8,128)(2,1)S(1)} %collective-permute-done.7.own_ref.refs_1_.refs_2_), channel_id=1, source_target_pairs={{1,0},{0,1},{3,2},{2,3},{5,4},{4,5},{7,6},{6,7},{9,8},{8,9},{11,10... | collective-permute-start | bytes 786440 | tf_op jit(solution)/shard_map/ppermute | solution.py:546
  40.1 1.5 %collective-permute-start.11 = (bf16[64,2048]{1,0:T(8,128)(2,1)S(1)}, bf16[64,2048]{1,0:T(8,128)(2,1)S(1)}, u32[]{:S(2)}, u32[]{:S(2)}) collective-permute-start(bf16[64,2048]{1,0:T(8,128)(2,1)S(1)} %get-tuple-element.59), channel_id=1, source_target_pairs={{0,1},{1,0},{2,3},{3,2},{4,5},{5,4},{6,7},{7,6},{8,9},{9,8},{10,11... | collective-permute-start | bytes 786440 | tf_op jit(solution)/shard_map/ppermute | solution.py:552
  41.6 12.4 %collective-permute-start.12 = (bf16[64,2048]{1,0:T(8,128)(2,1)S(1)}, bf16[64,2048]{1,0:T(8,128)(2,1)S(1)}, u32[]{:S(2)}, u32[]{:S(2)}) collective-permute-start(bf16[64,2048]{1,0:T(8,128)(2,1)S(1)} %get-tuple-element.60.refs_6_), channel_id=1, source_target_pairs={{8,0},{9,1},{10,2},{11,3},{12,4},{13,5},{14,6},{15,7}} | collective-permute-start | bytes 786440 | tf_op jit(solution)/shard_map/ppermute | solution.py:644
  42.9 15.9 %collective-permute-start.17 = (bf16[16,2048]{1,0:T(8,128)(2,1)S(1)}, bf16[16,2048]{1,0:T(8,128)(2,1)S(1)}, u32[]{:S(2)}, u32[]{:S(2)}) collective-permute-start(bf16[16,2048]{1,0:T(8,128)(2,1)S(1)} %get-tuple-element.66), channel_id=1, source_target_pairs={{24,30},{26,28},{28,26},{30,24},{25,31},{27,29},{29,27},{31,25}} | collective-permute-start | bytes 196616 | tf_op jit(solution)/shard_map/ppermute | solution.py:673
  43.8 14.9 %collective-permute-start.14 = (bf16[64,512]{1,0:T(8,128)(2,1)S(1)}, bf16[64,512]{1,0:T(8,128)(2,1)S(1)}, u32[]{:S(2)}, u32[]{:S(2)}) collective-permute-start(bf16[64,512]{1,0:T(8,128)(2,1)S(1)} %get-tuple-element.63), channel_id=1, source_target_pairs={{8,2},{10,0},{12,6},{14,4},{16,10},{18,8},{20,14},{22,12},{24,18},... | collective-permute-start | bytes 196616 | tf_op jit(solution)/shard_map/ppermute | solution.py:648
  45.1 13.7 %collective-permute-start.15 = (bf16[64,512]{1,0:T(8,128)(2,1)S(1)}, bf16[64,512]{1,0:T(8,128)(2,1)S(1)}, u32[]{:S(2)}, u32[]{:S(2)}) collective-permute-start(bf16[64,512]{1,0:T(8,128)(2,1)S(1)} %get-tuple-element.64), channel_id=1, source_target_pairs={{8,4},{10,6},{12,0},{14,2},{16,12},{18,14},{20,8},{22,10},{24,20},... | collective-permute-start | bytes 196616 | tf_op jit(solution)/shard_map/ppermute | solution.py:648
  46.4 13.2 %collective-permute-start.16 = (bf16[64,512]{1,0:T(8,128)(2,1)S(1)}, bf16[64,512]{1,0:T(8,128)(2,1)S(1)}, u32[]{:S(2)}, u32[]{:S(2)}) collective-permute-start(bf16[64,512]{1,0:T(8,128)(2,1)S(1)} %get-tuple-element.65), channel_id=1, source_target_pairs={{8,6},{10,4},{12,2},{14,0},{16,14},{18,12},{20,10},{22,8},{24,22},... | collective-permute-start | bytes 196616 | tf_op jit(solution)/shard_map/ppermute | solution.py:648
  58.6 1.6 %collective-permute-start.13 = (bf16[64,2048]{1,0:T(8,128)(2,1)S(1)}, bf16[64,2048]{1,0:T(8,128)(2,1)S(1)}, u32[]{:S(2)}, u32[]{:S(2)}) collective-permute-start(bf16[64,2048]{1,0:T(8,128)(2,1)S(1)} %get-tuple-element.62), channel_id=1, source_target_pairs={{0,1},{1,0},{2,3},{3,2},{4,5},{5,4},{6,7},{7,6},{8,9},{9,8},{10,11... | collective-permute-start | bytes 786440 | tf_op jit(solution)/shard_map/ppermute | solution.py:552
  59.7 1.6 %collective-permute-start.18 = (bf16[256,512]{1,0:T(8,128)(2,1)S(1)}, bf16[256,512]{1,0:T(8,128)(2,1)S(1)}, u32[]{:S(2)}, u32[]{:S(2)}) collective-permute-start(bf16[256,512]{1,0:T(8,128)(2,1)S(1)} %collect.1.refs_0_), channel_id=1, source_target_pairs={{1,0},{0,1},{3,2},{2,3},{5,4},{4,5},{7,6},{6,7},{9,8},{8,9},{11,10... | collective-permute-start | bytes 786440 | tf_op jit(solution)/shard_map/ppermute | solution.py:546

commit v6 on v5

--- a/solution.py
+++ b/solution.py
@@ -391,6 +391,8 @@
     count = sections + 2 * len(blocks)
 
     def kernel(*refs):
+        block_refs = refs[: owners - 1][::-1]
+        refs = [*refs[owners - 1 : owners - 1 + sections], *block_refs, *refs[owners - 1 + sections :]]
         out_ref = refs[-1]
         segment = lax.axis_index("pipe")
         at = pl.multiple_of(lax.axis_index("dp") * size, size)
@@ -424,7 +426,7 @@
         compiler_params=pltpu.CompilerParams(vmem_limit_bytes=4 * MIB),
         cost_estimate=CHEAP,
         name="collect",
-    )(*upstreams, *blocks, *[array for array, _ in packed], *after)
+    )(*blocks[::-1], *upstreams, *[array for array, _ in packed], *after)
 
 
 def adam_update(gradient, current, moment_one, moment_two):
@@ -439,9 +441,12 @@
 def adam_kernel(sizes, *refs):
     owners, parts, share, tile, part_rows = sizes
     up_refs = refs[:parts]
-    hidden_ref, down_ref, one_ref, two_ref = refs[parts : parts + 4]
-    outs = refs[parts + 4 : parts + 7]
-    rows_ref, *results, sem = refs[parts + 7 :]
+    refs = refs[parts:]
+    done_ref, hidden_ref, down_ref, one_ref, two_ref = refs[:5]
+    outs, done_out = refs[5:8], refs[8]
+    rows_ref, *results, sem, done_sem = refs[9:]
+    writing = pltpu.make_async_copy(done_ref, done_out, done_sem)
+    writing.start()
     rows = rows_ref.shape[1]
     me = lax.axis_index("dp")
     part = lax.axis_index("tensor")
@@ -470,25 +475,27 @@
                 writes[-1].start()
     for write in writes:
         write.wait()
-
-
-def adam_step(blocks, hidden_all, w_down, moment_one, moment_two, owners, parts):
+    writing.wait()
+
+
+def adam_step(blocks, done, hidden_all, w_down, moment_one, moment_two, owners, parts):
     rows, units = moment_one.shape
     tokens = hidden_all.shape[0]
     tile = tile_of(rows, 128)
     part_rows = tile_of(tile, 64)
     return pl.pallas_call(
         functools.partial(adam_kernel, (owners, parts, blocks[0].shape[0] // owners, tile, part_rows)),
-        out_shape=[jax.ShapeDtypeStruct((rows, units), F32)] * 3,
-        in_specs=[VMEM] * (len(blocks) + 4),
-        out_specs=[pl.BlockSpec(memory_space=pl.ANY)] * 3,
+        out_shape=[jax.ShapeDtypeStruct((rows, units), F32)] * 3
+        + [jax.ShapeDtypeStruct(done.shape, done.dtype)],
+        in_specs=[VMEM] * (len(blocks) + 5),
+        out_specs=[pl.BlockSpec(memory_space=pl.ANY)] * 4,
         scratch_shapes=[pltpu.VMEM((tokens, rows), BF16)]
         + [pltpu.VMEM((rows, units), F32)] * 3
-        + [pltpu.SemaphoreType.DMA((rows // part_rows, 3))],
+        + [pltpu.SemaphoreType.DMA((rows // part_rows, 3)), pltpu.SemaphoreType.DMA(())],
         compiler_params=pltpu.CompilerParams(vmem_limit_bytes=18 * MIB),
         cost_estimate=CHEAP,
         name="adam_step",
-    )(*blocks, hidden_all, w_down, moment_one, moment_two)
+    )(*blocks, done, hidden_all, w_down, moment_one, moment_two)
 
 
 def stack(order):
@@ -680,8 +687,8 @@
             else:
                 late = ()
     if planned:
-        first, second, updated = adam_step(
-            [own, *from_peers(own, "tensor")], hidden_all, w_down, *moments, owners, parts
+        first, second, updated, grads[-1] = adam_step(
+            [own, *from_peers(own, "tensor")], grads[-1], hidden_all, w_down, *moments, owners, parts
         )
     else:
         hidden_all = lax.all_gather(saved, "dp", axis=0, tiled=True)

time: 67.3 us -> 66.7 us (level)
    ppermute x3, waiting for transfers between devices: 0.87 us -> 0.01 us  [on_device(): lax.ppermute(cut, ('pipe', 'dp'), [(s * owners + i, (s - 1) * owners + (i...]
    pallas_call x4, Pallas kernels: 1.13 us -> 0.44 us  [norm_step(): pl.pallas_call(functools.partial(norm_kernel, layer, parts, len(earlier),...]
  transfers between devices with their start and end apart: 19 -> 19, of which waited for: 12 -> 10; matrix products, arithmetic and copies ran while one was open for 0% -> 0% of each run, Pallas kernels for 16% -> 15%
where the time goes in v6:
time: 66.7 us; the launch traced here: 66.5 us
  waiting for transfers between devices  28.3 us (42%)
  Pallas kernels  20.2 us (30%)
  starting transfers between devices  14.8 us (22%)
  blocking collectives  2.17 us (3%)
  between operations  0.98 us (1%)
    ppermute x4, waiting for transfers between devices, on_device(): lax.ppermute(piece, 'dp', [(i, i ^ k) for i in range(owners)])  15.1 us
    ppermute x4, starting transfers between devices, on_device(): lax.ppermute(piece, 'dp', [(i, i ^ k) for i in range(owners)])  6.34 us
    ppermute x3, waiting for transfers between devices, on_device(): upstreams.append(lax.ppermute(grad, 'pipe', [(layer, layer - 1)]))  6.3 us
    pallas_call x1, Pallas kernels, adam_step(): pl.pallas_call(functools.partial(adam_kernel, (owners, parts, blocks[0].s...  5.76 us
    ppermute x4, waiting for transfers between devices, to_peers(): lax.ppermute(value, axis, [(i, (i + k) % size) for i in range(size)])  5.42 us
    pallas_call x1, Pallas kernels, first_step(): pl.pallas_call(functools.partial(first_kernel, layer, parts, len(peers),...  4.16 us
    ppermute x3, starting transfers between devices, on_device(): lax.ppermute(cut, ('pipe', 'dp'), [(s * owners + i, (s - 1) * owners + (i...  3.88 us
    pallas_call x1, Pallas kernels, stage(): pl.pallas_call(kernel, out_shape=[pltpu.VMEM(a.shape, a.dtype) for a in a...  3.6 us
  transfers between devices with their start and end apart: 19, of which 10 were waited for; matrix products, arithmetic and copies ran while one was open for 0% of the time, Pallas kernels for 15%

profile of v6, /device:TPU:0, one launch (start us, length us, event | category | flops | bytes accessed | tf_op | source)
XLA Modules:
  0.0 66.5 jit_solution(10048640975040285671)
XLA Ops:
  0.6 0.5 collective-permute-start
  1.1 3.6 %stage.1 = (bf16[2048,2048]{1,0:T(8,128)(2,1)S(1)}, bf16[128,2048]{1,0:T(8,128)(2,1)S(1)}, bf16[64,2048]{1,0:T(8,128)(2,1)S(1)}) custom-call(bf16[2048,2048]{1,0:T(8,128)(2,1)} %bitcast.15, bf16[128,2048]{1,0:T(8,128)(2,1)} %bitcast.17, bf16[64,2048]{1,0:T(8,128)(2,1)} %refs_2_.1), custom_call_target="tpu_custom_call" | custom-call | bytes 18350080 | tf_op jit(solution)/shard_map/stage/pallas_call | solution.py:55
  4.8 0.0 collective-permute-done.refs_0_
  4.8 0.0 copy-start
  4.8 4.2 %first_step.1 = (bf16[2048,2048]{1,0:T(8,128)(2,1)S(1)}, f32[64,2048]{1,0:T(8,128)S(1)}, bf16[64,2048]{1,0:T(8,128)(2,1)S(1)}, bf16[64,2048]{1,0:T(8,128)(2,1)S(...) custom-call(bf16[64,2048]{1,0:T(8,128)(2,1)S(1)} %get-tuple-element.38.own_ref.refs_1_.refs_4_.refs_6_.refs_3_.refs_7_, ...), custom_call_target="tpu_custom_call" | custom-call | tf_op jit(solution)/shard_map/first_step/pallas_call | solution.py:246
  8.9 0.1 collective-permute-start.1
  9.1 1.5 %collective-permute-done.1.refs_0_ = bf16[64,2048]{1,0:T(8,128)(2,1)S(1)} collective-permute-done((bf16[64,2048]{1,0:T(8,128)(2,1)S(1)}, bf16[64,2048]{1,0:T(8,128)(2,1)S(1)}, u32[]{:S(2)}, u32[]{:S(2)}) %collective-permute-start.1) | collective-permute-done | bytes 262176 | tf_op jit(solution)/shard_map/ppermute | solution.py:559
  10.5 0.0 copy-done
  10.6 0.7 %collective-permute-start.2 = (bf16[64,2048]{1,0:T(8,128)(2,1)S(1)}, bf16[64,2048]{1,0:T(8,128)(2,1)S(1)}, u32[]{:S(2)}, u32[]{:S(2)}) collective-permute-start(bf16[64,2048]{1,0:T(8,128)(2,1)S(1)} %get-tuple-element.46.refs_2_.refs_4_), channel_id=1, source_target_pairs={{24,16},{25,17},{26,18},{27,19},{28,20},{29,21},{30,22},{31,23}} | collective-permute-start | bytes 786440 | tf_op jit(solution)/shard_map/ppermute | solution.py:651
  11.3 2.7 %collective-permute-start.4 = (bf16[80,2048]{1,0:T(8,128)(2,1)S(1)}, bf16[80,2048]{1,0:T(8,128)(2,1)S(1)}, u32[]{:S(2)}, u32[]{:S(2)}) collective-permute-start(bf16[80,2048]{1,0:T(8,128)(2,1)S(1)} %get-tuple-element.48), channel_id=1, source_target_pairs={{0,2},{2,0},{4,6},{6,4},{1,3},{3,1},{5,7},{7,5},{8,10},{10,8},{12,... | collective-permute-start | bytes 983048 | tf_op jit(solution)/shard_map/ppermute | solution.py:668
  14.0 1.5 %collective-permute-start.5 = (bf16[80,2048]{1,0:T(8,128)(2,1)S(1)}, bf16[80,2048]{1,0:T(8,128)(2,1)S(1)}, u32[]{:S(2)}, u32[]{:S(2)}) collective-permute-start(bf16[80,2048]{1,0:T(8,128)(2,1)S(1)} %get-tuple-element.49), channel_id=1, source_target_pairs={{0,4},{2,6},{4,0},{6,2},{1,5},{3,7},{5,1},{7,3},{8,12},{10,14},{12... | collective-permute-start | bytes 983048 | tf_op jit(solution)/shard_map/ppermute | solution.py:668
  15.5 0.0 collective-permute-done.2.own_ref.refs_1_.refs_4_
  15.5 0.0 collective-permute-start.3
  15.5 3.5 %stage_in_section.2 = (f32[512,2048]{1,0:T(8,128)S(1)}, f32[512,2048]{1,0:T(8,128)S(1)}) custom-call(f32[512,2048]{1,0:T(8,128)} %bitcast.11, f32[512,2048]{1,0:T(8,128)} %bitcast.13, bf16[64,2048]{1,0:T(8,128)(2,1)S(1)} %get-tuple-element.46.refs_2_.refs_4_), custom_call_target="tpu_custom_call" | custom-call | tf_op jit(solution)/shard_map/stage_in_section/pallas_call | solution.py:81
  19.0 0.0 collective-permute-done.3.refs_0_
  19.0 3.2 %collective-permute-done.4.refs_0_.refs_8_.refs_2_.refs_7_ = bf16[80,2048]{1,0:T(8,128)(2,1)S(1)} collective-permute-done((bf16[80,2048]{1,0:T(8,128)(2,1)S(1)}, bf16[80,2048]{1,0:T(8,128)(2,1)S(1)}, u32[]{:S(2)}, u32[]{:S(2)}) %collective-permute-start.4) | collective-permute-done | bytes 327712 | tf_op jit(solution)/shard_map/ppermute | solution.py:668
  22.2 1.5 %collective-permute-done.5.refs_1_.refs_6_.refs_5_.refs_8_ = bf16[80,2048]{1,0:T(8,128)(2,1)S(1)} collective-permute-done((bf16[80,2048]{1,0:T(8,128)(2,1)S(1)}, bf16[80,2048]{1,0:T(8,128)(2,1)S(1)}, u32[]{:S(2)}, u32[]{:S(2)}) %collective-permute-start.5) | collective-permute-done | bytes 327712 | tf_op jit(solution)/shard_map/ppermute | solution.py:668
  23.7 0.0 collective-permute-start.6
  23.7 1.5 %collective-permute-done.6.refs_0_ = bf16[64,2048]{1,0:T(8,128)(2,1)S(1)} collective-permute-done((bf16[64,2048]{1,0:T(8,128)(2,1)S(1)}, bf16[64,2048]{1,0:T(8,128)(2,1)S(1)}, u32[]{:S(2)}, u32[]{:S(2)}) %collective-permute-start.6) | collective-permute-done | bytes 262176 | tf_op jit(solution)/shard_map/ppermute | solution.py:559
  25.2 0.1 norm_step.5
  25.3 0.7 %collective-permute-start.7 = (bf16[64,2048]{1,0:T(8,128)(2,1)S(1)}, bf16[64,2048]{1,0:T(8,128)(2,1)S(1)}, u32[]{:S(2)}, u32[]{:S(2)}) collective-permute-start(bf16[64,2048]{1,0:T(8,128)(2,1)S(1)} %get-tuple-element.54.refs_4_.refs_5_), channel_id=1, source_target_pairs={{16,8},{17,9},{18,10},{19,11},{20,12},{21,13},{22,14},{23,15}} | collective-permute-start | bytes 786440 | tf_op jit(solution)/shard_map/ppermute | solution.py:651
  26.0 0.4 collective-permute-start.9
  26.4 1.7 %collective-permute-start.10 = (bf16[128,2048]{1,0:T(8,128)(2,1)S(1)}, bf16[128,2048]{1,0:T(8,128)(2,1)S(1)}, u32[]{:S(2)}, u32[]{:S(2)}) collective-permute-start(bf16[128,2048]{1,0:T(8,128)(2,1)S(1)} %get-tuple-element.56), channel_id=1, source_target_pairs={{0,4},{2,6},{4,0},{6,2},{1,5},{3,7},{5,1},{7,3},{8,12},{10,14},{12... | collective-permute-start | bytes 1572872 | tf_op jit(solution)/shard_map/ppermute | solution.py:668
  28.1 0.0 collective-permute-done.7.own_ref.refs_1_.refs_5_
  28.1 0.0 collective-permute-start.8
  28.1 1.5 %collective-permute-done.8.refs_0_ = bf16[64,2048]{1,0:T(8,128)(2,1)S(1)} collective-permute-done((bf16[64,2048]{1,0:T(8,128)(2,1)S(1)}, bf16[64,2048]{1,0:T(8,128)(2,1)S(1)}, u32[]{:S(2)}, u32[]{:S(2)}) %collective-permute-start.8) | collective-permute-done | bytes 262176 | tf_op jit(solution)/shard_map/ppermute | solution.py:553
  29.6 10.4 %collective-permute-done.9.refs_0_.refs_3_.refs_7_ = bf16[128,2048]{1,0:T(8,128)(2,1)S(1)} collective-permute-done((bf16[128,2048]{1,0:T(8,128)(2,1)S(1)}, bf16[128,2048]{1,0:T(8,128)(2,1)S(1)}, u32[]{:S(2)}, u32[]{:S(2)}) %collective-permute-start.9) | collective-permute-done | bytes 524320 | tf_op jit(solution)/shard_map/ppermute | solution.py:668
  40.0 0.1 collective-permute-done.10.refs_1_.refs_4_.refs_6_
  40.1 0.0 collective-permute-start.11
  40.1 1.5 %collective-permute-done.11.refs_0_ = bf16[64,2048]{1,0:T(8,128)(2,1)S(1)} collective-permute-done((bf16[64,2048]{1,0:T(8,128)(2,1)S(1)}, bf16[64,2048]{1,0:T(8,128)(2,1)S(1)}, u32[]{:S(2)}, u32[]{:S(2)}) %collective-permute-start.11) | collective-permute-done | bytes 262176 | tf_op jit(solution)/shard_map/ppermute | solution.py:559
  41.6 1.3 %collective-permute-start.15 = (bf16[64,2048]{1,0:T(8,128)(2,1)S(1)}, bf16[64,2048]{1,0:T(8,128)(2,1)S(1)}, u32[]{:S(2)}, u32[]{:S(2)}) collective-permute-start(bf16[64,2048]{1,0:T(8,128)(2,1)S(1)} %get-tuple-element.64.refs_6_), channel_id=1, source_target_pairs={{8,0},{9,1},{10,2},{11,3},{12,4},{13,5},{14,6},{15,7}} | collective-permute-start | bytes 786440 | tf_op jit(solution)/shard_map/ppermute | solution.py:651
  42.9 0.7 %collective-permute-start.16 = (bf16[16,2048]{1,0:T(8,128)(2,1)S(1)}, bf16[16,2048]{1,0:T(8,128)(2,1)S(1)}, u32[]{:S(2)}, u32[]{:S(2)}) collective-permute-start(bf16[16,2048]{1,0:T(8,128)(2,1)S(1)} %get-tuple-element.65), channel_id=1, source_target_pairs={{24,30},{26,28},{28,26},{30,24},{25,31},{27,29},{29,27},{31,25}} | collective-permute-start | bytes 196616 | tf_op jit(solution)/shard_map/ppermute | solution.py:680
  43.6 0.2 stack.1.refs_11_.refs_3_
  43.8 1.3 %collective-permute-start.12 = (bf16[64,512]{1,0:T(8,128)(2,1)S(1)}, bf16[64,512]{1,0:T(8,128)(2,1)S(1)}, u32[]{:S(2)}, u32[]{:S(2)}) collective-permute-start(bf16[64,512]{1,0:T(8,128)(2,1)S(1)} %get-tuple-element.61), channel_id=1, source_target_pairs={{8,6},{10,4},{12,2},{14,0},{16,14},{18,12},{20,10},{22,8},{24,22},... | collective-permute-start | bytes 196616 | tf_op jit(solution)/shard_map/ppermute | solution.py:655
  45.1 1.3 %collective-permute-start.13 = (bf16[64,512]{1,0:T(8,128)(2,1)S(1)}, bf16[64,512]{1,0:T(8,128)(2,1)S(1)}, u32[]{:S(2)}, u32[]{:S(2)}) collective-permute-start(bf16[64,512]{1,0:T(8,128)(2,1)S(1)} %get-tuple-element.62), channel_id=1, source_target_pairs={{8,4},{10,6},{12,0},{14,2},{16,12},{18,14},{20,8},{22,10},{24,20},... | collective-permute-start | bytes 196616 | tf_op jit(solution)/shard_map/ppermute | solution.py:655
  46.4 1.3 %collective-permute-start.14 = (bf16[64,512]{1,0:T(8,128)(2,1)S(1)}, bf16[64,512]{1,0:T(8,128)(2,1)S(1)}, u32[]{:S(2)}, u32[]{:S(2)}) collective-permute-start(bf16[64,512]{1,0:T(8,128)(2,1)S(1)} %get-tuple-element.63), channel_id=1, source_target_pairs={{8,2},{10,0},{12,6},{14,4},{16,10},{18,8},{20,14},{22,12},{24,18},... | collective-permute-start | bytes 196616 | tf_op jit(solution)/shard_map/ppermute | solution.py:655
  47.7 6.3 %collective-permute-done.15.refs_0_.refs_6_.refs_1_ = bf16[64,2048]{1,0:T(8,128)(2,1)S(1)} collective-permute-done((bf16[64,2048]{1,0:T(8,128)(2,1)S(1)}, bf16[64,2048]{1,0:T(8,128)(2,1)S(1)}, u32[]{:S(2)}, u32[]{:S(2)}) %collective-permute-start.15) | collective-permute-done | bytes 262176 | tf_op jit(solution)/shard_map/ppermute | solution.py:651
  54.0 2.2 %all_gather.3.refs_1_ = bf16[128,2048]{1,0:T(8,128)(2,1)S(1)} all-gather(bf16[64,2048]{1,0:T(8,128)(2,1)S(1)} %collective-permute-done.15.refs_0_.refs_6_.refs_1_), channel_id=1, replica_groups=mesh['pipe'=4,'dp'=4,'tensor'=2] {'tensor'}, dimensions={0}, use_global_device_ids=true | all-gather | bytes 786432 | tf_op jit(solution)/shard_map/all_gather | solution.py:592
  56.2 2.4 %section_step.1 = (f32[64,2048]{1,0:T(8,128)S(1)}, bf16[64,2048]{1,0:T(8,128)(2,1)S(1)}) custom-call(bf16[64,2048]{1,0:T(8,128)(2,1)S(1)} %collective-permute-done.15.refs_0_.refs_6_.refs_1_, bf16[128,2048]{1,0:T(8,128)(2,1)S(1)} %all_gather.3.refs_1_, bf16[2048,2048]{1,0:T(8,128)(2,1)S(1)} %get-tuple-element.39.refs_1_.refs_2_.refs_4_, ...), custom_call_target="tpu_custom_call" | custom-call | tf_op jit(solution)/shard_map/section_step/pallas_call | solution.py:284
  58.6 0.2 collective-permute-start.18
  58.8 0.0 collective-permute-done.16.refs_9_
  58.8 0.0 collective-permute-done.12.refs_0_
  58.8 0.0 collective-permute-done.13.refs_1_
  58.8 0.0 collective-permute-done.14.refs_2_
  58.8 0.1 collect.1.refs_0_
  58.9 0.4 collective-permute-start.17
  59.3 0.9 %collective-permute-done.18.refs_0_ = bf16[64,2048]{1,0:T(8,128)(2,1)S(1)} collective-permute-done((bf16[64,2048]{1,0:T(8,128)(2,1)S(1)}, bf16[64,2048]{1,0:T(8,128)(2,1)S(1)}, u32[]{:S(2)}, u32[]{:S(2)}) %collective-permute-start.18) | collective-permute-done | bytes 262176 | tf_op jit(solution)/shard_map/ppermute | solution.py:559
  60.2 0.3 norm_step.7.refs_2_
  60.5 0.0 collective-permute-done.17.refs_1_
  60.5 5.8 %adam_step.1 = (f32[512,2048]{1,0:T(8,128)}, f32[512,2048]{1,0:T(8,128)}, f32[512,2048]{1,0:T(8,128)}, bf16[64,2048]{1,0:T(8,128)(2,1)}) custom-call(bf16[256,512]{1,0:T(8,128)(2,1)S(1)} %collect.1.refs_0_, bf16[256,512]{1,0:T(8,128)(2,1)S(1)} %collective-permute-done.17.refs_1_, bf16[64,2048]{1,0:T(8,128)(2,1)S(1)} %norm_step.7.refs_2_, ...), custom_call_target="tpu_custom_call" | custom-call | tf_op jit(solution)/shard_map/adam_step/pallas_call | solution.py:486
  (7 shorter events, 0.1 us)
Async XLA Ops:
  0.6 4.1 %collective-permute-start = (bf16[64,2048]{1,0:T(8,128)(2,1)}, bf16[64,2048]{1,0:T(8,128)(2,1)S(1)}, u32[]{:S(2)}, u32[]{:S(2)}) collective-permute-start(bf16[64,2048]{1,0:T(8,128)(2,1)} %refs_2_.1), channel_id=1, source_target_pairs={{1,0},{0,1},{3,2},{2,3},{5,4},{4,5},{7,6},{6,7},{9,8},{8,9},{11,10... | collective-permute-start | bytes 786440 | tf_op jit(solution)/shard_map/ppermute | solution.py:553
  4.8 5.8 %copy-start = (f32[1,2048]{1,0:T(1,128)S(1)}, f32[1,2048]{1,0:T(1,128)}, u32[]{:S(2)}) copy-start(f32[1,2048]{1,0:T(1,128)} %refs_3_.7) | copy-start | bytes 24580
  8.9 1.6 %collective-permute-start.1 = (bf16[64,2048]{1,0:T(8,128)(2,1)S(1)}, bf16[64,2048]{1,0:T(8,128)(2,1)S(1)}, u32[]{:S(2)}, u32[]{:S(2)}) collective-permute-start(bf16[64,2048]{1,0:T(8,128)(2,1)S(1)} %get-tuple-element.42), channel_id=1, source_target_pairs={{0,1},{1,0},{2,3},{3,2},{4,5},{5,4},{6,7},{7,6},{8,9},{9,8},{10,11... | collective-permute-start | bytes 786440 | tf_op jit(solution)/shard_map/ppermute | solution.py:559
  10.6 4.9 %collective-permute-start.2 = (bf16[64,2048]{1,0:T(8,128)(2,1)S(1)}, bf16[64,2048]{1,0:T(8,128)(2,1)S(1)}, u32[]{:S(2)}, u32[]{:S(2)}) collective-permute-start(bf16[64,2048]{1,0:T(8,128)(2,1)S(1)} %get-tuple-element.46.refs_2_.refs_4_), channel_id=1, source_target_pairs={{24,16},{25,17},{26,18},{27,19},{28,20},{29,21},{30,22},{31,23}} | collective-permute-start | bytes 786440 | tf_op jit(solution)/shard_map/ppermute | solution.py:651
  11.3 10.9 %collective-permute-start.4 = (bf16[80,2048]{1,0:T(8,128)(2,1)S(1)}, bf16[80,2048]{1,0:T(8,128)(2,1)S(1)}, u32[]{:S(2)}, u32[]{:S(2)}) collective-permute-start(bf16[80,2048]{1,0:T(8,128)(2,1)S(1)} %get-tuple-element.48), channel_id=1, source_target_pairs={{0,2},{2,0},{4,6},{6,4},{1,3},{3,1},{5,7},{7,5},{8,10},{10,8},{12,... | collective-permute-start | bytes 983048 | tf_op jit(solution)/shard_map/ppermute | solution.py:668
  14.0 9.7 %collective-permute-start.5 = (bf16[80,2048]{1,0:T(8,128)(2,1)S(1)}, bf16[80,2048]{1,0:T(8,128)(2,1)S(1)}, u32[]{:S(2)}, u32[]{:S(2)}) collective-permute-start(bf16[80,2048]{1,0:T(8,128)(2,1)S(1)} %get-tuple-element.49), channel_id=1, source_target_pairs={{0,4},{2,6},{4,0},{6,2},{1,5},{3,7},{5,1},{7,3},{8,12},{10,14},{12... | collective-permute-start | bytes 983048 | tf_op jit(solution)/shard_map/ppermute | solution.py:668
  15.5 3.5 %collective-permute-start.3 = (bf16[64,2048]{1,0:T(8,128)(2,1)S(1)}, bf16[64,2048]{1,0:T(8,128)(2,1)S(1)}, u32[]{:S(2)}, u32[]{:S(2)}) collective-permute-start(bf16[64,2048]{1,0:T(8,128)(2,1)S(1)} %collective-permute-done.2.own_ref.refs_1_.refs_4_), channel_id=1, source_target_pairs={{1,0},{0,1},{3,2},{2,3},{5,4},{4,5},{7,6},{6,7},{9,8},{8,9},{11,10... | collective-permute-start | bytes 786440 | tf_op jit(solution)/shard_map/ppermute | solution.py:553
  23.7 1.5 %collective-permute-start.6 = (bf16[64,2048]{1,0:T(8,128)(2,1)S(1)}, bf16[64,2048]{1,0:T(8,128)(2,1)S(1)}, u32[]{:S(2)}, u32[]{:S(2)}) collective-permute-start(bf16[64,2048]{1,0:T(8,128)(2,1)S(1)} %get-tuple-element.53), channel_id=1, source_target_pairs={{0,1},{1,0},{2,3},{3,2},{4,5},{5,4},{6,7},{7,6},{8,9},{9,8},{10,11... | collective-permute-start | bytes 786440 | tf_op jit(solution)/shard_map/ppermute | solution.py:559
  25.3 2.8 %collective-permute-start.7 = (bf16[64,2048]{1,0:T(8,128)(2,1)S(1)}, bf16[64,2048]{1,0:T(8,128)(2,1)S(1)}, u32[]{:S(2)}, u32[]{:S(2)}) collective-permute-start(bf16[64,2048]{1,0:T(8,128)(2,1)S(1)} %get-tuple-element.54.refs_4_.refs_5_), channel_id=1, source_target_pairs={{16,8},{17,9},{18,10},{19,11},{20,12},{21,13},{22,14},{23,15}} | collective-permute-start | bytes 786440 | tf_op jit(solution)/shard_map/ppermute | solution.py:651
  26.0 14.0 %collective-permute-start.9 = (bf16[128,2048]{1,0:T(8,128)(2,1)S(1)}, bf16[128,2048]{1,0:T(8,128)(2,1)S(1)}, u32[]{:S(2)}, u32[]{:S(2)}) collective-permute-start(bf16[128,2048]{1,0:T(8,128)(2,1)S(1)} %get-tuple-element.55), channel_id=1, source_target_pairs={{0,2},{2,0},{4,6},{6,4},{1,3},{3,1},{5,7},{7,5},{8,10},{10,8},{12,... | collective-permute-start | bytes 1572872 | tf_op jit(solution)/shard_map/ppermute | solution.py:668
  26.4 13.7 %collective-permute-start.10 = (bf16[128,2048]{1,0:T(8,128)(2,1)S(1)}, bf16[128,2048]{1,0:T(8,128)(2,1)S(1)}, u32[]{:S(2)}, u32[]{:S(2)}) collective-permute-start(bf16[128,2048]{1,0:T(8,128)(2,1)S(1)} %get-tuple-element.56), channel_id=1, source_target_pairs={{0,4},{2,6},{4,0},{6,2},{1,5},{3,7},{5,1},{7,3},{8,12},{10,14},{12... | collective-permute-start | bytes 1572872 | tf_op jit(solution)/shard_map/ppermute | solution.py:668
  28.1 1.5 %collective-permute-start.8 = (bf16[64,2048]{1,0:T(8,128)(2,1)S(1)}, bf16[64,2048]{1,0:T(8,128)(2,1)S(1)}, u32[]{:S(2)}, u32[]{:S(2)}) collective-permute-start(bf16[64,2048]{1,0:T(8,128)(2,1)S(1)} %collective-permute-done.7.own_ref.refs_1_.refs_5_), channel_id=1, source_target_pairs={{1,0},{0,1},{3,2},{2,3},{5,4},{4,5},{7,6},{6,7},{9,8},{8,9},{11,10... | collective-permute-start | bytes 786440 | tf_op jit(solution)/shard_map/ppermute | solution.py:553
  40.1 1.5 %collective-permute-start.11 = (bf16[64,2048]{1,0:T(8,128)(2,1)S(1)}, bf16[64,2048]{1,0:T(8,128)(2,1)S(1)}, u32[]{:S(2)}, u32[]{:S(2)}) collective-permute-start(bf16[64,2048]{1,0:T(8,128)(2,1)S(1)} %get-tuple-element.60), channel_id=1, source_target_pairs={{0,1},{1,0},{2,3},{3,2},{4,5},{5,4},{6,7},{7,6},{8,9},{9,8},{10,11... | collective-permute-start | bytes 786440 | tf_op jit(solution)/shard_map/ppermute | solution.py:559
  41.6 12.4 %collective-permute-start.15 = (bf16[64,2048]{1,0:T(8,128)(2,1)S(1)}, bf16[64,2048]{1,0:T(8,128)(2,1)S(1)}, u32[]{:S(2)}, u32[]{:S(2)}) collective-permute-start(bf16[64,2048]{1,0:T(8,128)(2,1)S(1)} %get-tuple-element.64.refs_6_), channel_id=1, source_target_pairs={{8,0},{9,1},{10,2},{11,3},{12,4},{13,5},{14,6},{15,7}} | collective-permute-start | bytes 786440 | tf_op jit(solution)/shard_map/ppermute | solution.py:651
  42.9 15.9 %collective-permute-start.16 = (bf16[16,2048]{1,0:T(8,128)(2,1)S(1)}, bf16[16,2048]{1,0:T(8,128)(2,1)S(1)}, u32[]{:S(2)}, u32[]{:S(2)}) collective-permute-start(bf16[16,2048]{1,0:T(8,128)(2,1)S(1)} %get-tuple-element.65), channel_id=1, source_target_pairs={{24,30},{26,28},{28,26},{30,24},{25,31},{27,29},{29,27},{31,25}} | collective-permute-start | bytes 196616 | tf_op jit(solution)/shard_map/ppermute | solution.py:680
  43.8 14.9 %collective-permute-start.12 = (bf16[64,512]{1,0:T(8,128)(2,1)S(1)}, bf16[64,512]{1,0:T(8,128)(2,1)S(1)}, u32[]{:S(2)}, u32[]{:S(2)}) collective-permute-start(bf16[64,512]{1,0:T(8,128)(2,1)S(1)} %get-tuple-element.61), channel_id=1, source_target_pairs={{8,6},{10,4},{12,2},{14,0},{16,14},{18,12},{20,10},{22,8},{24,22},... | collective-permute-start | bytes 196616 | tf_op jit(solution)/shard_map/ppermute | solution.py:655
  45.1 13.7 %collective-permute-start.13 = (bf16[64,512]{1,0:T(8,128)(2,1)S(1)}, bf16[64,512]{1,0:T(8,128)(2,1)S(1)}, u32[]{:S(2)}, u32[]{:S(2)}) collective-permute-start(bf16[64,512]{1,0:T(8,128)(2,1)S(1)} %get-tuple-element.62), channel_id=1, source_target_pairs={{8,4},{10,6},{12,0},{14,2},{16,12},{18,14},{20,8},{22,10},{24,20},... | collective-permute-start | bytes 196616 | tf_op jit(solution)/shard_map/ppermute | solution.py:655
  46.4 12.4 %collective-permute-start.14 = (bf16[64,512]{1,0:T(8,128)(2,1)S(1)}, bf16[64,512]{1,0:T(8,128)(2,1)S(1)}, u32[]{:S(2)}, u32[]{:S(2)}) collective-permute-start(bf16[64,512]{1,0:T(8,128)(2,1)S(1)} %get-tuple-element.63), channel_id=1, source_target_pairs={{8,2},{10,0},{12,6},{14,4},{16,10},{18,8},{20,14},{22,12},{24,18},... | collective-permute-start | bytes 196616 | tf_op jit(solution)/shard_map/ppermute | solution.py:655
  58.6 1.6 %collective-permute-start.18 = (bf16[64,2048]{1,0:T(8,128)(2,1)S(1)}, bf16[64,2048]{1,0:T(8,128)(2,1)S(1)}, u32[]{:S(2)}, u32[]{:S(2)}) collective-permute-start(bf16[64,2048]{1,0:T(8,128)(2,1)S(1)} %get-tuple-element.67), channel_id=1, source_target_pairs={{0,1},{1,0},{2,3},{3,2},{4,5},{5,4},{6,7},{7,6},{8,9},{9,8},{10,11... | collective-permute-start | bytes 786440 | tf_op jit(solution)/shard_map/ppermute | solution.py:559
  58.9 1.7 %collective-permute-start.17 = (bf16[256,512]{1,0:T(8,128)(2,1)S(1)}, bf16[256,512]{1,0:T(8,128)(2,1)S(1)}, u32[]{:S(2)}, u32[]{:S(2)}) collective-permute-start(bf16[256,512]{1,0:T(8,128)(2,1)S(1)} %collect.1.refs_0_), channel_id=1, source_target_pairs={{1,0},{0,1},{3,2},{2,3},{5,4},{4,5},{7,6},{6,7},{9,8},{8,9},{11,10... | collective-permute-start | bytes 786440 | tf_op jit(solution)/shard_map/ppermute | solution.py:553

commit v7 on v6

--- a/solution.py
+++ b/solution.py
@@ -460,19 +460,26 @@
     for i in range(rows // tile):
         turned = rows_ref[:, i * tile : (i + 1) * tile].T
         gradient = jnp.dot(turned, hidden_ref[...], preferred_element_type=F32)
-        for j in range(tile // part_rows):
-            at = i * tile + j * part_rows
-            cut = slice(at, at + part_rows)
-            current = down_ref[pl.ds(pl.multiple_of(me * rows + at, part_rows), part_rows), :].astype(F32)
+        extents = [part_rows] * (tile // part_rows)
+        if i == 0:
+            extents[:1] = [part_rows // 2] * 2
+        if i == rows // tile - 1:
+            extents[-1:] = [part_rows // 2] * 2
+        at = i * tile
+        for extent in extents:
+            cut = slice(at, at + extent)
+            base = at - i * tile
+            current = down_ref[pl.ds(pl.multiple_of(me * rows + at, extent), extent), :].astype(F32)
             updates = adam_update(
-                gradient[j * part_rows : (j + 1) * part_rows], current, one_ref[cut, :], two_ref[cut, :]
+                gradient[base : base + extent], current, one_ref[cut, :], two_ref[cut, :]
             )
             for q, update in enumerate(updates):
                 results[q][cut, :] = update
                 writes.append(
-                    pltpu.make_async_copy(results[q].at[cut], outs[q].at[cut], sem.at[at // part_rows, q])
+                    pltpu.make_async_copy(results[q].at[cut], outs[q].at[cut], sem.at[len(writes) // 3, q])
                 )
                 writes[-1].start()
+            at += extent
     for write in writes:
         write.wait()
     writing.wait()
@@ -491,7 +498,7 @@
         out_specs=[pl.BlockSpec(memory_space=pl.ANY)] * 4,
         scratch_shapes=[pltpu.VMEM((tokens, rows), BF16)]
         + [pltpu.VMEM((rows, units), F32)] * 3
-        + [pltpu.SemaphoreType.DMA((rows // part_rows, 3)), pltpu.SemaphoreType.DMA(())],
+        + [pltpu.SemaphoreType.DMA((rows // part_rows + 2, 3)), pltpu.SemaphoreType.DMA(())],
         compiler_params=pltpu.CompilerParams(vmem_limit_bytes=18 * MIB),
         cost_estimate=CHEAP,
         name="adam_step",

time: 66.7 us -> 66.7 us (level)
  no operation moved by 1% of the time
where the time goes in v7:
time: 66.7 us; the launch traced here: 66.4 us
  waiting for transfers between devices  28.3 us (42%)
  Pallas kernels  20.2 us (30%)
  starting transfers between devices  14.8 us (22%)
  blocking collectives  2.17 us (3%)
  between operations  0.98 us (1%)
    ppermute x4, waiting for transfers between devices, on_device(): lax.ppermute(piece, 'dp', [(i, i ^ k) for i in range(owners)])  15.1 us
    ppermute x4, starting transfers between devices, on_device(): lax.ppermute(piece, 'dp', [(i, i ^ k) for i in range(owners)])  6.34 us
    ppermute x3, waiting for transfers between devices, on_device(): upstreams.append(lax.ppermute(grad, 'pipe', [(layer, layer - 1)]))  6.3 us
    pallas_call x1, Pallas kernels, adam_step(): pl.pallas_call(functools.partial(adam_kernel, (owners, parts, blocks[0].s...  5.75 us
    ppermute x4, waiting for transfers between devices, to_peers(): lax.ppermute(value, axis, [(i, (i + k) % size) for i in range(size)])  5.42 us
    pallas_call x1, Pallas kernels, first_step(): pl.pallas_call(functools.partial(first_kernel, layer, parts, len(peers),...  4.16 us
    ppermute x3, starting transfers between devices, on_device(): lax.ppermute(cut, ('pipe', 'dp'), [(s * owners + i, (s - 1) * owners + (i...  3.88 us
    pallas_call x1, Pallas kernels, stage(): pl.pallas_call(kernel, out_shape=[pltpu.VMEM(a.shape, a.dtype) for a in a...  3.6 us
  transfers between devices with their start and end apart: 19, of which 10 were waited for; matrix products, arithmetic and copies ran while one was open for 0% of the time, Pallas kernels for 15%

profile of v7, /device:TPU:0, one launch (start us, length us, event | category | flops | bytes accessed | tf_op | source)
XLA Modules:
  0.0 66.4 jit_solution(11030373989871412935)
XLA Ops:
  0.6 0.5 collective-permute-start
  1.1 3.6 %stage.1 = (bf16[2048,2048]{1,0:T(8,128)(2,1)S(1)}, bf16[128,2048]{1,0:T(8,128)(2,1)S(1)}, bf16[64,2048]{1,0:T(8,128)(2,1)S(1)}) custom-call(bf16[2048,2048]{1,0:T(8,128)(2,1)} %bitcast.15, bf16[128,2048]{1,0:T(8,128)(2,1)} %bitcast.17, bf16[64,2048]{1,0:T(8,128)(2,1)} %refs_2_.1), custom_call_target="tpu_custom_call" | custom-call | bytes 18350080 | tf_op jit(solution)/shard_map/stage/pallas_call | solution.py:55
  4.8 0.0 collective-permute-done.refs_0_
  4.8 0.0 copy-start
  4.8 4.2 %first_step.1 = (bf16[2048,2048]{1,0:T(8,128)(2,1)S(1)}, f32[64,2048]{1,0:T(8,128)S(1)}, bf16[64,2048]{1,0:T(8,128)(2,1)S(1)}, bf16[64,2048]{1,0:T(8,128)(2,1)S(...) custom-call(bf16[64,2048]{1,0:T(8,128)(2,1)S(1)} %get-tuple-element.38.own_ref.refs_1_.refs_4_.refs_6_.refs_3_.refs_7_, ...), custom_call_target="tpu_custom_call" | custom-call | tf_op jit(solution)/shard_map/first_step/pallas_call | solution.py:246
  8.9 0.1 collective-permute-start.1
  9.1 1.5 %collective-permute-done.1.refs_0_ = bf16[64,2048]{1,0:T(8,128)(2,1)S(1)} collective-permute-done((bf16[64,2048]{1,0:T(8,128)(2,1)S(1)}, bf16[64,2048]{1,0:T(8,128)(2,1)S(1)}, u32[]{:S(2)}, u32[]{:S(2)}) %collective-permute-start.1) | collective-permute-done | bytes 262176 | tf_op jit(solution)/shard_map/ppermute | solution.py:566
  10.5 0.0 copy-done
  10.6 0.7 %collective-permute-start.2 = (bf16[64,2048]{1,0:T(8,128)(2,1)S(1)}, bf16[64,2048]{1,0:T(8,128)(2,1)S(1)}, u32[]{:S(2)}, u32[]{:S(2)}) collective-permute-start(bf16[64,2048]{1,0:T(8,128)(2,1)S(1)} %get-tuple-element.46.refs_2_.refs_4_), channel_id=1, source_target_pairs={{24,16},{25,17},{26,18},{27,19},{28,20},{29,21},{30,22},{31,23}} | collective-permute-start | bytes 786440 | tf_op jit(solution)/shard_map/ppermute | solution.py:658
  11.3 2.7 %collective-permute-start.4 = (bf16[80,2048]{1,0:T(8,128)(2,1)S(1)}, bf16[80,2048]{1,0:T(8,128)(2,1)S(1)}, u32[]{:S(2)}, u32[]{:S(2)}) collective-permute-start(bf16[80,2048]{1,0:T(8,128)(2,1)S(1)} %get-tuple-element.48), channel_id=1, source_target_pairs={{0,2},{2,0},{4,6},{6,4},{1,3},{3,1},{5,7},{7,5},{8,10},{10,8},{12,... | collective-permute-start | bytes 983048 | tf_op jit(solution)/shard_map/ppermute | solution.py:675
  14.0 1.5 %collective-permute-start.5 = (bf16[80,2048]{1,0:T(8,128)(2,1)S(1)}, bf16[80,2048]{1,0:T(8,128)(2,1)S(1)}, u32[]{:S(2)}, u32[]{:S(2)}) collective-permute-start(bf16[80,2048]{1,0:T(8,128)(2,1)S(1)} %get-tuple-element.49), channel_id=1, source_target_pairs={{0,4},{2,6},{4,0},{6,2},{1,5},{3,7},{5,1},{7,3},{8,12},{10,14},{12... | collective-permute-start | bytes 983048 | tf_op jit(solution)/shard_map/ppermute | solution.py:675
  15.5 0.0 collective-permute-done.2.own_ref.refs_1_.refs_4_
  15.5 0.0 collective-permute-start.3
  15.5 3.5 %stage_in_section.2 = (f32[512,2048]{1,0:T(8,128)S(1)}, f32[512,2048]{1,0:T(8,128)S(1)}) custom-call(f32[512,2048]{1,0:T(8,128)} %bitcast.11, f32[512,2048]{1,0:T(8,128)} %bitcast.13, bf16[64,2048]{1,0:T(8,128)(2,1)S(1)} %get-tuple-element.46.refs_2_.refs_4_), custom_call_target="tpu_custom_call" | custom-call | tf_op jit(solution)/shard_map/stage_in_section/pallas_call | solution.py:81
  19.0 0.0 collective-permute-done.3.refs_0_
  19.0 3.2 %collective-permute-done.4.refs_0_.refs_8_.refs_2_.refs_7_ = bf16[80,2048]{1,0:T(8,128)(2,1)S(1)} collective-permute-done((bf16[80,2048]{1,0:T(8,128)(2,1)S(1)}, bf16[80,2048]{1,0:T(8,128)(2,1)S(1)}, u32[]{:S(2)}, u32[]{:S(2)}) %collective-permute-start.4) | collective-permute-done | bytes 327712 | tf_op jit(solution)/shard_map/ppermute | solution.py:675
  22.2 1.5 %collective-permute-done.5.refs_1_.refs_6_.refs_5_.refs_8_ = bf16[80,2048]{1,0:T(8,128)(2,1)S(1)} collective-permute-done((bf16[80,2048]{1,0:T(8,128)(2,1)S(1)}, bf16[80,2048]{1,0:T(8,128)(2,1)S(1)}, u32[]{:S(2)}, u32[]{:S(2)}) %collective-permute-start.5) | collective-permute-done | bytes 327712 | tf_op jit(solution)/shard_map/ppermute | solution.py:675
  23.7 0.0 collective-permute-start.6
  23.7 1.5 %collective-permute-done.6.refs_0_ = bf16[64,2048]{1,0:T(8,128)(2,1)S(1)} collective-permute-done((bf16[64,2048]{1,0:T(8,128)(2,1)S(1)}, bf16[64,2048]{1,0:T(8,128)(2,1)S(1)}, u32[]{:S(2)}, u32[]{:S(2)}) %collective-permute-start.6) | collective-permute-done | bytes 262176 | tf_op jit(solution)/shard_map/ppermute | solution.py:566
  25.2 0.1 norm_step.5
  25.3 0.7 %collective-permute-start.7 = (bf16[64,2048]{1,0:T(8,128)(2,1)S(1)}, bf16[64,2048]{1,0:T(8,128)(2,1)S(1)}, u32[]{:S(2)}, u32[]{:S(2)}) collective-permute-start(bf16[64,2048]{1,0:T(8,128)(2,1)S(1)} %get-tuple-element.54.refs_4_.refs_5_), channel_id=1, source_target_pairs={{16,8},{17,9},{18,10},{19,11},{20,12},{21,13},{22,14},{23,15}} | collective-permute-start | bytes 786440 | tf_op jit(solution)/shard_map/ppermute | solution.py:658
  26.0 0.4 collective-permute-start.9
  26.4 1.7 %collective-permute-start.10 = (bf16[128,2048]{1,0:T(8,128)(2,1)S(1)}, bf16[128,2048]{1,0:T(8,128)(2,1)S(1)}, u32[]{:S(2)}, u32[]{:S(2)}) collective-permute-start(bf16[128,2048]{1,0:T(8,128)(2,1)S(1)} %get-tuple-element.56), channel_id=1, source_target_pairs={{0,4},{2,6},{4,0},{6,2},{1,5},{3,7},{5,1},{7,3},{8,12},{10,14},{12... | collective-permute-start | bytes 1572872 | tf_op jit(solution)/shard_map/ppermute | solution.py:675
  28.1 0.0 collective-permute-done.7.own_ref.refs_1_.refs_5_
  28.1 0.0 collective-permute-start.8
  28.1 1.5 %collective-permute-done.8.refs_0_ = bf16[64,2048]{1,0:T(8,128)(2,1)S(1)} collective-permute-done((bf16[64,2048]{1,0:T(8,128)(2,1)S(1)}, bf16[64,2048]{1,0:T(8,128)(2,1)S(1)}, u32[]{:S(2)}, u32[]{:S(2)}) %collective-permute-start.8) | collective-permute-done | bytes 262176 | tf_op jit(solution)/shard_map/ppermute | solution.py:560
  29.6 10.4 %collective-permute-done.9.refs_0_.refs_3_.refs_7_ = bf16[128,2048]{1,0:T(8,128)(2,1)S(1)} collective-permute-done((bf16[128,2048]{1,0:T(8,128)(2,1)S(1)}, bf16[128,2048]{1,0:T(8,128)(2,1)S(1)}, u32[]{:S(2)}, u32[]{:S(2)}) %collective-permute-start.9) | collective-permute-done | bytes 524320 | tf_op jit(solution)/shard_map/ppermute | solution.py:675
  40.0 0.1 collective-permute-done.10.refs_1_.refs_4_.refs_6_
  40.1 0.0 collective-permute-start.11
  40.1 1.5 %collective-permute-done.11.refs_0_ = bf16[64,2048]{1,0:T(8,128)(2,1)S(1)} collective-permute-done((bf16[64,2048]{1,0:T(8,128)(2,1)S(1)}, bf16[64,2048]{1,0:T(8,128)(2,1)S(1)}, u32[]{:S(2)}, u32[]{:S(2)}) %collective-permute-start.11) | collective-permute-done | bytes 262176 | tf_op jit(solution)/shard_map/ppermute | solution.py:566
  41.6 1.3 %collective-permute-start.15 = (bf16[64,2048]{1,0:T(8,128)(2,1)S(1)}, bf16[64,2048]{1,0:T(8,128)(2,1)S(1)}, u32[]{:S(2)}, u32[]{:S(2)}) collective-permute-start(bf16[64,2048]{1,0:T(8,128)(2,1)S(1)} %get-tuple-element.64.refs_6_), channel_id=1, source_target_pairs={{8,0},{9,1},{10,2},{11,3},{12,4},{13,5},{14,6},{15,7}} | collective-permute-start | bytes 786440 | tf_op jit(solution)/shard_map/ppermute | solution.py:658
  42.9 0.7 %collective-permute-start.16 = (bf16[16,2048]{1,0:T(8,128)(2,1)S(1)}, bf16[16,2048]{1,0:T(8,128)(2,1)S(1)}, u32[]{:S(2)}, u32[]{:S(2)}) collective-permute-start(bf16[16,2048]{1,0:T(8,128)(2,1)S(1)} %get-tuple-element.65), channel_id=1, source_target_pairs={{24,30},{26,28},{28,26},{30,24},{25,31},{27,29},{29,27},{31,25}} | collective-permute-start | bytes 196616 | tf_op jit(solution)/shard_map/ppermute | solution.py:687
  43.6 0.2 stack.1.refs_11_.refs_3_
  43.8 1.3 %collective-permute-start.12 = (bf16[64,512]{1,0:T(8,128)(2,1)S(1)}, bf16[64,512]{1,0:T(8,128)(2,1)S(1)}, u32[]{:S(2)}, u32[]{:S(2)}) collective-permute-start(bf16[64,512]{1,0:T(8,128)(2,1)S(1)} %get-tuple-element.61), channel_id=1, source_target_pairs={{8,6},{10,4},{12,2},{14,0},{16,14},{18,12},{20,10},{22,8},{24,22},... | collective-permute-start | bytes 196616 | tf_op jit(solution)/shard_map/ppermute | solution.py:662
  45.1 1.3 %collective-permute-start.13 = (bf16[64,512]{1,0:T(8,128)(2,1)S(1)}, bf16[64,512]{1,0:T(8,128)(2,1)S(1)}, u32[]{:S(2)}, u32[]{:S(2)}) collective-permute-start(bf16[64,512]{1,0:T(8,128)(2,1)S(1)} %get-tuple-element.62), channel_id=1, source_target_pairs={{8,4},{10,6},{12,0},{14,2},{16,12},{18,14},{20,8},{22,10},{24,20},... | collective-permute-start | bytes 196616 | tf_op jit(solution)/shard_map/ppermute | solution.py:662
  46.4 1.3 %collective-permute-start.14 = (bf16[64,512]{1,0:T(8,128)(2,1)S(1)}, bf16[64,512]{1,0:T(8,128)(2,1)S(1)}, u32[]{:S(2)}, u32[]{:S(2)}) collective-permute-start(bf16[64,512]{1,0:T(8,128)(2,1)S(1)} %get-tuple-element.63), channel_id=1, source_target_pairs={{8,2},{10,0},{12,6},{14,4},{16,10},{18,8},{20,14},{22,12},{24,18},... | collective-permute-start | bytes 196616 | tf_op jit(solution)/shard_map/ppermute | solution.py:662
  47.7 6.3 %collective-permute-done.15.refs_0_.refs_6_.refs_1_ = bf16[64,2048]{1,0:T(8,128)(2,1)S(1)} collective-permute-done((bf16[64,2048]{1,0:T(8,128)(2,1)S(1)}, bf16[64,2048]{1,0:T(8,128)(2,1)S(1)}, u32[]{:S(2)}, u32[]{:S(2)}) %collective-permute-start.15) | collective-permute-done | bytes 262176 | tf_op jit(solution)/shard_map/ppermute | solution.py:658
  54.0 2.2 %all_gather.3.refs_1_ = bf16[128,2048]{1,0:T(8,128)(2,1)S(1)} all-gather(bf16[64,2048]{1,0:T(8,128)(2,1)S(1)} %collective-permute-done.15.refs_0_.refs_6_.refs_1_), channel_id=1, replica_groups=mesh['pipe'=4,'dp'=4,'tensor'=2] {'tensor'}, dimensions={0}, use_global_device_ids=true | all-gather | bytes 786432 | tf_op jit(solution)/shard_map/all_gather | solution.py:599
  56.2 2.4 %section_step.1 = (f32[64,2048]{1,0:T(8,128)S(1)}, bf16[64,2048]{1,0:T(8,128)(2,1)S(1)}) custom-call(bf16[64,2048]{1,0:T(8,128)(2,1)S(1)} %collective-permute-done.15.refs_0_.refs_6_.refs_1_, bf16[128,2048]{1,0:T(8,128)(2,1)S(1)} %all_gather.3.refs_1_, bf16[2048,2048]{1,0:T(8,128)(2,1)S(1)} %get-tuple-element.39.refs_1_.refs_2_.refs_4_, ...), custom_call_target="tpu_custom_call" | custom-call | tf_op jit(solution)/shard_map/section_step/pallas_call | solution.py:284
  58.6 0.2 collective-permute-start.18
  58.8 0.0 collective-permute-done.16.refs_9_
  58.8 0.0 collective-permute-done.12.refs_0_
  58.8 0.0 collective-permute-done.13.refs_1_
  58.8 0.0 collective-permute-done.14.refs_2_
  58.8 0.1 collect.1.refs_0_
  58.9 0.4 collective-permute-start.17
  59.3 0.9 %collective-permute-done.18.refs_0_ = bf16[64,2048]{1,0:T(8,128)(2,1)S(1)} collective-permute-done((bf16[64,2048]{1,0:T(8,128)(2,1)S(1)}, bf16[64,2048]{1,0:T(8,128)(2,1)S(1)}, u32[]{:S(2)}, u32[]{:S(2)}) %collective-permute-start.18) | collective-permute-done | bytes 262176 | tf_op jit(solution)/shard_map/ppermute | solution.py:566
  60.2 0.3 norm_step.7.refs_2_
  60.5 0.0 collective-permute-done.17.refs_1_
  60.5 5.7 %adam_step.1 = (f32[512,2048]{1,0:T(8,128)}, f32[512,2048]{1,0:T(8,128)}, f32[512,2048]{1,0:T(8,128)}, bf16[64,2048]{1,0:T(8,128)(2,1)}) custom-call(bf16[256,512]{1,0:T(8,128)(2,1)S(1)} %collect.1.refs_0_, bf16[256,512]{1,0:T(8,128)(2,1)S(1)} %collective-permute-done.17.refs_1_, bf16[64,2048]{1,0:T(8,128)(2,1)S(1)} %norm_step.7.refs_2_, ...), custom_call_target="tpu_custom_call" | custom-call | tf_op jit(solution)/shard_map/adam_step/pallas_call | solution.py:493
  (7 shorter events, 0.1 us)
Async XLA Ops:
  0.6 4.1 %collective-permute-start = (bf16[64,2048]{1,0:T(8,128)(2,1)}, bf16[64,2048]{1,0:T(8,128)(2,1)S(1)}, u32[]{:S(2)}, u32[]{:S(2)}) collective-permute-start(bf16[64,2048]{1,0:T(8,128)(2,1)} %refs_2_.1), channel_id=1, source_target_pairs={{1,0},{0,1},{3,2},{2,3},{5,4},{4,5},{7,6},{6,7},{9,8},{8,9},{11,10... | collective-permute-start | bytes 786440 | tf_op jit(solution)/shard_map/ppermute | solution.py:560
  4.8 5.8 %copy-start = (f32[1,2048]{1,0:T(1,128)S(1)}, f32[1,2048]{1,0:T(1,128)}, u32[]{:S(2)}) copy-start(f32[1,2048]{1,0:T(1,128)} %refs_3_.7) | copy-start | bytes 24580
  8.9 1.6 %collective-permute-start.1 = (bf16[64,2048]{1,0:T(8,128)(2,1)S(1)}, bf16[64,2048]{1,0:T(8,128)(2,1)S(1)}, u32[]{:S(2)}, u32[]{:S(2)}) collective-permute-start(bf16[64,2048]{1,0:T(8,128)(2,1)S(1)} %get-tuple-element.42), channel_id=1, source_target_pairs={{0,1},{1,0},{2,3},{3,2},{4,5},{5,4},{6,7},{7,6},{8,9},{9,8},{10,11... | collective-permute-start | bytes 786440 | tf_op jit(solution)/shard_map/ppermute | solution.py:566
  10.6 4.9 %collective-permute-start.2 = (bf16[64,2048]{1,0:T(8,128)(2,1)S(1)}, bf16[64,2048]{1,0:T(8,128)(2,1)S(1)}, u32[]{:S(2)}, u32[]{:S(2)}) collective-permute-start(bf16[64,2048]{1,0:T(8,128)(2,1)S(1)} %get-tuple-element.46.refs_2_.refs_4_), channel_id=1, source_target_pairs={{24,16},{25,17},{26,18},{27,19},{28,20},{29,21},{30,22},{31,23}} | collective-permute-start | bytes 786440 | tf_op jit(solution)/shard_map/ppermute | solution.py:658
  11.3 10.9 %collective-permute-start.4 = (bf16[80,2048]{1,0:T(8,128)(2,1)S(1)}, bf16[80,2048]{1,0:T(8,128)(2,1)S(1)}, u32[]{:S(2)}, u32[]{:S(2)}) collective-permute-start(bf16[80,2048]{1,0:T(8,128)(2,1)S(1)} %get-tuple-element.48), channel_id=1, source_target_pairs={{0,2},{2,0},{4,6},{6,4},{1,3},{3,1},{5,7},{7,5},{8,10},{10,8},{12,... | collective-permute-start | bytes 983048 | tf_op jit(solution)/shard_map/ppermute | solution.py:675
  14.0 9.7 %collective-permute-start.5 = (bf16[80,2048]{1,0:T(8,128)(2,1)S(1)}, bf16[80,2048]{1,0:T(8,128)(2,1)S(1)}, u32[]{:S(2)}, u32[]{:S(2)}) collective-permute-start(bf16[80,2048]{1,0:T(8,128)(2,1)S(1)} %get-tuple-element.49), channel_id=1, source_target_pairs={{0,4},{2,6},{4,0},{6,2},{1,5},{3,7},{5,1},{7,3},{8,12},{10,14},{12... | collective-permute-start | bytes 983048 | tf_op jit(solution)/shard_map/ppermute | solution.py:675
  15.5 3.5 %collective-permute-start.3 = (bf16[64,2048]{1,0:T(8,128)(2,1)S(1)}, bf16[64,2048]{1,0:T(8,128)(2,1)S(1)}, u32[]{:S(2)}, u32[]{:S(2)}) collective-permute-start(bf16[64,2048]{1,0:T(8,128)(2,1)S(1)} %collective-permute-done.2.own_ref.refs_1_.refs_4_), channel_id=1, source_target_pairs={{1,0},{0,1},{3,2},{2,3},{5,4},{4,5},{7,6},{6,7},{9,8},{8,9},{11,10... | collective-permute-start | bytes 786440 | tf_op jit(solution)/shard_map/ppermute | solution.py:560
  23.7 1.5 %collective-permute-start.6 = (bf16[64,2048]{1,0:T(8,128)(2,1)S(1)}, bf16[64,2048]{1,0:T(8,128)(2,1)S(1)}, u32[]{:S(2)}, u32[]{:S(2)}) collective-permute-start(bf16[64,2048]{1,0:T(8,128)(2,1)S(1)} %get-tuple-element.53), channel_id=1, source_target_pairs={{0,1},{1,0},{2,3},{3,2},{4,5},{5,4},{6,7},{7,6},{8,9},{9,8},{10,11... | collective-permute-start | bytes 786440 | tf_op jit(solution)/shard_map/ppermute | solution.py:566
  25.3 2.8 %collective-permute-start.7 = (bf16[64,2048]{1,0:T(8,128)(2,1)S(1)}, bf16[64,2048]{1,0:T(8,128)(2,1)S(1)}, u32[]{:S(2)}, u32[]{:S(2)}) collective-permute-start(bf16[64,2048]{1,0:T(8,128)(2,1)S(1)} %get-tuple-element.54.refs_4_.refs_5_), channel_id=1, source_target_pairs={{16,8},{17,9},{18,10},{19,11},{20,12},{21,13},{22,14},{23,15}} | collective-permute-start | bytes 786440 | tf_op jit(solution)/shard_map/ppermute | solution.py:658
  26.0 14.0 %collective-permute-start.9 = (bf16[128,2048]{1,0:T(8,128)(2,1)S(1)}, bf16[128,2048]{1,0:T(8,128)(2,1)S(1)}, u32[]{:S(2)}, u32[]{:S(2)}) collective-permute-start(bf16[128,2048]{1,0:T(8,128)(2,1)S(1)} %get-tuple-element.55), channel_id=1, source_target_pairs={{0,2},{2,0},{4,6},{6,4},{1,3},{3,1},{5,7},{7,5},{8,10},{10,8},{12,... | collective-permute-start | bytes 1572872 | tf_op jit(solution)/shard_map/ppermute | solution.py:675
  26.4 13.7 %collective-permute-start.10 = (bf16[128,2048]{1,0:T(8,128)(2,1)S(1)}, bf16[128,2048]{1,0:T(8,128)(2,1)S(1)}, u32[]{:S(2)}, u32[]{:S(2)}) collective-permute-start(bf16[128,2048]{1,0:T(8,128)(2,1)S(1)} %get-tuple-element.56), channel_id=1, source_target_pairs={{0,4},{2,6},{4,0},{6,2},{1,5},{3,7},{5,1},{7,3},{8,12},{10,14},{12... | collective-permute-start | bytes 1572872 | tf_op jit(solution)/shard_map/ppermute | solution.py:675
  28.1 1.5 %collective-permute-start.8 = (bf16[64,2048]{1,0:T(8,128)(2,1)S(1)}, bf16[64,2048]{1,0:T(8,128)(2,1)S(1)}, u32[]{:S(2)}, u32[]{:S(2)}) collective-permute-start(bf16[64,2048]{1,0:T(8,128)(2,1)S(1)} %collective-permute-done.7.own_ref.refs_1_.refs_5_), channel_id=1, source_target_pairs={{1,0},{0,1},{3,2},{2,3},{5,4},{4,5},{7,6},{6,7},{9,8},{8,9},{11,10... | collective-permute-start | bytes 786440 | tf_op jit(solution)/shard_map/ppermute | solution.py:560
  40.1 1.5 %collective-permute-start.11 = (bf16[64,2048]{1,0:T(8,128)(2,1)S(1)}, bf16[64,2048]{1,0:T(8,128)(2,1)S(1)}, u32[]{:S(2)}, u32[]{:S(2)}) collective-permute-start(bf16[64,2048]{1,0:T(8,128)(2,1)S(1)} %get-tuple-element.60), channel_id=1, source_target_pairs={{0,1},{1,0},{2,3},{3,2},{4,5},{5,4},{6,7},{7,6},{8,9},{9,8},{10,11... | collective-permute-start | bytes 786440 | tf_op jit(solution)/shard_map/ppermute | solution.py:566
  41.6 12.4 %collective-permute-start.15 = (bf16[64,2048]{1,0:T(8,128)(2,1)S(1)}, bf16[64,2048]{1,0:T(8,128)(2,1)S(1)}, u32[]{:S(2)}, u32[]{:S(2)}) collective-permute-start(bf16[64,2048]{1,0:T(8,128)(2,1)S(1)} %get-tuple-element.64.refs_6_), channel_id=1, source_target_pairs={{8,0},{9,1},{10,2},{11,3},{12,4},{13,5},{14,6},{15,7}} | collective-permute-start | bytes 786440 | tf_op jit(solution)/shard_map/ppermute | solution.py:658
  42.9 15.9 %collective-permute-start.16 = (bf16[16,2048]{1,0:T(8,128)(2,1)S(1)}, bf16[16,2048]{1,0:T(8,128)(2,1)S(1)}, u32[]{:S(2)}, u32[]{:S(2)}) collective-permute-start(bf16[16,2048]{1,0:T(8,128)(2,1)S(1)} %get-tuple-element.65), channel_id=1, source_target_pairs={{24,30},{26,28},{28,26},{30,24},{25,31},{27,29},{29,27},{31,25}} | collective-permute-start | bytes 196616 | tf_op jit(solution)/shard_map/ppermute | solution.py:687
  43.8 14.9 %collective-permute-start.12 = (bf16[64,512]{1,0:T(8,128)(2,1)S(1)}, bf16[64,512]{1,0:T(8,128)(2,1)S(1)}, u32[]{:S(2)}, u32[]{:S(2)}) collective-permute-start(bf16[64,512]{1,0:T(8,128)(2,1)S(1)} %get-tuple-element.61), channel_id=1, source_target_pairs={{8,6},{10,4},{12,2},{14,0},{16,14},{18,12},{20,10},{22,8},{24,22},... | collective-permute-start | bytes 196616 | tf_op jit(solution)/shard_map/ppermute | solution.py:662
  45.1 13.7 %collective-permute-start.13 = (bf16[64,512]{1,0:T(8,128)(2,1)S(1)}, bf16[64,512]{1,0:T(8,128)(2,1)S(1)}, u32[]{:S(2)}, u32[]{:S(2)}) collective-permute-start(bf16[64,512]{1,0:T(8,128)(2,1)S(1)} %get-tuple-element.62), channel_id=1, source_target_pairs={{8,4},{10,6},{12,0},{14,2},{16,12},{18,14},{20,8},{22,10},{24,20},... | collective-permute-start | bytes 196616 | tf_op jit(solution)/shard_map/ppermute | solution.py:662
  46.4 12.4 %collective-permute-start.14 = (bf16[64,512]{1,0:T(8,128)(2,1)S(1)}, bf16[64,512]{1,0:T(8,128)(2,1)S(1)}, u32[]{:S(2)}, u32[]{:S(2)}) collective-permute-start(bf16[64,512]{1,0:T(8,128)(2,1)S(1)} %get-tuple-element.63), channel_id=1, source_target_pairs={{8,2},{10,0},{12,6},{14,4},{16,10},{18,8},{20,14},{22,12},{24,18},... | collective-permute-start | bytes 196616 | tf_op jit(solution)/shard_map/ppermute | solution.py:662
  58.6 1.6 %collective-permute-start.18 = (bf16[64,2048]{1,0:T(8,128)(2,1)S(1)}, bf16[64,2048]{1,0:T(8,128)(2,1)S(1)}, u32[]{:S(2)}, u32[]{:S(2)}) collective-permute-start(bf16[64,2048]{1,0:T(8,128)(2,1)S(1)} %get-tuple-element.67), channel_id=1, source_target_pairs={{0,1},{1,0},{2,3},{3,2},{4,5},{5,4},{6,7},{7,6},{8,9},{9,8},{10,11... | collective-permute-start | bytes 786440 | tf_op jit(solution)/shard_map/ppermute | solution.py:566
  58.9 1.7 %collective-permute-start.17 = (bf16[256,512]{1,0:T(8,128)(2,1)S(1)}, bf16[256,512]{1,0:T(8,128)(2,1)S(1)}, u32[]{:S(2)}, u32[]{:S(2)}) collective-permute-start(bf16[256,512]{1,0:T(8,128)(2,1)S(1)} %collect.1.refs_0_), channel_id=1, source_target_pairs={{1,0},{0,1},{3,2},{2,3},{5,4},{4,5},{7,6},{6,7},{9,8},{8,9},{11,10... | collective-permute-start | bytes 786440 | tf_op jit(solution)/shard_map/ppermute | solution.py:560

commit v8 on v7

--- a/solution.py
+++ b/solution.py
@@ -690,7 +690,7 @@
                 moments = stage_in_section(
                     [moment_one[0], moment_two[0]], lambda section: section == sections - 2, moments, [grad]
                 )
-                late = [*exchange, *moments]
+                late = [*exchange, *moments, corner]
             else:
                 late = ()
     if planned:

time: 66.7 us -> 66.7 us (level)
    ppermute x3, waiting for transfers between devices: 6.3 us -> 6.98 us  [on_device(): upstreams.append(lax.ppermute(grad, 'pipe', [(layer, layer - 1)]))]
    ppermute x4, waiting for transfers between devices: 1.53 us -> 0.87 us  [from_peers(): lax.ppermute(value, axis, [((i + k) % size, i) for i in range(size)])]
  transfers between devices with their start and end apart: 19 -> 19, of which waited for: 10 -> 11; matrix products, arithmetic and copies ran while one was open for 0% -> 0% of each run, Pallas kernels for 15% -> 15%
where the time goes in v8:
time: 66.7 us; the launch traced here: 66.4 us
  waiting for transfers between devices  28.3 us (42%)
  Pallas kernels  20.2 us (30%)
  starting transfers between devices  14.8 us (22%)
  blocking collectives  2.17 us (3%)
  between operations  0.97 us (1%)
    ppermute x4, waiting for transfers between devices, on_device(): lax.ppermute(piece, 'dp', [(i, i ^ k) for i in range(owners)])  15.1 us
    ppermute x3, waiting for transfers between devices, on_device(): upstreams.append(lax.ppermute(grad, 'pipe', [(layer, layer - 1)]))  6.98 us
    ppermute x4, starting transfers between devices, on_device(): lax.ppermute(piece, 'dp', [(i, i ^ k) for i in range(owners)])  6.34 us
    pallas_call x1, Pallas kernels, adam_step(): pl.pallas_call(functools.partial(adam_kernel, (owners, parts, blocks[0].s...  5.75 us
    ppermute x4, waiting for transfers between devices, to_peers(): lax.ppermute(value, axis, [(i, (i + k) % size) for i in range(size)])  5.43 us
    pallas_call x1, Pallas kernels, first_step(): pl.pallas_call(functools.partial(first_kernel, layer, parts, len(peers),...  4.16 us
    ppermute x3, starting transfers between devices, on_device(): lax.ppermute(cut, ('pipe', 'dp'), [(s * owners + i, (s - 1) * owners + (i...  3.88 us
    pallas_call x1, Pallas kernels, stage(): pl.pallas_call(kernel, out_shape=[pltpu.VMEM(a.shape, a.dtype) for a in a...  3.6 us
  transfers between devices with their start and end apart: 19, of which 11 were waited for; matrix products, arithmetic and copies ran while one was open for 0% of the time, Pallas kernels for 15%

profile of v8, /device:TPU:0, one launch (start us, length us, event | category | flops | bytes accessed | tf_op | source)
XLA Modules:
  0.0 66.4 jit_solution(12280800358781243784)
XLA Ops:
  0.6 0.5 collective-permute-start
  1.1 3.6 %stage.1 = (bf16[2048,2048]{1,0:T(8,128)(2,1)S(1)}, bf16[128,2048]{1,0:T(8,128)(2,1)S(1)}, bf16[64,2048]{1,0:T(8,128)(2,1)S(1)}) custom-call(bf16[2048,2048]{1,0:T(8,128)(2,1)} %bitcast.15, bf16[128,2048]{1,0:T(8,128)(2,1)} %bitcast.17, bf16[64,2048]{1,0:T(8,128)(2,1)} %refs_2_.1), custom_call_target="tpu_custom_call" | custom-call | bytes 18350080 | tf_op jit(solution)/shard_map/stage/pallas_call | solution.py:55
  4.8 0.0 collective-permute-done.refs_0_
  4.8 0.0 copy-start
  4.8 4.2 %first_step.1 = (bf16[2048,2048]{1,0:T(8,128)(2,1)S(1)}, f32[64,2048]{1,0:T(8,128)S(1)}, bf16[64,2048]{1,0:T(8,128)(2,1)S(1)}, bf16[64,2048]{1,0:T(8,128)(2,1)S(...) custom-call(bf16[64,2048]{1,0:T(8,128)(2,1)S(1)} %get-tuple-element.38.own_ref.refs_1_.refs_4_.refs_6_.refs_3_.refs_7_, ...), custom_call_target="tpu_custom_call" | custom-call | tf_op jit(solution)/shard_map/first_step/pallas_call | solution.py:246
  8.9 0.1 collective-permute-start.1
  9.1 1.5 %collective-permute-done.1.refs_0_ = bf16[64,2048]{1,0:T(8,128)(2,1)S(1)} collective-permute-done((bf16[64,2048]{1,0:T(8,128)(2,1)S(1)}, bf16[64,2048]{1,0:T(8,128)(2,1)S(1)}, u32[]{:S(2)}, u32[]{:S(2)}) %collective-permute-start.1) | collective-permute-done | bytes 262176 | tf_op jit(solution)/shard_map/ppermute | solution.py:566
  10.5 0.0 copy-done
  10.6 0.7 %collective-permute-start.2 = (bf16[64,2048]{1,0:T(8,128)(2,1)S(1)}, bf16[64,2048]{1,0:T(8,128)(2,1)S(1)}, u32[]{:S(2)}, u32[]{:S(2)}) collective-permute-start(bf16[64,2048]{1,0:T(8,128)(2,1)S(1)} %get-tuple-element.46.refs_2_.refs_4_), channel_id=1, source_target_pairs={{24,16},{25,17},{26,18},{27,19},{28,20},{29,21},{30,22},{31,23}} | collective-permute-start | bytes 786440 | tf_op jit(solution)/shard_map/ppermute | solution.py:658
  11.3 2.7 %collective-permute-start.4 = (bf16[80,2048]{1,0:T(8,128)(2,1)S(1)}, bf16[80,2048]{1,0:T(8,128)(2,1)S(1)}, u32[]{:S(2)}, u32[]{:S(2)}) collective-permute-start(bf16[80,2048]{1,0:T(8,128)(2,1)S(1)} %get-tuple-element.48), channel_id=1, source_target_pairs={{0,2},{2,0},{4,6},{6,4},{1,3},{3,1},{5,7},{7,5},{8,10},{10,8},{12,... | collective-permute-start | bytes 983048 | tf_op jit(solution)/shard_map/ppermute | solution.py:675
  14.0 1.5 %collective-permute-start.5 = (bf16[80,2048]{1,0:T(8,128)(2,1)S(1)}, bf16[80,2048]{1,0:T(8,128)(2,1)S(1)}, u32[]{:S(2)}, u32[]{:S(2)}) collective-permute-start(bf16[80,2048]{1,0:T(8,128)(2,1)S(1)} %get-tuple-element.49), channel_id=1, source_target_pairs={{0,4},{2,6},{4,0},{6,2},{1,5},{3,7},{5,1},{7,3},{8,12},{10,14},{12... | collective-permute-start | bytes 983048 | tf_op jit(solution)/shard_map/ppermute | solution.py:675
  15.5 0.0 collective-permute-done.2.own_ref.refs_1_.refs_4_
  15.5 0.0 collective-permute-start.3
  15.5 3.5 %stage_in_section.2 = (f32[512,2048]{1,0:T(8,128)S(1)}, f32[512,2048]{1,0:T(8,128)S(1)}) custom-call(f32[512,2048]{1,0:T(8,128)} %bitcast.11, f32[512,2048]{1,0:T(8,128)} %bitcast.13, bf16[64,2048]{1,0:T(8,128)(2,1)S(1)} %get-tuple-element.46.refs_2_.refs_4_), custom_call_target="tpu_custom_call" | custom-call | tf_op jit(solution)/shard_map/stage_in_section/pallas_call | solution.py:81
  19.0 0.0 collective-permute-done.3.refs_0_
  19.0 3.2 %collective-permute-done.4.refs_0_.refs_8_.refs_2_.refs_7_ = bf16[80,2048]{1,0:T(8,128)(2,1)S(1)} collective-permute-done((bf16[80,2048]{1,0:T(8,128)(2,1)S(1)}, bf16[80,2048]{1,0:T(8,128)(2,1)S(1)}, u32[]{:S(2)}, u32[]{:S(2)}) %collective-permute-start.4) | collective-permute-done | bytes 327712 | tf_op jit(solution)/shard_map/ppermute | solution.py:675
  22.2 1.5 %collective-permute-done.5.refs_1_.refs_6_.refs_5_.refs_8_ = bf16[80,2048]{1,0:T(8,128)(2,1)S(1)} collective-permute-done((bf16[80,2048]{1,0:T(8,128)(2,1)S(1)}, bf16[80,2048]{1,0:T(8,128)(2,1)S(1)}, u32[]{:S(2)}, u32[]{:S(2)}) %collective-permute-start.5) | collective-permute-done | bytes 327712 | tf_op jit(solution)/shard_map/ppermute | solution.py:675
  23.7 0.0 collective-permute-start.6
  23.7 1.5 %collective-permute-done.6.refs_0_ = bf16[64,2048]{1,0:T(8,128)(2,1)S(1)} collective-permute-done((bf16[64,2048]{1,0:T(8,128)(2,1)S(1)}, bf16[64,2048]{1,0:T(8,128)(2,1)S(1)}, u32[]{:S(2)}, u32[]{:S(2)}) %collective-permute-start.6) | collective-permute-done | bytes 262176 | tf_op jit(solution)/shard_map/ppermute | solution.py:566
  25.2 0.1 norm_step.5
  25.3 0.7 %collective-permute-start.7 = (bf16[64,2048]{1,0:T(8,128)(2,1)S(1)}, bf16[64,2048]{1,0:T(8,128)(2,1)S(1)}, u32[]{:S(2)}, u32[]{:S(2)}) collective-permute-start(bf16[64,2048]{1,0:T(8,128)(2,1)S(1)} %get-tuple-element.54.refs_4_.refs_5_), channel_id=1, source_target_pairs={{16,8},{17,9},{18,10},{19,11},{20,12},{21,13},{22,14},{23,15}} | collective-permute-start | bytes 786440 | tf_op jit(solution)/shard_map/ppermute | solution.py:658
  26.0 0.4 collective-permute-start.9
  26.4 1.7 %collective-permute-start.10 = (bf16[128,2048]{1,0:T(8,128)(2,1)S(1)}, bf16[128,2048]{1,0:T(8,128)(2,1)S(1)}, u32[]{:S(2)}, u32[]{:S(2)}) collective-permute-start(bf16[128,2048]{1,0:T(8,128)(2,1)S(1)} %get-tuple-element.56), channel_id=1, source_target_pairs={{0,4},{2,6},{4,0},{6,2},{1,5},{3,7},{5,1},{7,3},{8,12},{10,14},{12... | collective-permute-start | bytes 1572872 | tf_op jit(solution)/shard_map/ppermute | solution.py:675
  28.1 0.0 collective-permute-done.7.own_ref.refs_1_.refs_5_
  28.1 0.0 collective-permute-start.8
  28.1 0.7 collective-permute-start.11
  28.8 0.1 stage_in_section.3
  28.8 0.8 %collective-permute-done.8.refs_0_ = bf16[64,2048]{1,0:T(8,128)(2,1)S(1)} collective-permute-done((bf16[64,2048]{1,0:T(8,128)(2,1)S(1)}, bf16[64,2048]{1,0:T(8,128)(2,1)S(1)}, u32[]{:S(2)}, u32[]{:S(2)}) %collective-permute-start.8) | collective-permute-done | bytes 262176 | tf_op jit(solution)/shard_map/ppermute | solution.py:560
  29.6 0.0 collective-permute-done.11.refs_4_.refs_9_
  29.6 10.4 %collective-permute-done.9.refs_0_.refs_3_.refs_7_ = bf16[128,2048]{1,0:T(8,128)(2,1)S(1)} collective-permute-done((bf16[128,2048]{1,0:T(8,128)(2,1)S(1)}, bf16[128,2048]{1,0:T(8,128)(2,1)S(1)}, u32[]{:S(2)}, u32[]{:S(2)}) %collective-permute-start.9) | collective-permute-done | bytes 524320 | tf_op jit(solution)/shard_map/ppermute | solution.py:675
  40.0 0.1 collective-permute-done.10.refs_1_.refs_4_.refs_6_
  40.1 0.0 collective-permute-start.12
  40.1 1.5 %collective-permute-done.12.refs_0_ = bf16[64,2048]{1,0:T(8,128)(2,1)S(1)} collective-permute-done((bf16[64,2048]{1,0:T(8,128)(2,1)S(1)}, bf16[64,2048]{1,0:T(8,128)(2,1)S(1)}, u32[]{:S(2)}, u32[]{:S(2)}) %collective-permute-start.12) | collective-permute-done | bytes 262176 | tf_op jit(solution)/shard_map/ppermute | solution.py:566
  41.6 1.3 %collective-permute-start.16 = (bf16[64,2048]{1,0:T(8,128)(2,1)S(1)}, bf16[64,2048]{1,0:T(8,128)(2,1)S(1)}, u32[]{:S(2)}, u32[]{:S(2)}) collective-permute-start(bf16[64,2048]{1,0:T(8,128)(2,1)S(1)} %get-tuple-element.65.refs_6_), channel_id=1, source_target_pairs={{8,0},{9,1},{10,2},{11,3},{12,4},{13,5},{14,6},{15,7}} | collective-permute-start | bytes 786440 | tf_op jit(solution)/shard_map/ppermute | solution.py:658
  42.9 0.2 stack.1.refs_11_.refs_3_
  43.2 1.3 %collective-permute-start.13 = (bf16[64,512]{1,0:T(8,128)(2,1)S(1)}, bf16[64,512]{1,0:T(8,128)(2,1)S(1)}, u32[]{:S(2)}, u32[]{:S(2)}) collective-permute-start(bf16[64,512]{1,0:T(8,128)(2,1)S(1)} %get-tuple-element.62), channel_id=1, source_target_pairs={{8,6},{10,4},{12,2},{14,0},{16,14},{18,12},{20,10},{22,8},{24,22},... | collective-permute-start | bytes 196616 | tf_op jit(solution)/shard_map/ppermute | solution.py:662
  44.5 1.3 %collective-permute-start.14 = (bf16[64,512]{1,0:T(8,128)(2,1)S(1)}, bf16[64,512]{1,0:T(8,128)(2,1)S(1)}, u32[]{:S(2)}, u32[]{:S(2)}) collective-permute-start(bf16[64,512]{1,0:T(8,128)(2,1)S(1)} %get-tuple-element.63), channel_id=1, source_target_pairs={{8,4},{10,6},{12,0},{14,2},{16,12},{18,14},{20,8},{22,10},{24,20},... | collective-permute-start | bytes 196616 | tf_op jit(solution)/shard_map/ppermute | solution.py:662
  45.8 1.3 %collective-permute-start.15 = (bf16[64,512]{1,0:T(8,128)(2,1)S(1)}, bf16[64,512]{1,0:T(8,128)(2,1)S(1)}, u32[]{:S(2)}, u32[]{:S(2)}) collective-permute-start(bf16[64,512]{1,0:T(8,128)(2,1)S(1)} %get-tuple-element.64), channel_id=1, source_target_pairs={{8,2},{10,0},{12,6},{14,4},{16,10},{18,8},{20,14},{22,12},{24,18},... | collective-permute-start | bytes 196616 | tf_op jit(solution)/shard_map/ppermute | solution.py:662
  47.1 7.0 %collective-permute-done.16.refs_0_.refs_6_.refs_1_ = bf16[64,2048]{1,0:T(8,128)(2,1)S(1)} collective-permute-done((bf16[64,2048]{1,0:T(8,128)(2,1)S(1)}, bf16[64,2048]{1,0:T(8,128)(2,1)S(1)}, u32[]{:S(2)}, u32[]{:S(2)}) %collective-permute-start.16) | collective-permute-done | bytes 262176 | tf_op jit(solution)/shard_map/ppermute | solution.py:658
  54.0 2.2 %all_gather.3.refs_1_ = bf16[128,2048]{1,0:T(8,128)(2,1)S(1)} all-gather(bf16[64,2048]{1,0:T(8,128)(2,1)S(1)} %collective-permute-done.16.refs_0_.refs_6_.refs_1_), channel_id=1, replica_groups=mesh['pipe'=4,'dp'=4,'tensor'=2] {'tensor'}, dimensions={0}, use_global_device_ids=true | all-gather | bytes 786432 | tf_op jit(solution)/shard_map/all_gather | solution.py:599
  56.2 2.4 %section_step.1 = (f32[64,2048]{1,0:T(8,128)S(1)}, bf16[64,2048]{1,0:T(8,128)(2,1)S(1)}) custom-call(bf16[64,2048]{1,0:T(8,128)(2,1)S(1)} %collective-permute-done.16.refs_0_.refs_6_.refs_1_, bf16[128,2048]{1,0:T(8,128)(2,1)S(1)} %all_gather.3.refs_1_, bf16[2048,2048]{1,0:T(8,128)(2,1)S(1)} %get-tuple-element.39.refs_1_.refs_2_.refs_4_, ...), custom_call_target="tpu_custom_call" | custom-call | tf_op jit(solution)/shard_map/section_step/pallas_call | solution.py:284
  58.6 0.2 collective-permute-start.18
  58.8 0.0 collective-permute-done.13.refs_0_
  58.8 0.0 collective-permute-done.14.refs_1_
  58.8 0.0 collective-permute-done.15.refs_2_
  58.8 0.1 collect.1.refs_0_
  58.8 0.4 collective-permute-start.17
  59.3 0.9 %collective-permute-done.18.refs_0_ = bf16[64,2048]{1,0:T(8,128)(2,1)S(1)} collective-permute-done((bf16[64,2048]{1,0:T(8,128)(2,1)S(1)}, bf16[64,2048]{1,0:T(8,128)(2,1)S(1)}, u32[]{:S(2)}, u32[]{:S(2)}) %collective-permute-start.18) | collective-permute-done | bytes 262176 | tf_op jit(solution)/shard_map/ppermute | solution.py:566
  60.2 0.3 norm_step.7.refs_2_
  60.5 0.1 collective-permute-done.17.refs_1_
  60.5 5.7 %adam_step.1 = (f32[512,2048]{1,0:T(8,128)}, f32[512,2048]{1,0:T(8,128)}, f32[512,2048]{1,0:T(8,128)}, bf16[64,2048]{1,0:T(8,128)(2,1)}) custom-call(bf16[256,512]{1,0:T(8,128)(2,1)S(1)} %collect.1.refs_0_, bf16[256,512]{1,0:T(8,128)(2,1)S(1)} %collective-permute-done.17.refs_1_, bf16[64,2048]{1,0:T(8,128)(2,1)S(1)} %norm_step.7.refs_2_, ...), custom_call_target="tpu_custom_call" | custom-call | tf_op jit(solution)/shard_map/adam_step/pallas_call | solution.py:493
  (6 shorter events, 0.1 us)
Async XLA Ops:
  0.6 4.1 %collective-permute-start = (bf16[64,2048]{1,0:T(8,128)(2,1)}, bf16[64,2048]{1,0:T(8,128)(2,1)S(1)}, u32[]{:S(2)}, u32[]{:S(2)}) collective-permute-start(bf16[64,2048]{1,0:T(8,128)(2,1)} %refs_2_.1), channel_id=1, source_target_pairs={{1,0},{0,1},{3,2},{2,3},{5,4},{4,5},{7,6},{6,7},{9,8},{8,9},{11,10... | collective-permute-start | bytes 786440 | tf_op jit(solution)/shard_map/ppermute | solution.py:560
  4.8 5.8 %copy-start = (f32[1,2048]{1,0:T(1,128)S(1)}, f32[1,2048]{1,0:T(1,128)}, u32[]{:S(2)}) copy-start(f32[1,2048]{1,0:T(1,128)} %refs_3_.7) | copy-start | bytes 24580
  8.9 1.6 %collective-permute-start.1 = (bf16[64,2048]{1,0:T(8,128)(2,1)S(1)}, bf16[64,2048]{1,0:T(8,128)(2,1)S(1)}, u32[]{:S(2)}, u32[]{:S(2)}) collective-permute-start(bf16[64,2048]{1,0:T(8,128)(2,1)S(1)} %get-tuple-element.42), channel_id=1, source_target_pairs={{0,1},{1,0},{2,3},{3,2},{4,5},{5,4},{6,7},{7,6},{8,9},{9,8},{10,11... | collective-permute-start | bytes 786440 | tf_op jit(solution)/shard_map/ppermute | solution.py:566
  10.6 4.9 %collective-permute-start.2 = (bf16[64,2048]{1,0:T(8,128)(2,1)S(1)}, bf16[64,2048]{1,0:T(8,128)(2,1)S(1)}, u32[]{:S(2)}, u32[]{:S(2)}) collective-permute-start(bf16[64,2048]{1,0:T(8,128)(2,1)S(1)} %get-tuple-element.46.refs_2_.refs_4_), channel_id=1, source_target_pairs={{24,16},{25,17},{26,18},{27,19},{28,20},{29,21},{30,22},{31,23}} | collective-permute-start | bytes 786440 | tf_op jit(solution)/shard_map/ppermute | solution.py:658
  11.3 10.9 %collective-permute-start.4 = (bf16[80,2048]{1,0:T(8,128)(2,1)S(1)}, bf16[80,2048]{1,0:T(8,128)(2,1)S(1)}, u32[]{:S(2)}, u32[]{:S(2)}) collective-permute-start(bf16[80,2048]{1,0:T(8,128)(2,1)S(1)} %get-tuple-element.48), channel_id=1, source_target_pairs={{0,2},{2,0},{4,6},{6,4},{1,3},{3,1},{5,7},{7,5},{8,10},{10,8},{12,... | collective-permute-start | bytes 983048 | tf_op jit(solution)/shard_map/ppermute | solution.py:675
  14.0 9.7 %collective-permute-start.5 = (bf16[80,2048]{1,0:T(8,128)(2,1)S(1)}, bf16[80,2048]{1,0:T(8,128)(2,1)S(1)}, u32[]{:S(2)}, u32[]{:S(2)}) collective-permute-start(bf16[80,2048]{1,0:T(8,128)(2,1)S(1)} %get-tuple-element.49), channel_id=1, source_target_pairs={{0,4},{2,6},{4,0},{6,2},{1,5},{3,7},{5,1},{7,3},{8,12},{10,14},{12... | collective-permute-start | bytes 983048 | tf_op jit(solution)/shard_map/ppermute | solution.py:675
  15.5 3.5 %collective-permute-start.3 = (bf16[64,2048]{1,0:T(8,128)(2,1)S(1)}, bf16[64,2048]{1,0:T(8,128)(2,1)S(1)}, u32[]{:S(2)}, u32[]{:S(2)}) collective-permute-start(bf16[64,2048]{1,0:T(8,128)(2,1)S(1)} %collective-permute-done.2.own_ref.refs_1_.refs_4_), channel_id=1, source_target_pairs={{1,0},{0,1},{3,2},{2,3},{5,4},{4,5},{7,6},{6,7},{9,8},{8,9},{11,10... | collective-permute-start | bytes 786440 | tf_op jit(solution)/shard_map/ppermute | solution.py:560
  23.7 1.5 %collective-permute-start.6 = (bf16[64,2048]{1,0:T(8,128)(2,1)S(1)}, bf16[64,2048]{1,0:T(8,128)(2,1)S(1)}, u32[]{:S(2)}, u32[]{:S(2)}) collective-permute-start(bf16[64,2048]{1,0:T(8,128)(2,1)S(1)} %get-tuple-element.53), channel_id=1, source_target_pairs={{0,1},{1,0},{2,3},{3,2},{4,5},{5,4},{6,7},{7,6},{8,9},{9,8},{10,11... | collective-permute-start | bytes 786440 | tf_op jit(solution)/shard_map/ppermute | solution.py:566
  25.3 2.8 %collective-permute-start.7 = (bf16[64,2048]{1,0:T(8,128)(2,1)S(1)}, bf16[64,2048]{1,0:T(8,128)(2,1)S(1)}, u32[]{:S(2)}, u32[]{:S(2)}) collective-permute-start(bf16[64,2048]{1,0:T(8,128)(2,1)S(1)} %get-tuple-element.54.refs_4_.refs_5_), channel_id=1, source_target_pairs={{16,8},{17,9},{18,10},{19,11},{20,12},{21,13},{22,14},{23,15}} | collective-permute-start | bytes 786440 | tf_op jit(solution)/shard_map/ppermute | solution.py:658
  26.0 14.0 %collective-permute-start.9 = (bf16[128,2048]{1,0:T(8,128)(2,1)S(1)}, bf16[128,2048]{1,0:T(8,128)(2,1)S(1)}, u32[]{:S(2)}, u32[]{:S(2)}) collective-permute-start(bf16[128,2048]{1,0:T(8,128)(2,1)S(1)} %get-tuple-element.55), channel_id=1, source_target_pairs={{0,2},{2,0},{4,6},{6,4},{1,3},{3,1},{5,7},{7,5},{8,10},{10,8},{12,... | collective-permute-start | bytes 1572872 | tf_op jit(solution)/shard_map/ppermute | solution.py:675
  26.4 13.7 %collective-permute-start.10 = (bf16[128,2048]{1,0:T(8,128)(2,1)S(1)}, bf16[128,2048]{1,0:T(8,128)(2,1)S(1)}, u32[]{:S(2)}, u32[]{:S(2)}) collective-permute-start(bf16[128,2048]{1,0:T(8,128)(2,1)S(1)} %get-tuple-element.56), channel_id=1, source_target_pairs={{0,4},{2,6},{4,0},{6,2},{1,5},{3,7},{5,1},{7,3},{8,12},{10,14},{12... | collective-permute-start | bytes 1572872 | tf_op jit(solution)/shard_map/ppermute | solution.py:675
  28.1 1.5 %collective-permute-start.8 = (bf16[64,2048]{1,0:T(8,128)(2,1)S(1)}, bf16[64,2048]{1,0:T(8,128)(2,1)S(1)}, u32[]{:S(2)}, u32[]{:S(2)}) collective-permute-start(bf16[64,2048]{1,0:T(8,128)(2,1)S(1)} %collective-permute-done.7.own_ref.refs_1_.refs_5_), channel_id=1, source_target_pairs={{1,0},{0,1},{3,2},{2,3},{5,4},{4,5},{7,6},{6,7},{9,8},{8,9},{11,10... | collective-permute-start | bytes 786440 | tf_op jit(solution)/shard_map/ppermute | solution.py:560
  28.1 1.5 %collective-permute-start.11 = (bf16[16,2048]{1,0:T(8,128)(2,1)S(1)}, bf16[16,2048]{1,0:T(8,128)(2,1)S(1)}, u32[]{:S(2)}, u32[]{:S(2)}) collective-permute-start(bf16[16,2048]{1,0:T(8,128)(2,1)S(1)} %get-tuple-element.59), channel_id=1, source_target_pairs={{24,30},{26,28},{28,26},{30,24},{25,31},{27,29},{29,27},{31,25}} | collective-permute-start | bytes 196616 | tf_op jit(solution)/shard_map/ppermute | solution.py:687
  40.1 1.5 %collective-permute-start.12 = (bf16[64,2048]{1,0:T(8,128)(2,1)S(1)}, bf16[64,2048]{1,0:T(8,128)(2,1)S(1)}, u32[]{:S(2)}, u32[]{:S(2)}) collective-permute-start(bf16[64,2048]{1,0:T(8,128)(2,1)S(1)} %get-tuple-element.61), channel_id=1, source_target_pairs={{0,1},{1,0},{2,3},{3,2},{4,5},{5,4},{6,7},{7,6},{8,9},{9,8},{10,11... | collective-permute-start | bytes 786440 | tf_op jit(solution)/shard_map/ppermute | solution.py:566
  41.6 12.4 %collective-permute-start.16 = (bf16[64,2048]{1,0:T(8,128)(2,1)S(1)}, bf16[64,2048]{1,0:T(8,128)(2,1)S(1)}, u32[]{:S(2)}, u32[]{:S(2)}) collective-permute-start(bf16[64,2048]{1,0:T(8,128)(2,1)S(1)} %get-tuple-element.65.refs_6_), channel_id=1, source_target_pairs={{8,0},{9,1},{10,2},{11,3},{12,4},{13,5},{14,6},{15,7}} | collective-permute-start | bytes 786440 | tf_op jit(solution)/shard_map/ppermute | solution.py:658
  43.2 15.6 %collective-permute-start.13 = (bf16[64,512]{1,0:T(8,128)(2,1)S(1)}, bf16[64,512]{1,0:T(8,128)(2,1)S(1)}, u32[]{:S(2)}, u32[]{:S(2)}) collective-permute-start(bf16[64,512]{1,0:T(8,128)(2,1)S(1)} %get-tuple-element.62), channel_id=1, source_target_pairs={{8,6},{10,4},{12,2},{14,0},{16,14},{18,12},{20,10},{22,8},{24,22},... | collective-permute-start | bytes 196616 | tf_op jit(solution)/shard_map/ppermute | solution.py:662
  44.5 14.3 %collective-permute-start.14 = (bf16[64,512]{1,0:T(8,128)(2,1)S(1)}, bf16[64,512]{1,0:T(8,128)(2,1)S(1)}, u32[]{:S(2)}, u32[]{:S(2)}) collective-permute-start(bf16[64,512]{1,0:T(8,128)(2,1)S(1)} %get-tuple-element.63), channel_id=1, source_target_pairs={{8,4},{10,6},{12,0},{14,2},{16,12},{18,14},{20,8},{22,10},{24,20},... | collective-permute-start | bytes 196616 | tf_op jit(solution)/shard_map/ppermute | solution.py:662
  45.8 13.0 %collective-permute-start.15 = (bf16[64,512]{1,0:T(8,128)(2,1)S(1)}, bf16[64,512]{1,0:T(8,128)(2,1)S(1)}, u32[]{:S(2)}, u32[]{:S(2)}) collective-permute-start(bf16[64,512]{1,0:T(8,128)(2,1)S(1)} %get-tuple-element.64), channel_id=1, source_target_pairs={{8,2},{10,0},{12,6},{14,4},{16,10},{18,8},{20,14},{22,12},{24,18},... | collective-permute-start | bytes 196616 | tf_op jit(solution)/shard_map/ppermute | solution.py:662
  58.6 1.6 %collective-permute-start.18 = (bf16[64,2048]{1,0:T(8,128)(2,1)S(1)}, bf16[64,2048]{1,0:T(8,128)(2,1)S(1)}, u32[]{:S(2)}, u32[]{:S(2)}) collective-permute-start(bf16[64,2048]{1,0:T(8,128)(2,1)S(1)} %get-tuple-element.67), channel_id=1, source_target_pairs={{0,1},{1,0},{2,3},{3,2},{4,5},{5,4},{6,7},{7,6},{8,9},{9,8},{10,11... | collective-permute-start | bytes 786440 | tf_op jit(solution)/shard_map/ppermute | solution.py:566
  58.8 1.7 %collective-permute-start.17 = (bf16[256,512]{1,0:T(8,128)(2,1)S(1)}, bf16[256,512]{1,0:T(8,128)(2,1)S(1)}, u32[]{:S(2)}, u32[]{:S(2)}) collective-permute-start(bf16[256,512]{1,0:T(8,128)(2,1)S(1)} %collect.1.refs_0_), channel_id=1, source_target_pairs={{1,0},{0,1},{3,2},{2,3},{5,4},{4,5},{7,6},{6,7},{9,8},{8,9},{11,10... | collective-permute-start | bytes 786440 | tf_op jit(solution)/shard_map/ppermute | solution.py:560
